TPU v7x, 32 devices: a whole 2x2x4 slice. The times are simulated.
32 devices in a mesh: job: 2 (over x), col: 16 (over z, y, core).
Axes of the slice: x: 2, y: 2, z: 4, core: 2. Of those that a mesh axis runs over, the one named last changes fastest.
Arguments:
- tau_packed: bfloat16 [256, 1200], P(('job', 'col')), parts along dimension 0, may hold values from -6 to 6
- pair_irrep: int32 [256], P('job'), parts along dimension 0, may hold values from 0 to 7
- cd_sizes: int32 [16], P('job'), parts along dimension 0, may hold values from 1 to 1200, 3200 in all
- ab_sizes: int32 [16], P('job'), parts along dimension 0, may hold values from 1 to 6400, 25600 in all
- integrals: bfloat16 [6400, 25600], P('job', 'col'), parts along dimension 0, may hold values from -0.1875 to 0.1875
- occ_energy: float32 [256], P('job'), parts along dimension 0, may hold values from -2 to -0.5
- virt_energy: float32 [51200], P(('job', 'col')), parts along dimension 0, may hold values from 1 to 8
Outputs:
- update: float32 [256, 25600], P('job', 'col'), parts along dimension 0
- pair_energy: float32 [256], P('job'), parts along dimension 0
There are 2 independent parts, one for each index of `job`. A program takes and returns all parts, laid end to end along the dimension named above; each array names one. Nothing has to cross between parts.
All inputs are finite; a program needn't handle non-finite values.
Results may differ from a plain program's by a relative error of at most 0.0003.
Values may be sent and summed in bfloat16 or wider, within the bound.
No kernel may reach another device: no remote copies, remote signals or barrier semaphores. Data moves between devices by JAX's collectives and lax.ppermute only.
A program may use at most 64 MiB of HBM per device.

v0:
```python
import jax
import jax.numpy as jnp
from jax import lax
from jax.sharding import PartitionSpec as P


def expand(packed, irreps, cd_sizes, total_rows):
    starts = jnp.cumsum(cd_sizes) - cd_sizes
    width = packed.shape[1]
    padded = jnp.pad(packed, ((0, 0), (total_rows, total_rows - width)))
    position = jnp.arange(total_rows, dtype=jnp.int32)
    result = jnp.zeros((packed.shape[0], total_rows), packed.dtype)
    for label in range(cd_sizes.shape[0]):
        begin = starts[label]
        shifted = lax.dynamic_slice_in_dim(padded, total_rows - begin, total_rows, 1)
        offset = position - begin
        valid = (offset >= 0) & (offset < cd_sizes[label])
        keep = (irreps[:, None] == label) & valid[None, :]
        result = jnp.where(keep, shifted, result)
    return result


def shards(tau_packed, pair_irrep, cd_sizes, ab_sizes, integrals, occ_energy, virt_energy):
    cd_rows, col_count = integrals.shape
    pair_count = tau_packed.shape[0]
    my_index = lax.axis_index("col")
    columns = my_index * col_count + jnp.arange(col_count, dtype=jnp.int32)
    col_irrep = jnp.sum(
        (columns[:, None] >= jnp.cumsum(ab_sizes)[None, :]).astype(jnp.int32), axis=1
    )
    own_irreps = lax.dynamic_slice_in_dim(pair_irrep, my_index * pair_count, pair_count)
    spread = expand(tau_packed, own_irreps, cd_sizes, cd_rows)
    product = jnp.dot(
        lax.all_gather(spread, "col", axis=0, tiled=True),
        integrals,
        preferred_element_type=jnp.float32,
    )
    ladder = jnp.where(pair_irrep[:, None] == col_irrep[None, :], product, jnp.zeros_like(product))
    denom = virt_energy[None, :] - occ_energy[:, None]
    update = ladder / denom
    partial_energy = jnp.sum(ladder * update, axis=1) / (col_count * lax.axis_size("col"))
    pair_energy = lax.psum(partial_energy, "col")
    return (update, pair_energy)


def solution(mesh):
    placed = (
        P(("job", "col"), None),
        P("job"),
        P("job"),
        P("job"),
        P("job", "col"),
        P("job"),
        P(("job", "col")),
    )
    return jax.shard_map(
        shards, mesh=mesh, in_specs=placed, out_specs=(P("job", "col"), P("job")), check_vma=False
    )
```

profile of v0, /device:TPU:0, one launch (start us, length us, event | category | flops | bytes accessed | tf_op | source)
XLA Modules:
  0.0 91.5 jit_solution(14559671901939327631)
XLA Ops:
  0.6 0.8 reduce-window.17
  1.5 0.8 reduce-window.18
  2.3 0.7 bitcast_subtract_fusion
  3.0 0.7 broadcast_compare_fusion.7
  3.7 0.7 fusion.25
  14.5 1.6 %fusion.24 = (s32[1]{0:T(128)}, s32[1]{0:T(128)}, s32[1]{0:T(128)}, s32[1]{0:T(128)}, s32[1]{0:T(128)}, /*index=5*/s32[1]{0:T(128)}, s32[1]{0:T(128)}, s32[1]{0:T(128)}) fusion(s32[8]{0:T(128)} %param.9), kind=kLoop, calls=%fused_computation.63 | loop fusion | bytes 64 | tf_op jit(solution)/shard_map/slice | solution.py:17
  16.1 2.5 %fusion.16 = (pred[3200]{0:T(1024)(128)(4,1)S(1)}, pred[3200]{0:T(1024)(128)(4,1)S(1)}) fusion(s32[]{:T(128)} %bitcast.5, s32[]{:T(128)} %bitcast.4, s32[]{:T(128)} %bitcast.7, s32[]{:T(128)} %bitcast.6), kind=kLoop, calls=%fused_computation.44 | loop fusion | flops 25600 | bytes 6416 | tf_op jit(solution)/shard_map/and | solution.py:17
  18.6 2.5 %fusion.20 = (pred[3200]{0:T(1024)(128)(4,1)S(1)}, pred[3200]{0:T(1024)(128)(4,1)S(1)}) fusion(s32[]{:T(128)} %bitcast.13, s32[]{:T(128)} %bitcast.12, s32[]{:T(128)} %bitcast.15, s32[]{:T(128)} %bitcast.14), kind=kLoop, calls=%fused_computation.48 | loop fusion | flops 25600 | bytes 6416 | tf_op jit(solution)/shard_map/and | solution.py:17
  21.2 2.5 %fusion.18 = (pred[3200]{0:T(1024)(128)(4,1)S(1)}, pred[3200]{0:T(1024)(128)(4,1)S(1)}) fusion(s32[]{:T(128)} %bitcast.9, s32[]{:T(128)} %bitcast.8, s32[]{:T(128)} %bitcast.11, s32[]{:T(128)} %bitcast.10), kind=kLoop, calls=%fused_computation.46 | loop fusion | flops 25600 | bytes 6416 | tf_op jit(solution)/shard_map/and | solution.py:17
  23.7 2.5 %fusion.22 = (pred[3200]{0:T(1024)(128)(4,1)S(1)}, pred[3200]{0:T(1024)(128)(4,1)S(1)}) fusion(s32[]{:T(128)} %bitcast.17, s32[]{:T(128)} %bitcast.16, s32[]{:T(128)} %bitcast.19, s32[]{:T(128)} %bitcast.18), kind=kLoop, calls=%fused_computation.50 | loop fusion | flops 25600 | bytes 6416 | tf_op jit(solution)/shard_map/and | solution.py:17
  26.2 0.1 convert_reduce_fusion
  26.3 1.5 %and_select_fusion.7 = bf16[8,3200]{1,0:T(8,128)(2,1)S(1)} fusion(s32[]{:T(128)S(6)} %select_n.57, bf16[8,1200]{1,0:T(8,128)(2,1)} %param.7, s32[]{:T(128)S(6)} %select_n.58, s32[]{:T(128)S(6)} %select_n.59, s32[]{:T(128)S(6)} %select_n.60, s32[]{:T(128)S(6)} %select_n.61, s32[]{:T(128)S(6)} %select_n.62, s32[]{:T(128)S(6)} %select_n.63, s32[]{:T(128)S(6)} %select_n.64, ...), kind=kLoop, calls=%fused_computation.18 | loop fusion | flops 409600 | bytes 96096 | tf_op jit(solution)/shard_map/jit(_where)/select_n | solution.py:19
  27.8 25.6 %all_gather.3 = bf16[128,3200]{1,0:T(8,128)(2,1)S(1)} all-gather(bf16[8,3200]{1,0:T(8,128)(2,1)S(1)} %and_select_fusion.7), channel_id=1, replica_groups=mesh['job'=2,'col'=16] {'col'}, dimensions={0}, use_global_device_ids=true | all-gather | bytes 870400 | tf_op jit(solution)/shard_map/all_gather | solution.py:34
  53.4 7.8 %multiply_reduce_fusion = (f32[128]{0:T(128)S(1)}, f32[128,1600]{0,1:T(8,128)}) fusion(f32[128]{0:T(128)} %param.12, f32[1600]{0:T(1024)} %param.13, bf16[128,3200]{1,0:T(8,128)(2,1)S(1)} %all_gather.3, bf16[3200,1600]{0,1:T(8,128)(2,1)} %param.11, s32[1600]{0:T(1024)S(1)} %convert_reduce_fusion, s32[128]{0:T(128)} %param.8), kind=kOutput, calls=%fused_computation.1 | convolution fusion | flops 1311948672 | bytes 11892736 | tf_op jit(solution)/shard_map/dot_general | solution.py:33
  61.1 30.3 %psum.7 = f32[128]{0:T(128)} all-reduce(f32[128]{0:T(128)S(1)} %broadcast_multiply_fusion), channel_id=1, replica_groups=mesh['job'=2,'col'=16] {'col'}, use_global_device_ids=true, to_apply=%region_4.5 | all-reduce | flops 128 | bytes 1024 | tf_op jit(solution)/shard_map/psum | solution.py:42
  (3 shorter events, 0.0 us)
where the time goes:
time: 92 us; the launch traced here: 91.5 us
  blocking collectives  55.9 us (61%)
  other arithmetic  14.7 us (16%)
  between operations  10.8 us (12%)
  matrix products  7.76 us (8%)
  local copies, waits for them, and re-layouts  2.32 us (3%)
    psum x1, blocking collectives, shards(): pair_energy = lax.psum(partial_energy, 'col')  30.3 us
    all_gather x1, blocking collectives, shards(): lax.all_gather(spread, 'col', axis=0, tiled=True)  25.6 us
    and x4, other arithmetic, expand(): valid = (offset >= 0) & (offset < cd_sizes[label])  10.1 us
    dot_general x1, matrix products, shards(): jnp.dot(lax.all_gather(spread, 'col', axis=0, tiled=True), integrals, pre...  7.76 us

commit v1 on v0

v1 whole, which is shorter than its diff:
```python
import functools
import jax
import jax.numpy as jnp
from jax import lax
from jax.experimental import pallas as pl
from jax.experimental.pallas import tpu as pltpu
from jax.sharding import PartitionSpec as P

LANES = 128
F32 = jnp.float32
I32 = jnp.int32


def generators(count):
    bits = count.bit_length() - 1
    return [(1 << b) | 1 for b in range(bits - 1, 0, -1)] + ([1] if bits else [])


def swap(value, key, count):
    return lax.ppermute(value, "col", [(i, i ^ key) for i in range(count)])


def ceil_lanes(extent):
    return -(-extent // LANES) * LANES


def setup_kernel(count, rows, ab_ref, irrep_ref, occ_ref, virt_ref, weight_ref, order_ref, label_ref):
    me = lax.axis_index("col")
    pairs = irrep_ref.shape[1]
    cols = weight_ref.shape[0]
    label = irrep_ref[...]
    low = jnp.zeros((1, pairs), I32)
    high = jnp.zeros((1, pairs), I32)
    start = -me * cols
    for g in range(ab_ref.shape[0]):
        end = start + ab_ref[g]
        low = jnp.where(label == g, start, low)
        high = jnp.where(label == g, end, high)
        start = end
    occ = occ_ref[...]
    for c in range(0, cols, LANES):
        width = min(LANES, cols - c)
        spread = jnp.broadcast_to(virt_ref[:, c:c + width], (LANES, width))
        virt = jnp.transpose(spread)
        at = c + lax.broadcasted_iota(I32, (width, LANES), 0)
        for p in range(0, pairs, LANES):
            lanes = slice(p, p + LANES)
            keep = (at >= low[:, lanes]) & (at < high[:, lanes])
            weight_ref[c:c + width, lanes] = jnp.where(keep, 1.0 / (virt - occ[:, lanes]), 0.0)
    source = lax.broadcasted_iota(I32, (1, pairs), 1)
    block = source // rows
    owner = jnp.full((1, pairs), me, I32)
    for step, key in enumerate(generators(count)):
        owner = owner ^ jnp.where((block >> step) & 1 == 1, key, 0)
    place = owner * rows + (source - block * rows)
    mine = lax.broadcasted_iota(I32, (pairs, pairs), 0)
    order_ref[...] = jnp.where(mine == place, 1.0, 0.0).astype(order_ref.dtype)
    for p in range(0, pairs, LANES):
        label_ref[p:p + LANES, :] = jnp.transpose(jnp.broadcast_to(label[:, p:p + LANES].astype(F32), (LANES, LANES)))


def ladder_kernel(
    total, tile, cd_ref, ab_ref, first_ref, second_ref, integrals_ref, weight_ref, order_ref, label_ref,
    update_ref, energy_ref, tau_ref, dense_ref,
):
    me = lax.axis_index("col")
    cols, cd_rows = integrals_ref.shape
    pairs = order_ref.shape[0]
    half, width = first_ref.shape
    window = tau_ref.shape[1]
    irreps = cd_ref.shape[0]
    tau_ref[:, :width] = jnp.dot(
        order_ref[:, :half], first_ref[...], preferred_element_type=F32
    ) + jnp.dot(order_ref[:, half:], second_ref[...], preferred_element_type=F32)
    dense_ref[:, :cd_rows] = jnp.zeros((pairs, cd_rows), dense_ref.dtype)
    lane = lax.broadcasted_iota(I32, (1, window), 1)

    def spread(g, starts):
        cd_start, ab_start = starts
        cd_end, ab_end = cd_start + cd_ref[g], ab_start + ab_ref[g]

        @pl.when((ab_end > 0) & (ab_start < cols))
        def _():
            shift = lax.rem(cd_start, LANES)
            base = pl.multiple_of(cd_start - shift, LANES)
            moved = pltpu.roll(tau_ref[...], shift, 1)
            valid = (lane >= shift) & (lane < shift + cd_ref[g])
            here = label_ref[:, :1] == g.astype(F32)
            old = dense_ref[:, pl.ds(base, window)]
            dense_ref[:, pl.ds(base, window)] = jnp.where(valid & here, moved, old.astype(F32)).astype(old.dtype)

        return cd_end, ab_end

    lax.fori_loop(0, irreps, spread, (jnp.int32(0), -me * cols))

    sizes = [s for s in (256, 512, 768, 1024, 1280, 1408, 2048) if s < cd_rows] + [cd_rows]
    sums = jnp.zeros((1, pairs), F32)
    energy_ref[...] = sums
    for t in range(0, cols, tile):
        cd_start, ab_start = jnp.int32(0), -me * cols
        begin, end = jnp.int32(0), jnp.int32(0)
        for g in range(irreps):
            cd_end, ab_end = cd_start + cd_ref[g], ab_start + ab_ref[g]
            begin = jnp.where(ab_end <= t, cd_end, begin)
            end = jnp.where(ab_start < t + tile, cd_end, end)
            cd_start, ab_start = cd_end, ab_end
        base = begin - lax.rem(begin, LANES)
        need = end - base
        below = 0
        for size in sizes:
            @pl.when((need > below) & (need <= size))
            def _(size=size):
                at = pl.multiple_of(jnp.minimum(base, cd_rows - size), LANES)
                ladder = lax.dot_general(
                    integrals_ref[t:t + tile, pl.ds(at, size)],
                    dense_ref[:, pl.ds(at, size)],
                    (((1,), (1,)), ((), ())),
                    preferred_element_type=F32,
                )
                update = ladder * weight_ref[t:t + tile, :]
                update_ref[t:t + tile, :] = update
                energy_ref[...] += jnp.sum(ladder * update, axis=0, keepdims=True)
            below = size
    energy_ref[...] = energy_ref[...] / total


def shards(tau_packed, pair_irrep, cd_sizes, ab_sizes, integrals, occ_energy, virt_energy):
    cd_rows, cols = integrals.shape
    rows, width = tau_packed.shape
    pairs = pair_irrep.shape[0]
    count = lax.axis_size("col")
    keys = generators(count)
    held = tau_packed
    for key in keys[:-1]:
        held = jnp.concatenate([held, swap(held, key, count)], axis=0)
    last = swap(held, keys[-1], count)

    vmem = pl.BlockSpec(memory_space=pltpu.VMEM)
    smem = pl.BlockSpec(memory_space=pltpu.SMEM)
    weight, order, label = pl.pallas_call(
        functools.partial(setup_kernel, count, rows),
        out_shape=(
            jax.ShapeDtypeStruct((cols, pairs), F32),
            jax.ShapeDtypeStruct((pairs, pairs), jnp.bfloat16),
            jax.ShapeDtypeStruct((pairs, LANES), F32),
        ),
        in_specs=[smem, vmem, vmem, vmem],
        out_specs=(vmem, vmem, vmem),
        cost_estimate=pl.CostEstimate(flops=10 * cols * pairs, bytes_accessed=4 * cols * pairs, transcendentals=0),
    )(ab_sizes, pair_irrep.reshape(1, pairs), occ_energy.reshape(1, pairs), virt_energy.reshape(1, cols))

    tile = 320 if cols % 320 == 0 else cols
    window = ceil_lanes(width + LANES - 1)
    turned = pltpu.with_memory_space_constraint(integrals.T, pltpu.VMEM)
    update, energy = pl.pallas_call(
        functools.partial(ladder_kernel, cols * count, tile),
        out_shape=(jax.ShapeDtypeStruct((cols, pairs), F32), jax.ShapeDtypeStruct((1, pairs), F32)),
        in_specs=[smem, smem] + [vmem] * 6,
        out_specs=(vmem, vmem),
        scratch_shapes=[pltpu.VMEM((pairs, window), F32), pltpu.VMEM((pairs, cd_rows + window), jnp.bfloat16)],
        compiler_params=pltpu.CompilerParams(vmem_limit_bytes=24 * 1024 * 1024),
        cost_estimate=pl.CostEstimate(
            flops=2 * cols * width * pairs, bytes_accessed=2 * cols * width + 4 * cols * pairs, transcendentals=0
        ),
    )(cd_sizes, ab_sizes, held, last, turned, weight, order, label)
    for key in keys:
        energy = energy + swap(energy, key, count)
    return update.T, energy.reshape(pairs)


def solution(mesh):
    placed = (
        P(("job", "col"), None),
        P("job"),
        P("job"),
        P("job"),
        P("job", "col"),
        P("job"),
        P(("job", "col")),
    )
    return jax.shard_map(
        shards, mesh=mesh, in_specs=placed, out_specs=(P("job", "col"), P("job")), check_vma=False
    )
```

time: 92 us -> 44.4 us (0.48)
  blocking collectives: 55.9 us -> 0 us
  starting transfers between devices: 0 us -> 14.4 us
  other arithmetic: 14.7 us -> 1.99 us
  waiting for transfers between devices: 0 us -> 10.9 us
  between operations: 10.8 us -> 0.65 us
  matrix products: 7.76 us -> 0 us
  local copies, waits for them, and re-layouts: 2.32 us -> 10 us
  Pallas kernels: 0 us -> 5.86 us
    psum x1 -> x0, blocking collectives: 30.3 us -> none  [shards(): pair_energy = lax.psum(partial_energy, 'col')]
    all_gather x1 -> x0, blocking collectives: 25.6 us -> none  [shards(): lax.all_gather(spread, 'col', axis=0, tiled=True)]
    ppermute x0 -> x8, starting transfers between devices: none -> 14.4 us  [swap(): return lax.ppermute(value, 'col', [(i, i ^ key) for i in range(count)])]
    ppermute x0 -> x8, waiting for transfers between devices: none -> 10.9 us  [swap(): return lax.ppermute(value, 'col', [(i, i ^ key) for i in range(count)])]
    and x4 -> x0, other arithmetic: 10.1 us -> none  [expand(): valid = (offset >= 0) & (offset < cd_sizes[label])]
    unnamed x0 -> x15, local copies, waits for them, and re-layouts: none -> 8.73 us
    dot_general x1 -> x0, matrix products: 7.76 us -> none  [shards(): jnp.dot(lax.all_gather(spread, 'col', axis=0, tiled=True), integrals, pre...]
    pallas_call x0 -> x2, Pallas kernels: none -> 5.86 us  [the longest x1 3.87 us: shards(): pl.pallas_call(functools.partial(ladder_kernel, cols * count, tile), out_...]
  transfers between devices with their start and end apart: 0 -> 8, of which waited for: 0 -> 7; matrix products, arithmetic and copies ran while one was open for 0% -> 5% of each run, Pallas kernels for 0% -> 5%
where the time goes in v1:
time: 44.4 us; the launch traced here: 43.8 us
  starting transfers between devices  14.4 us (32%)
  waiting for transfers between devices  10.9 us (25%)
  local copies, waits for them, and re-layouts  10 us (23%)
  Pallas kernels  5.86 us (13%)
  other arithmetic  1.99 us (4%)
  between operations  0.65 us (1%)
    ppermute x8, starting transfers between devices, swap(): return lax.ppermute(value, 'col', [(i, i ^ key) for i in range(count)])  14.4 us
    ppermute x8, waiting for transfers between devices, swap(): return lax.ppermute(value, 'col', [(i, i ^ key) for i in range(count)])  10.9 us
    unnamed x15, local copies, waits for them, and re-layouts  8.73 us
    pallas_call x1, Pallas kernels, shards(): pl.pallas_call(functools.partial(ladder_kernel, cols * count, tile), out_...  3.87 us
    pallas_call x1, Pallas kernels, shards(): pl.pallas_call(functools.partial(setup_kernel, count, rows), out_shape=(j...  1.99 us
    concatenate x2, other arithmetic, shards(): held = jnp.concatenate([held, swap(held, key, count)], axis=0)  1.47 us
    reshape x1, local copies, waits for them, and re-layouts, shards(): virt_energy.reshape(1, cols)  1.29 us
  transfers between devices with their start and end apart: 8, of which 7 were waited for; matrix products, arithmetic and copies ran while one was open for 5% of the time, Pallas kernels for 5%

profile of v1, /device:TPU:0, one launch (start us, length us, event | category | flops | bytes accessed | tf_op | source)
XLA Modules:
  0.0 43.8 jit_solution(7625955758097167846)
XLA Ops:
  0.6 3.5 %collective-permute-start = (bf16[8,1200]{1,0:T(8,128)(2,1)}, bf16[8,1200]{1,0:T(8,128)(2,1)S(1)}, u32[]{:S(2)}, u32[]{:S(2)}) collective-permute-start(bf16[8,1200]{1,0:T(8,128)(2,1)} %param.7), channel_id=1, source_target_pairs={{0,9},{1,8},{2,11},{3,10},{4,13},{5,12},{6,15},{7,14},{8,1},{9,0},... | collective-permute-start | bytes 57608 | tf_op jit(solution)/shard_map/ppermute | solution.py:20
  4.2 0.8 %constant_dynamic-update-slice_fusion.3 = bf16[64,1200]{1,0:T(8,128)(2,1)S(1)} fusion(bf16[8,1200]{1,0:T(8,128)(2,1)} %param.7), kind=kLoop, calls=%fused_computation.5 | loop fusion | bytes 39680
  4.9 1.0 %collective-permute-done = bf16[8,1200]{1,0:T(8,128)(2,1)S(1)} collective-permute-done((bf16[8,1200]{1,0:T(8,128)(2,1)}, bf16[8,1200]{1,0:T(8,128)(2,1)S(1)}, u32[]{:S(2)}, u32[]{:S(2)}) %collective-permute-start) | collective-permute-done | bytes 19232 | tf_op jit(solution)/shard_map/ppermute | solution.py:20
  5.9 0.7 %pad_maximum_fusion.1 = bf16[16,1200]{1,0:T(8,128)(2,1)S(1)} fusion(bf16[8,1200]{1,0:T(8,128)(2,1)S(1)} %collective-permute-done, bf16[8,1200]{1,0:T(8,128)(2,1)} %param.7), kind=kLoop, calls=%fused_computation.1 | loop fusion | flops 76800 | bytes 76800 | tf_op jit(solution)/shard_map/concatenate | solution.py:135
  6.6 1.9 %collective-permute-start.1 = (bf16[16,1200]{1,0:T(8,128)(2,1)S(1)}, bf16[16,1200]{1,0:T(8,128)(2,1)S(1)}, u32[]{:S(2)}, u32[]{:S(2)}) collective-permute-start(bf16[16,1200]{1,0:T(8,128)(2,1)S(1)} %pad_maximum_fusion.1), channel_id=1, source_target_pairs={{0,5},{1,4},{2,7},{3,6},{4,1},{5,0},{6,3},{7,2},{8,13},{9,12},{10,... | collective-permute-start | bytes 115208 | tf_op jit(solution)/shard_map/ppermute | solution.py:20
  8.5 1.7 %collective-permute-done.1 = bf16[16,1200]{1,0:T(8,128)(2,1)S(1)} collective-permute-done((bf16[16,1200]{1,0:T(8,128)(2,1)S(1)}, bf16[16,1200]{1,0:T(8,128)(2,1)S(1)}, u32[]{:S(2)}, u32[]{:S(2)}) %collective-permute-start.1) | collective-permute-done | bytes 38432 | tf_op jit(solution)/shard_map/ppermute | solution.py:20
  10.2 0.7 %pad_maximum_fusion = bf16[32,1200]{1,0:T(8,128)(2,1)S(1)} fusion(bf16[16,1200]{1,0:T(8,128)(2,1)S(1)} %collective-permute-done.1, bf16[8,1200]{1,0:T(8,128)(2,1)S(1)} %collective-permute-done, bf16[8,1200]{1,0:T(8,128)(2,1)} %param.7), kind=kLoop, calls=%fused_computation | loop fusion | flops 230400 | bytes 153600 | tf_op jit(solution)/shard_map/concatenate | solution.py:135
  10.9 1.9 %collective-permute-start.2 = (bf16[32,1200]{1,0:T(8,128)(2,1)S(1)}, bf16[32,1200]{1,0:T(8,128)(2,1)S(1)}, u32[]{:S(2)}, u32[]{:S(2)}) collective-permute-start(bf16[32,1200]{1,0:T(8,128)(2,1)S(1)} %pad_maximum_fusion), channel_id=1, source_target_pairs={{0,3},{1,2},{2,1},{3,0},{4,7},{5,6},{6,5},{7,4},{8,11},{9,10},{10,... | collective-permute-start | bytes 230408 | tf_op jit(solution)/shard_map/ppermute | solution.py:20
  12.8 2.5 %collective-permute-done.2 = bf16[32,1200]{1,0:T(8,128)(2,1)S(1)} collective-permute-done((bf16[32,1200]{1,0:T(8,128)(2,1)S(1)}, bf16[32,1200]{1,0:T(8,128)(2,1)S(1)}, u32[]{:S(2)}, u32[]{:S(2)}) %collective-permute-start.2) | collective-permute-done | bytes 76832 | tf_op jit(solution)/shard_map/ppermute | solution.py:20
  15.4 0.3 collective-permute-start.3
  15.6 1.3 %reshape.18.virt_ref = f32[1,1600]{1,0:T(1,128)} reshape(f32[1600]{0:T(1024)} %param.13) | data formatting | bytes 12800 | tf_op jit(solution)/shard_map/reshape | solution.py:150
  16.9 2.0 %shard_map.86 = (f32[1600,128]{1,0:T(8,128)}, bf16[128,128]{1,0:T(8,128)(2,1)}, f32[128,128]{1,0:T(8,128)}) custom-call(s32[8]{0:T(128)} %ab_ref.3, s32[1,128]{1,0:T(1,128)} %bitcast.7, f32[1,128]{1,0:T(1,128)} %bitcast.8, f32[1,1600]{1,0:T(1,128)} %reshape.18.virt_ref), custom_call_target="tpu_custom_call" | custom-call | flops 2048000 | bytes 819200 | tf_op jit(solution)/shard_map/pallas_call | solution.py:140
  18.9 0.0 collective-permute-done.3.second_ref
  18.9 0.0 copy-start
  18.9 3.9 %copy-done = bf16[3200,1600]{0,1:T(8,128)(2,1)S(1)} copy-done((bf16[3200,1600]{0,1:T(8,128)(2,1)S(1)}, bf16[3200,1600]{0,1:T(8,128)(2,1)}, u32[]{:S(2)}) %copy-start) | copy-done | bytes 10240024
  22.8 0.0 copy-start.1
  22.8 1.1 %copy-done.1 = f32[1600,128]{1,0:T(8,128)S(1)} copy-done((f32[1600,128]{1,0:T(8,128)S(1)}, f32[1600,128]{1,0:T(8,128)}, u32[]{:S(2)}) %copy-start.1) | copy-done | bytes 819224
  24.0 0.0 copy-start.2
  24.0 0.8 %copy-done.2 = f32[128,128]{1,0:T(8,128)S(1)} copy-done((f32[128,128]{1,0:T(8,128)S(1)}, f32[128,128]{1,0:T(8,128)}, u32[]{:S(2)}) %copy-start.2) | copy-done | bytes 65560
  24.8 0.0 copy-start.3
  24.8 0.8 %copy-done.3 = bf16[128,128]{1,0:T(8,128)(2,1)S(1)} copy-done((bf16[128,128]{1,0:T(8,128)(2,1)S(1)}, bf16[128,128]{1,0:T(8,128)(2,1)}, u32[]{:S(2)}) %copy-start.3) | copy-done | bytes 32792
  25.6 0.0 copy-start.4
  25.6 0.7 %copy-done.4 = s32[8]{0:T(128)S(1)} copy-done((s32[8]{0:T(128)S(1)}, s32[8]{0:T(128)}, u32[]{:S(2)}) %copy-start.4) | copy-done | bytes 56
  26.2 0.0 copy-start.5
  26.2 0.7 %copy-done.5 = s32[8]{0:T(128)S(1)} copy-done((s32[8]{0:T(128)S(1)}, s32[8]{0:T(128)}, u32[]{:S(2)}) %copy-start.5) | copy-done | bytes 56
  26.9 3.9 %shard_map.87 = (f32[1600,128]{1,0:T(8,128)}, f32[1,128]{1,0:T(1,128)S(1)}) custom-call(s32[8]{0:T(128)S(1)} %copy-done.5, s32[8]{0:T(128)S(1)} %copy-done.4, bf16[64,1200]{1,0:T(8,128)(2,1)S(1)} %constant_dynamic-update-slice_fusion.first_ref, bf16[64,1200]{1,0:T(8,128)(2,1)S(1)} %collective-permute-done.3.second_ref, bf16[1600,3200]{1,0:T(8,128)(2,1)S(1)} %bitcast.6, ...), custom_call_target="tpu_custom_call" | custom-call | flops 491520000 | bytes 4659200 | tf_op jit(solution)/shard_map/pallas_call | solution.py:155
  30.8 3.7 %collective-permute-start.4 = (f32[1,128]{1,0:T(1,128)S(1)}, f32[1,128]{1,0:T(1,128)S(1)}, u32[]{:S(2)}, u32[]{:S(2)}) collective-permute-start(f32[1,128]{1,0:T(1,128)S(1)} %get-tuple-element.11), channel_id=1, source_target_pairs={{0,9},{1,8},{2,11},{3,10},{4,13},{5,12},{6,15},{7,14},{8,1},{9,0},... | collective-permute-start | bytes 1544 | tf_op jit(solution)/shard_map/ppermute | solution.py:20
  34.5 1.3 %collective-permute-done.4 = f32[1,128]{1,0:T(1,128)S(1)} collective-permute-done((f32[1,128]{1,0:T(1,128)S(1)}, f32[1,128]{1,0:T(1,128)S(1)}, u32[]{:S(2)}, u32[]{:S(2)}) %collective-permute-start.4) | collective-permute-done | bytes 544 | tf_op jit(solution)/shard_map/ppermute | solution.py:20
  35.8 2.1 %collective-permute-start.5 = (f32[1,128]{1,0:T(1,128)S(1)}, f32[1,128]{1,0:T(1,128)S(1)}, u32[]{:S(2)}, u32[]{:S(2)}) collective-permute-start(f32[1,128]{1,0:T(1,128)S(1)} %add.12), channel_id=1, source_target_pairs={{0,5},{1,4},{2,7},{3,6},{4,1},{5,0},{6,3},{7,2},{8,13},{9,12},{10,... | collective-permute-start | bytes 1544 | tf_op jit(solution)/shard_map/ppermute | solution.py:20
  37.9 1.3 %collective-permute-done.5 = f32[1,128]{1,0:T(1,128)S(1)} collective-permute-done((f32[1,128]{1,0:T(1,128)S(1)}, f32[1,128]{1,0:T(1,128)S(1)}, u32[]{:S(2)}, u32[]{:S(2)}) %collective-permute-start.5) | collective-permute-done | bytes 544 | tf_op jit(solution)/shard_map/ppermute | solution.py:20
  39.2 1.0 %collective-permute-start.6 = (f32[1,128]{1,0:T(1,128)S(1)}, f32[1,128]{1,0:T(1,128)S(1)}, u32[]{:S(2)}, u32[]{:S(2)}) collective-permute-start(f32[1,128]{1,0:T(1,128)S(1)} %add.13), channel_id=1, source_target_pairs={{0,3},{1,2},{2,1},{3,0},{4,7},{5,6},{6,5},{7,4},{8,11},{9,10},{10,... | collective-permute-start | bytes 1544 | tf_op jit(solution)/shard_map/ppermute | solution.py:20
  40.2 2.0 %collective-permute-done.6 = f32[1,128]{1,0:T(1,128)S(1)} collective-permute-done((f32[1,128]{1,0:T(1,128)S(1)}, f32[1,128]{1,0:T(1,128)S(1)}, u32[]{:S(2)}, u32[]{:S(2)}) %collective-permute-start.6) | collective-permute-done | bytes 544 | tf_op jit(solution)/shard_map/ppermute | solution.py:20
  42.2 0.0 collective-permute-start.7
  42.2 1.1 %collective-permute-done.7 = f32[1,128]{1,0:T(1,128)S(1)} collective-permute-done((f32[1,128]{1,0:T(1,128)S(1)}, f32[1,128]{1,0:T(1,128)S(1)}, u32[]{:S(2)}, u32[]{:S(2)}) %collective-permute-start.7) | collective-permute-done | bytes 544 | tf_op jit(solution)/shard_map/ppermute | solution.py:20
  43.3 0.5 %add_bitcast_fusion = f32[128]{0:T(128)} fusion(f32[1,128]{1,0:T(1,128)S(1)} %add.14, f32[1,128]{1,0:T(1,128)S(1)} %collective-permute-done.7), kind=kLoop, calls=%fused_computation.6 | loop fusion | flops 128 | bytes 1536 | tf_op jit(solution)/shard_map/reshape | solution.py:168
  (6 shorter events, 0.0 us)
Async XLA Ops:
  0.6 5.3 %collective-permute-start = (bf16[8,1200]{1,0:T(8,128)(2,1)}, bf16[8,1200]{1,0:T(8,128)(2,1)S(1)}, u32[]{:S(2)}, u32[]{:S(2)}) collective-permute-start(bf16[8,1200]{1,0:T(8,128)(2,1)} %param.7), channel_id=1, source_target_pairs={{0,9},{1,8},{2,11},{3,10},{4,13},{5,12},{6,15},{7,14},{8,1},{9,0},... | collective-permute-start | bytes 57608 | tf_op jit(solution)/shard_map/ppermute | solution.py:20
  6.6 3.5 %collective-permute-start.1 = (bf16[16,1200]{1,0:T(8,128)(2,1)S(1)}, bf16[16,1200]{1,0:T(8,128)(2,1)S(1)}, u32[]{:S(2)}, u32[]{:S(2)}) collective-permute-start(bf16[16,1200]{1,0:T(8,128)(2,1)S(1)} %pad_maximum_fusion.1), channel_id=1, source_target_pairs={{0,5},{1,4},{2,7},{3,6},{4,1},{5,0},{6,3},{7,2},{8,13},{9,12},{10,... | collective-permute-start | bytes 115208 | tf_op jit(solution)/shard_map/ppermute | solution.py:20
  10.9 4.4 %collective-permute-start.2 = (bf16[32,1200]{1,0:T(8,128)(2,1)S(1)}, bf16[32,1200]{1,0:T(8,128)(2,1)S(1)}, u32[]{:S(2)}, u32[]{:S(2)}) collective-permute-start(bf16[32,1200]{1,0:T(8,128)(2,1)S(1)} %pad_maximum_fusion), channel_id=1, source_target_pairs={{0,3},{1,2},{2,1},{3,0},{4,7},{5,6},{6,5},{7,4},{8,11},{9,10},{10,... | collective-permute-start | bytes 230408 | tf_op jit(solution)/shard_map/ppermute | solution.py:20
  15.4 3.6 %collective-permute-start.3 = (bf16[64,1200]{1,0:T(8,128)(2,1)S(1)}, bf16[64,1200]{1,0:T(8,128)(2,1)S(1)}, u32[]{:S(2)}, u32[]{:S(2)}) collective-permute-start(bf16[64,1200]{1,0:T(8,128)(2,1)S(1)} %constant_dynamic-update-slice_fusion.first_ref), channel_id=1, source_target_pairs={{0,1},{1,0},{2,3},{3,2},{4,5},{5,4},{6,7},{7,6},{8,9},{9,8},{10,11... | collective-permute-start | bytes 460808 | tf_op jit(solution)/shard_map/ppermute | solution.py:20
  18.9 3.9 %copy-start = (bf16[3200,1600]{0,1:T(8,128)(2,1)S(1)}, bf16[3200,1600]{0,1:T(8,128)(2,1)}, u32[]{:S(2)}) copy-start(bf16[3200,1600]{0,1:T(8,128)(2,1)} %param.11) | copy-start | bytes 30720004
  22.8 1.1 %copy-start.1 = (f32[1600,128]{1,0:T(8,128)S(1)}, f32[1600,128]{1,0:T(8,128)}, u32[]{:S(2)}) copy-start(f32[1600,128]{1,0:T(8,128)} %get-tuple-element.7.weight_ref) | copy-start | bytes 2457604
  24.0 0.8 %copy-start.2 = (f32[128,128]{1,0:T(8,128)S(1)}, f32[128,128]{1,0:T(8,128)}, u32[]{:S(2)}) copy-start(f32[128,128]{1,0:T(8,128)} %get-tuple-element.9.label_ref) | copy-start | bytes 196612
  24.8 0.8 %copy-start.3 = (bf16[128,128]{1,0:T(8,128)(2,1)S(1)}, bf16[128,128]{1,0:T(8,128)(2,1)}, u32[]{:S(2)}) copy-start(bf16[128,128]{1,0:T(8,128)(2,1)} %get-tuple-element.8.order_ref) | copy-start | bytes 98308
  25.6 0.7 %copy-start.4 = (s32[8]{0:T(128)S(1)}, s32[8]{0:T(128)}, u32[]{:S(2)}) copy-start(s32[8]{0:T(128)} %ab_ref.3) | copy-start | bytes 100
  26.2 0.7 %copy-start.5 = (s32[8]{0:T(128)S(1)}, s32[8]{0:T(128)}, u32[]{:S(2)}) copy-start(s32[8]{0:T(128)} %cd_ref.1) | copy-start | bytes 100
  30.8 5.0 %collective-permute-start.4 = (f32[1,128]{1,0:T(1,128)S(1)}, f32[1,128]{1,0:T(1,128)S(1)}, u32[]{:S(2)}, u32[]{:S(2)}) collective-permute-start(f32[1,128]{1,0:T(1,128)S(1)} %get-tuple-element.11), channel_id=1, source_target_pairs={{0,9},{1,8},{2,11},{3,10},{4,13},{5,12},{6,15},{7,14},{8,1},{9,0},... | collective-permute-start | bytes 1544 | tf_op jit(solution)/shard_map/ppermute | solution.py:20
  35.8 3.4 %collective-permute-start.5 = (f32[1,128]{1,0:T(1,128)S(1)}, f32[1,128]{1,0:T(1,128)S(1)}, u32[]{:S(2)}, u32[]{:S(2)}) collective-permute-start(f32[1,128]{1,0:T(1,128)S(1)} %add.12), channel_id=1, source_target_pairs={{0,5},{1,4},{2,7},{3,6},{4,1},{5,0},{6,3},{7,2},{8,13},{9,12},{10,... | collective-permute-start | bytes 1544 | tf_op jit(solution)/shard_map/ppermute | solution.py:20
  39.2 3.0 %collective-permute-start.6 = (f32[1,128]{1,0:T(1,128)S(1)}, f32[1,128]{1,0:T(1,128)S(1)}, u32[]{:S(2)}, u32[]{:S(2)}) collective-permute-start(f32[1,128]{1,0:T(1,128)S(1)} %add.13), channel_id=1, source_target_pairs={{0,3},{1,2},{2,1},{3,0},{4,7},{5,6},{6,5},{7,4},{8,11},{9,10},{10,... | collective-permute-start | bytes 1544 | tf_op jit(solution)/shard_map/ppermute | solution.py:20
  42.2 1.1 %collective-permute-start.7 = (f32[1,128]{1,0:T(1,128)S(1)}, f32[1,128]{1,0:T(1,128)S(1)}, u32[]{:S(2)}, u32[]{:S(2)}) collective-permute-start(f32[1,128]{1,0:T(1,128)S(1)} %add.14), channel_id=1, source_target_pairs={{0,1},{1,0},{2,3},{3,2},{4,5},{5,4},{6,7},{7,6},{8,9},{9,8},{10,11... | collective-permute-start | bytes 1544 | tf_op jit(solution)/shard_map/ppermute | solution.py:20

commit v2 on v1

--- a/solution.py
+++ b/solution.py
@@ -24,10 +24,63 @@
     return -(-extent // LANES) * LANES
 
 
-def setup_kernel(count, rows, ab_ref, irrep_ref, occ_ref, virt_ref, weight_ref, order_ref, label_ref):
+def window_sizes(cd_rows):
+    return [size for size in (256, 512, 768, 1024, 1280, 1408, 2048) if size < cd_rows] + [cd_rows]
+
+
+def windows(cd_ref, ab_ref, me, cols, tile, cd_rows):
+    found = []
+    for t in range(0, cols, tile):
+        cd_start, ab_start = jnp.int32(0), -me * cols
+        begin, end = jnp.int32(0), jnp.int32(0)
+        for g in range(cd_ref.shape[0]):
+            cd_end, ab_end = cd_start + cd_ref[g], ab_start + ab_ref[g]
+            begin = jnp.where(ab_end <= t, cd_end, begin)
+            end = jnp.where(ab_start < t + tile, cd_end, end)
+            cd_start, ab_start = cd_end, ab_end
+        base = begin - lax.rem(begin, LANES)
+        size = jnp.int32(cd_rows)
+        for choice in reversed(window_sizes(cd_rows)):
+            size = jnp.where(end - base <= choice, choice, size)
+        found.append((jnp.minimum(base, cd_rows - size), size))
+    return found
+
+
+def copy_kernel(source_ref, result_ref):
+    result_ref[...] = source_ref[...]
+
+
+def setup_kernel(
+    count, rows, tile, cd_hbm, ab_hbm, irrep_hbm, occ_hbm, virt_ref, integrals_ref,
+    weight_ref, order_ref, label_ref, packed_ref, table_ref, cd_ref, ab_ref, irrep_ref, occ_ref, arrived, here,
+):
+    small = [
+        pltpu.make_async_copy(source, target, here.at[i])
+        for i, (source, target) in enumerate(
+            ((cd_hbm, cd_ref), (ab_hbm, ab_ref), (irrep_hbm, irrep_ref), (occ_hbm, occ_ref))
+        )
+    ]
+    for copy in small:
+        copy.start()
     me = lax.axis_index("col")
     pairs = irrep_ref.shape[1]
-    cols = weight_ref.shape[0]
+    cols, cd_rows = integrals_ref.shape
+    for copy in small:
+        copy.wait()
+    tiles = windows(cd_ref, ab_ref, me, cols, tile, cd_rows)
+
+    def each_copy(act):
+        for t, (at, size) in enumerate(tiles):
+            for choice in window_sizes(cd_rows):
+                @pl.when(size == choice)
+                def _():
+                    part = (pl.ds(t * tile, tile), pl.ds(pl.multiple_of(at, LANES), choice))
+                    act(pltpu.make_async_copy(integrals_ref.at[part], packed_ref.at[part], arrived.at[t]))
+
+    each_copy(lambda copy: copy.start())
+    for t, (at, size) in enumerate(tiles):
+        table_ref[2 * t] = at
+        table_ref[2 * t + 1] = size
     label = irrep_ref[...]
     low = jnp.zeros((1, pairs), I32)
     high = jnp.zeros((1, pairs), I32)
@@ -57,14 +110,15 @@
     order_ref[...] = jnp.where(mine == place, 1.0, 0.0).astype(order_ref.dtype)
     for p in range(0, pairs, LANES):
         label_ref[p:p + LANES, :] = jnp.transpose(jnp.broadcast_to(label[:, p:p + LANES].astype(F32), (LANES, LANES)))
+    each_copy(lambda copy: copy.wait())
 
 
 def ladder_kernel(
-    total, tile, cd_ref, ab_ref, first_ref, second_ref, integrals_ref, weight_ref, order_ref, label_ref,
+    total, tile, cd_ref, ab_ref, table_ref, first_ref, second_ref, packed_ref, weight_ref, order_ref, label_ref,
     update_ref, energy_ref, tau_ref, dense_ref,
 ):
     me = lax.axis_index("col")
-    cols, cd_rows = integrals_ref.shape
+    cols, cd_rows = packed_ref.shape
     pairs = order_ref.shape[0]
     half, width = first_ref.shape
     window = tau_ref.shape[1]
@@ -92,35 +146,22 @@
         return cd_end, ab_end
 
     lax.fori_loop(0, irreps, spread, (jnp.int32(0), -me * cols))
-
-    sizes = [s for s in (256, 512, 768, 1024, 1280, 1408, 2048) if s < cd_rows] + [cd_rows]
-    sums = jnp.zeros((1, pairs), F32)
-    energy_ref[...] = sums
-    for t in range(0, cols, tile):
-        cd_start, ab_start = jnp.int32(0), -me * cols
-        begin, end = jnp.int32(0), jnp.int32(0)
-        for g in range(irreps):
-            cd_end, ab_end = cd_start + cd_ref[g], ab_start + ab_ref[g]
-            begin = jnp.where(ab_end <= t, cd_end, begin)
-            end = jnp.where(ab_start < t + tile, cd_end, end)
-            cd_start, ab_start = cd_end, ab_end
-        base = begin - lax.rem(begin, LANES)
-        need = end - base
-        below = 0
-        for size in sizes:
-            @pl.when((need > below) & (need <= size))
-            def _(size=size):
-                at = pl.multiple_of(jnp.minimum(base, cd_rows - size), LANES)
+    energy_ref[...] = jnp.zeros((1, pairs), F32)
+    for t in range(cols // tile):
+        here = pl.ds(t * tile, tile)
+        at, size = pl.multiple_of(table_ref[2 * t], LANES), table_ref[2 * t + 1]
+        for choice in window_sizes(cd_rows):
+            @pl.when(size == choice)
+            def _():
                 ladder = lax.dot_general(
-                    integrals_ref[t:t + tile, pl.ds(at, size)],
-                    dense_ref[:, pl.ds(at, size)],
+                    packed_ref[here, pl.ds(at, choice)],
+                    dense_ref[:, pl.ds(at, choice)],
                     (((1,), (1,)), ((), ())),
                     preferred_element_type=F32,
                 )
-                update = ladder * weight_ref[t:t + tile, :]
-                update_ref[t:t + tile, :] = update
+                update = ladder * weight_ref[here, :]
+                update_ref[here, :] = update
                 energy_ref[...] += jnp.sum(ladder * update, axis=0, keepdims=True)
-            below = size
     energy_ref[...] = energy_ref[...] / total
 
 
@@ -130,39 +171,71 @@
     pairs = pair_irrep.shape[0]
     count = lax.axis_size("col")
     keys = generators(count)
-    held = tau_packed
-    for key in keys[:-1]:
-        held = jnp.concatenate([held, swap(held, key, count)], axis=0)
-    last = swap(held, keys[-1], count)
-
+    tile = 320 if cols % 320 == 0 else cols
+    window = ceil_lanes(width + LANES - 1)
     vmem = pl.BlockSpec(memory_space=pltpu.VMEM)
     smem = pl.BlockSpec(memory_space=pltpu.SMEM)
-    weight, order, label = pl.pallas_call(
-        functools.partial(setup_kernel, count, rows),
-        out_shape=(
-            jax.ShapeDtypeStruct((cols, pairs), F32),
-            jax.ShapeDtypeStruct((pairs, pairs), jnp.bfloat16),
-            jax.ShapeDtypeStruct((pairs, LANES), F32),
-        ),
-        in_specs=[smem, vmem, vmem, vmem],
-        out_specs=(vmem, vmem, vmem),
-        cost_estimate=pl.CostEstimate(flops=10 * cols * pairs, bytes_accessed=4 * cols * pairs, transcendentals=0),
-    )(ab_sizes, pair_irrep.reshape(1, pairs), occ_energy.reshape(1, pairs), virt_energy.reshape(1, cols))
-
-    tile = 320 if cols % 320 == 0 else cols
-    window = ceil_lanes(width + LANES - 1)
-    turned = pltpu.with_memory_space_constraint(integrals.T, pltpu.VMEM)
+    anywhere = pl.BlockSpec(memory_space=pl.ANY)
+    near = lambda value: pltpu.with_memory_space_constraint(value, pltpu.VMEM)
+
+    far = lambda value: pltpu.with_memory_space_constraint(value, pltpu.HBM)
+
+    virt_row = virt_energy.reshape(1, cols)
+    held = pl.pallas_call(
+        copy_kernel, out_shape=pltpu.VMEM(tau_packed.shape, tau_packed.dtype), in_specs=[vmem], out_specs=vmem,
+        compiler_params=pltpu.CompilerParams(vmem_limit_bytes=1 << 20),
+    )(tau_packed)
+    sent = tau_packed
+    for step, key in enumerate(keys[:-1]):
+        got = swap(sent, key, count)
+        held = sent = jnp.concatenate([held, got], axis=0)
+        if step == 1:
+            sent, occ_energy = lax.optimization_barrier((held, occ_energy))
+            held = sent
+            weight, order, label, packed, table = pl.pallas_call(
+                functools.partial(setup_kernel, count, rows, tile),
+                out_shape=(
+                    pltpu.VMEM((cols, pairs), F32),
+                    pltpu.VMEM((pairs, pairs), jnp.bfloat16),
+                    pltpu.VMEM((pairs, LANES), F32),
+                    pltpu.VMEM((cols, cd_rows), integrals.dtype),
+                    pltpu.SMEM((2 * (cols // tile),), I32),
+                ),
+                in_specs=[anywhere] * 4 + [vmem, anywhere],
+                out_specs=(vmem, vmem, vmem, vmem, smem),
+                scratch_shapes=[
+                    pltpu.SMEM(cd_sizes.shape, I32),
+                    pltpu.SMEM(ab_sizes.shape, I32),
+                    pltpu.VMEM((1, pairs), I32),
+                    pltpu.VMEM((1, pairs), F32),
+                    pltpu.SemaphoreType.DMA((cols // tile,)),
+                    pltpu.SemaphoreType.DMA((4,)),
+                ],
+                compiler_params=pltpu.CompilerParams(vmem_limit_bytes=(2 << 20) + 32 * pairs * pairs),
+                cost_estimate=pl.CostEstimate(flops=10 * cols * pairs, bytes_accessed=4 * cols * pairs, transcendentals=0),
+            )(
+                far(cd_sizes), far(ab_sizes), far(pair_irrep.reshape(1, pairs)), far(occ_energy.reshape(1, pairs)),
+                near(virt_row), far(integrals.T),
+            )
+        elif step == 0:
+            held, virt_row = lax.optimization_barrier((held, virt_row))
+            sent = held
+    sent, order = lax.optimization_barrier((sent, order))
+    last = swap(sent, keys[-1], count)
     update, energy = pl.pallas_call(
         functools.partial(ladder_kernel, cols * count, tile),
-        out_shape=(jax.ShapeDtypeStruct((cols, pairs), F32), jax.ShapeDtypeStruct((1, pairs), F32)),
-        in_specs=[smem, smem] + [vmem] * 6,
+        out_shape=(pltpu.VMEM((cols, pairs), F32), pltpu.VMEM((1, pairs), F32)),
+        in_specs=[smem, smem, smem] + [vmem] * 6,
         out_specs=(vmem, vmem),
         scratch_shapes=[pltpu.VMEM((pairs, window), F32), pltpu.VMEM((pairs, cd_rows + window), jnp.bfloat16)],
-        compiler_params=pltpu.CompilerParams(vmem_limit_bytes=24 * 1024 * 1024),
+        compiler_params=pltpu.CompilerParams(vmem_limit_bytes=(8 << 20) + 32768 * pairs),
         cost_estimate=pl.CostEstimate(
             flops=2 * cols * width * pairs, bytes_accessed=2 * cols * width + 4 * cols * pairs, transcendentals=0
         ),
-    )(cd_sizes, ab_sizes, held, last, turned, weight, order, label)
+    )(
+        cd_sizes, ab_sizes, pltpu.with_memory_space_constraint(table, pltpu.SMEM),
+        near(sent), near(last), near(packed), near(weight), near(order), near(label),
+    )
     for key in keys:
         energy = energy + swap(energy, key, count)
     return update.T, energy.reshape(pairs)

time: 44.4 us -> 31.8 us (0.72); the launches traced: 43.8 us -> 31.7 us
  local copies, waits for them, and re-layouts: 10 us -> 2.38 us
  waiting for transfers between devices: 10.9 us -> 7.37 us
  other arithmetic: 1.99 us -> 0.56 us
  starting transfers between devices: 14.4 us -> 15.5 us
  Pallas kernels: 5.86 us -> 5.2 us
    unnamed x15 -> x7, local copies, waits for them, and re-layouts: 8.73 us -> 1.66 us
    ppermute x8, waiting for transfers between devices: 10.9 us -> 7.37 us  [swap(): return lax.ppermute(value, 'col', [(i, i ^ key) for i in range(count)])]
    concatenate x2 -> x3, other arithmetic: 1.47 us -> 0.03 us  [shards(): held = sent = jnp.concatenate([held, got], axis=0)]
    ppermute x8, starting transfers between devices: 14.4 us -> 15.5 us  [swap(): return lax.ppermute(value, 'col', [(i, i ^ key) for i in range(count)])]
    pallas_call x1, Pallas kernels: 3.87 us -> 2.83 us  [shards(): pl.pallas_call(functools.partial(ladder_kernel, cols * count, tile), out_...]
    reshape x1, local copies, waits for them, and re-layouts: 1.29 us -> 0.73 us  [shards(): virt_row = virt_energy.reshape(1, cols)]
    pallas_call x1 -> x2, Pallas kernels: 1.99 us -> 2.37 us  [the longest x1 2.37 us: shards(): pl.pallas_call(functools.partial(setup_kernel, count, rows, tile), out_sh...]
  transfers between devices with their start and end apart: 8 -> 8, of which waited for: 7 -> 7; matrix products, arithmetic and copies ran while one was open for 5% -> 5% of each run, Pallas kernels for 5% -> 7%
where the time goes in v2:
time: 31.8 us; the launch traced here: 31.7 us
  starting transfers between devices  15.5 us (49%)
  waiting for transfers between devices  7.37 us (23%)
  Pallas kernels  5.2 us (16%)
  local copies, waits for them, and re-layouts  2.38 us (7%)
  between operations  0.67 us (2%)
  other arithmetic  0.56 us (2%)
    ppermute x8, starting transfers between devices, swap(): return lax.ppermute(value, 'col', [(i, i ^ key) for i in range(count)])  15.5 us
    ppermute x8, waiting for transfers between devices, swap(): return lax.ppermute(value, 'col', [(i, i ^ key) for i in range(count)])  7.37 us
    pallas_call x1, Pallas kernels, shards(): pl.pallas_call(functools.partial(ladder_kernel, cols * count, tile), out_...  2.83 us
    pallas_call x1, Pallas kernels, shards(): pl.pallas_call(functools.partial(setup_kernel, count, rows, tile), out_sh...  2.37 us
    unnamed x7, local copies, waits for them, and re-layouts  1.66 us
    reshape x1, local copies, waits for them, and re-layouts, shards(): virt_row = virt_energy.reshape(1, cols)  0.73 us
  transfers between devices with their start and end apart: 8, of which 7 were waited for; matrix products, arithmetic and copies ran while one was open for 5% of the time, Pallas kernels for 7%

profile of v2, /device:TPU:0, one launch (start us, length us, event | category | flops | bytes accessed | tf_op | source)
XLA Modules:
  0.0 31.7 jit_solution(4447107878170481504)
XLA Ops:
  0.6 3.5 %collective-permute-start = (bf16[8,1200]{1,0:T(8,128)(2,1)}, bf16[8,1200]{1,0:T(8,128)(2,1)S(1)}, u32[]{:S(2)}, u32[]{:S(2)}) collective-permute-start(bf16[8,1200]{1,0:T(8,128)(2,1)} %source_ref.1), channel_id=1, source_target_pairs={{0,9},{1,8},{2,11},{3,10},{4,13},{5,12},{6,15},{7,14},{8,1},{9,0},... | collective-permute-start | bytes 57608 | tf_op jit(solution)/shard_map/ppermute | solution.py:20
  4.2 0.0 copy-start
  4.2 0.8 %copy-done = bf16[8,1200]{1,0:T(8,128)(2,1)S(1)} copy-done((bf16[8,1200]{1,0:T(8,128)(2,1)S(1)}, bf16[8,1200]{1,0:T(8,128)(2,1)}, u32[]{:S(2)}) %copy-start) | copy-done | bytes 19224
  4.9 0.0 copy-start.1
  4.9 0.0 copy-start.2
  4.9 0.7 %reshape.17.virt_ref = f32[1,1600]{1,0:T(1,128)S(1)} reshape(f32[1600]{0:T(1024)} %param.13) | data formatting | bytes 12800 | tf_op jit(solution)/shard_map/reshape | solution.py:183
  5.7 0.2 collective-permute-done
  5.9 1.9 %collective-permute-start.1 = (bf16[16,1200]{1,0:T(8,128)(2,1)S(1)}, bf16[16,1200]{1,0:T(8,128)(2,1)S(1)}, u32[]{:S(2)}, u32[]{:S(2)}) collective-permute-start(bf16[16,1200]{1,0:T(8,128)(2,1)S(1)} %pad_maximum_fusion.2), channel_id=1, source_target_pairs={{0,5},{1,4},{2,7},{3,6},{4,1},{5,0},{6,3},{7,2},{8,13},{9,12},{10,... | collective-permute-start | bytes 115208 | tf_op jit(solution)/shard_map/ppermute | solution.py:20
  7.8 1.7 %collective-permute-done.1 = bf16[16,1200]{1,0:T(8,128)(2,1)S(1)} collective-permute-done((bf16[16,1200]{1,0:T(8,128)(2,1)S(1)}, bf16[16,1200]{1,0:T(8,128)(2,1)S(1)}, u32[]{:S(2)}, u32[]{:S(2)}) %collective-permute-start.1) | collective-permute-done | bytes 38432 | tf_op jit(solution)/shard_map/ppermute | solution.py:20
  9.5 1.9 %collective-permute-start.2 = (bf16[32,1200]{1,0:T(8,128)(2,1)S(1)}, bf16[32,1200]{1,0:T(8,128)(2,1)S(1)}, u32[]{:S(2)}, u32[]{:S(2)}) collective-permute-start(bf16[32,1200]{1,0:T(8,128)(2,1)S(1)} %pad_maximum_fusion.1), channel_id=1, source_target_pairs={{0,3},{1,2},{2,1},{3,0},{4,7},{5,6},{6,5},{7,4},{8,11},{9,10},{10,... | collective-permute-start | bytes 230408 | tf_op jit(solution)/shard_map/ppermute | solution.py:20
  11.4 2.4 %shard_map.87 = (f32[1600,128]{1,0:T(8,128)S(1)}, bf16[128,128]{1,0:T(8,128)(2,1)S(1)}, f32[128,128]{1,0:T(8,128)S(1)}, bf16[1600,3200]{1,0:T(8,128)(2,1)S(1)}, s32[10]{0:T(128)S(4)}) custom-call(s32[8]{0:T(128)} %cd_ref.1, s32[8]{0:T(128)} %ab_ref.1, s32[1,128]{1,0:T(1,128)} %bitcast.8, f32[1,128]{1,0:T(1,128)} %bitcast.9, f32[1,1600]{1,0:T(1,128)S(1)} %reshape.17.virt_ref, ...), custom_call_target="tpu_custom_call" | custom-call | flops 2048000 | bytes 819200 | tf_op jit(solution)/shard_map/pallas_call | solution.py:195
  13.8 0.2 collective-permute-done.2
  14.0 0.3 %collective-permute-start.3 = (bf16[64,1200]{1,0:T(8,128)(2,1)S(1)}, bf16[64,1200]{1,0:T(8,128)(2,1)S(1)}, u32[]{:S(2)}, u32[]{:S(2)}) collective-permute-start(bf16[64,1200]{1,0:T(8,128)(2,1)S(1)} %pad_maximum_fusion.first_ref), channel_id=1, source_target_pairs={{0,1},{1,0},{2,3},{3,2},{4,5},{5,4},{6,7},{7,6},{8,9},{9,8},{10,11... | collective-permute-start | bytes 460808 | tf_op jit(solution)/shard_map/ppermute | solution.py:20
  14.3 1.1 %collective-permute-done.3.second_ref = bf16[64,1200]{1,0:T(8,128)(2,1)S(1)} collective-permute-done((bf16[64,1200]{1,0:T(8,128)(2,1)S(1)}, bf16[64,1200]{1,0:T(8,128)(2,1)S(1)}, u32[]{:S(2)}, u32[]{:S(2)}) %collective-permute-start.3) | collective-permute-done | bytes 153632 | tf_op jit(solution)/shard_map/ppermute | solution.py:20
  15.4 0.0 copy-done.1
  15.4 0.0 copy-done.2
  15.4 2.8 %shard_map.88 = (f32[1600,128]{1,0:T(8,128)S(1)}, f32[1,128]{1,0:T(1,128)S(1)}) custom-call(s32[8]{0:T(128)S(1)} %copy-done.1, s32[8]{0:T(128)S(1)} %copy-done.2, s32[10]{0:T(128)S(4)} %get-tuple-element.18.table_ref, bf16[64,1200]{1,0:T(8,128)(2,1)S(1)} %pad_maximum_fusion.first_ref, bf16[64,1200]{1,0:T(8,128)(2,1)S(1)} %collective-permute-done.3.second_ref, ...), custom_call_target="tpu_custom_call" | custom-call | flops 491520000 | bytes 4659200 | tf_op jit(solution)/shard_map/pallas_call | solution.py:225
  18.3 3.2 %collective-permute-start.4 = (f32[1,128]{1,0:T(1,128)S(1)}, f32[1,128]{1,0:T(1,128)S(1)}, u32[]{:S(2)}, u32[]{:S(2)}) collective-permute-start(f32[1,128]{1,0:T(1,128)S(1)} %get-tuple-element.27), channel_id=1, source_target_pairs={{0,9},{1,8},{2,11},{3,10},{4,13},{5,12},{6,15},{7,14},{8,1},{9,0},... | collective-permute-start | bytes 1544 | tf_op jit(solution)/shard_map/ppermute | solution.py:20
  21.4 1.3 %collective-permute-done.4 = f32[1,128]{1,0:T(1,128)S(1)} collective-permute-done((f32[1,128]{1,0:T(1,128)S(1)}, f32[1,128]{1,0:T(1,128)S(1)}, u32[]{:S(2)}, u32[]{:S(2)}) %collective-permute-start.4) | collective-permute-done | bytes 544 | tf_op jit(solution)/shard_map/ppermute | solution.py:20
  22.7 2.7 %collective-permute-start.5 = (f32[1,128]{1,0:T(1,128)S(1)}, f32[1,128]{1,0:T(1,128)S(1)}, u32[]{:S(2)}, u32[]{:S(2)}) collective-permute-start(f32[1,128]{1,0:T(1,128)S(1)} %add.12), channel_id=1, source_target_pairs={{0,5},{1,4},{2,7},{3,6},{4,1},{5,0},{6,3},{7,2},{8,13},{9,12},{10,... | collective-permute-start | bytes 1544 | tf_op jit(solution)/shard_map/ppermute | solution.py:20
  25.4 1.3 %collective-permute-done.5 = f32[1,128]{1,0:T(1,128)S(1)} collective-permute-done((f32[1,128]{1,0:T(1,128)S(1)}, f32[1,128]{1,0:T(1,128)S(1)}, u32[]{:S(2)}, u32[]{:S(2)}) %collective-permute-start.5) | collective-permute-done | bytes 544 | tf_op jit(solution)/shard_map/ppermute | solution.py:20
  26.7 1.4 %collective-permute-start.6 = (f32[1,128]{1,0:T(1,128)S(1)}, f32[1,128]{1,0:T(1,128)S(1)}, u32[]{:S(2)}, u32[]{:S(2)}) collective-permute-start(f32[1,128]{1,0:T(1,128)S(1)} %add.13), channel_id=1, source_target_pairs={{0,3},{1,2},{2,1},{3,0},{4,7},{5,6},{6,5},{7,4},{8,11},{9,10},{10,... | collective-permute-start | bytes 1544 | tf_op jit(solution)/shard_map/ppermute | solution.py:20
  28.1 1.6 %collective-permute-done.6 = f32[1,128]{1,0:T(1,128)S(1)} collective-permute-done((f32[1,128]{1,0:T(1,128)S(1)}, f32[1,128]{1,0:T(1,128)S(1)}, u32[]{:S(2)}, u32[]{:S(2)}) %collective-permute-start.6) | collective-permute-done | bytes 544 | tf_op jit(solution)/shard_map/ppermute | solution.py:20
  29.7 0.6 %collective-permute-start.7 = (f32[1,128]{1,0:T(1,128)S(1)}, f32[1,128]{1,0:T(1,128)S(1)}, u32[]{:S(2)}, u32[]{:S(2)}) collective-permute-start(f32[1,128]{1,0:T(1,128)S(1)} %add.14), channel_id=1, source_target_pairs={{0,1},{1,0},{2,3},{3,2},{4,5},{5,4},{6,7},{7,6},{8,9},{9,8},{10,11... | collective-permute-start | bytes 1544 | tf_op jit(solution)/shard_map/ppermute | solution.py:20
  30.3 0.9 %copy.9 = f32[128,1600]{0,1:T(8,128)} copy(f32[128,1600]{0,1:T(8,128)S(1)} %bitcast.6) | data formatting | bytes 1638400
  31.2 0.0 collective-permute-done.7
  31.2 0.5 %add_bitcast_fusion = f32[128]{0:T(128)} fusion(f32[1,128]{1,0:T(1,128)S(1)} %add.14, f32[1,128]{1,0:T(1,128)S(1)} %collective-permute-done.7), kind=kLoop, calls=%fused_computation.3 | loop fusion | flops 128 | bytes 1536 | tf_op jit(solution)/shard_map/reshape | solution.py:241
  (7 shorter events, 0.0 us)
Async XLA Ops:
  0.6 5.3 %collective-permute-start = (bf16[8,1200]{1,0:T(8,128)(2,1)}, bf16[8,1200]{1,0:T(8,128)(2,1)S(1)}, u32[]{:S(2)}, u32[]{:S(2)}) collective-permute-start(bf16[8,1200]{1,0:T(8,128)(2,1)} %source_ref.1), channel_id=1, source_target_pairs={{0,9},{1,8},{2,11},{3,10},{4,13},{5,12},{6,15},{7,14},{8,1},{9,0},... | collective-permute-start | bytes 57608 | tf_op jit(solution)/shard_map/ppermute | solution.py:20
  4.2 0.8 %copy-start = (bf16[8,1200]{1,0:T(8,128)(2,1)S(1)}, bf16[8,1200]{1,0:T(8,128)(2,1)}, u32[]{:S(2)}) copy-start(bf16[8,1200]{1,0:T(8,128)(2,1)} %source_ref.1) | copy-start | bytes 57604
  4.9 10.5 %copy-start.1 = (s32[8]{0:T(128)S(1)}, s32[8]{0:T(128)}, u32[]{:S(2)}) copy-start(s32[8]{0:T(128)} %cd_ref.1) | copy-start | bytes 100
  4.9 10.5 %copy-start.2 = (s32[8]{0:T(128)S(1)}, s32[8]{0:T(128)}, u32[]{:S(2)}) copy-start(s32[8]{0:T(128)} %ab_ref.1) | copy-start | bytes 100
  5.9 3.6 %collective-permute-start.1 = (bf16[16,1200]{1,0:T(8,128)(2,1)S(1)}, bf16[16,1200]{1,0:T(8,128)(2,1)S(1)}, u32[]{:S(2)}, u32[]{:S(2)}) collective-permute-start(bf16[16,1200]{1,0:T(8,128)(2,1)S(1)} %pad_maximum_fusion.2), channel_id=1, source_target_pairs={{0,5},{1,4},{2,7},{3,6},{4,1},{5,0},{6,3},{7,2},{8,13},{9,12},{10,... | collective-permute-start | bytes 115208 | tf_op jit(solution)/shard_map/ppermute | solution.py:20
  9.5 4.4 %collective-permute-start.2 = (bf16[32,1200]{1,0:T(8,128)(2,1)S(1)}, bf16[32,1200]{1,0:T(8,128)(2,1)S(1)}, u32[]{:S(2)}, u32[]{:S(2)}) collective-permute-start(bf16[32,1200]{1,0:T(8,128)(2,1)S(1)} %pad_maximum_fusion.1), channel_id=1, source_target_pairs={{0,3},{1,2},{2,1},{3,0},{4,7},{5,6},{6,5},{7,4},{8,11},{9,10},{10,... | collective-permute-start | bytes 230408 | tf_op jit(solution)/shard_map/ppermute | solution.py:20
  14.0 1.5 %collective-permute-start.3 = (bf16[64,1200]{1,0:T(8,128)(2,1)S(1)}, bf16[64,1200]{1,0:T(8,128)(2,1)S(1)}, u32[]{:S(2)}, u32[]{:S(2)}) collective-permute-start(bf16[64,1200]{1,0:T(8,128)(2,1)S(1)} %pad_maximum_fusion.first_ref), channel_id=1, source_target_pairs={{0,1},{1,0},{2,3},{3,2},{4,5},{5,4},{6,7},{7,6},{8,9},{9,8},{10,11... | collective-permute-start | bytes 460808 | tf_op jit(solution)/shard_map/ppermute | solution.py:20
  18.3 4.5 %collective-permute-start.4 = (f32[1,128]{1,0:T(1,128)S(1)}, f32[1,128]{1,0:T(1,128)S(1)}, u32[]{:S(2)}, u32[]{:S(2)}) collective-permute-start(f32[1,128]{1,0:T(1,128)S(1)} %get-tuple-element.27), channel_id=1, source_target_pairs={{0,9},{1,8},{2,11},{3,10},{4,13},{5,12},{6,15},{7,14},{8,1},{9,0},... | collective-permute-start | bytes 1544 | tf_op jit(solution)/shard_map/ppermute | solution.py:20
  22.7 4.0 %collective-permute-start.5 = (f32[1,128]{1,0:T(1,128)S(1)}, f32[1,128]{1,0:T(1,128)S(1)}, u32[]{:S(2)}, u32[]{:S(2)}) collective-permute-start(f32[1,128]{1,0:T(1,128)S(1)} %add.12), channel_id=1, source_target_pairs={{0,5},{1,4},{2,7},{3,6},{4,1},{5,0},{6,3},{7,2},{8,13},{9,12},{10,... | collective-permute-start | bytes 1544 | tf_op jit(solution)/shard_map/ppermute | solution.py:20
  26.7 3.0 %collective-permute-start.6 = (f32[1,128]{1,0:T(1,128)S(1)}, f32[1,128]{1,0:T(1,128)S(1)}, u32[]{:S(2)}, u32[]{:S(2)}) collective-permute-start(f32[1,128]{1,0:T(1,128)S(1)} %add.13), channel_id=1, source_target_pairs={{0,3},{1,2},{2,1},{3,0},{4,7},{5,6},{6,5},{7,4},{8,11},{9,10},{10,... | collective-permute-start | bytes 1544 | tf_op jit(solution)/shard_map/ppermute | solution.py:20
  29.7 1.5 %collective-permute-start.7 = (f32[1,128]{1,0:T(1,128)S(1)}, f32[1,128]{1,0:T(1,128)S(1)}, u32[]{:S(2)}, u32[]{:S(2)}) collective-permute-start(f32[1,128]{1,0:T(1,128)S(1)} %add.14), channel_id=1, source_target_pairs={{0,1},{1,0},{2,3},{3,2},{4,5},{5,4},{6,7},{7,6},{8,9},{9,8},{10,11... | collective-permute-start | bytes 1544 | tf_op jit(solution)/shard_map/ppermute | solution.py:20

commit v3 on v0

v3 whole, which is shorter than its diff:
```python
import functools
import jax
import jax.numpy as jnp
from jax import lax
from jax.experimental import pallas as pl
from jax.experimental.pallas import tpu as pltpu
from jax.sharding import PartitionSpec as P

LANES = 128
F32 = jnp.float32
I32 = jnp.int32
VMEM = pl.BlockSpec(memory_space=pltpu.VMEM)
SMEM = pl.BlockSpec(memory_space=pltpu.SMEM)
ANY = pl.BlockSpec(memory_space=pl.ANY)


def generators(count):
    bits = count.bit_length() - 1
    return [(1 << b) | 1 for b in range(bits - 1, 0, -1)] + [1]


def swap(value, key, count):
    return lax.ppermute(value, "col", [(i, i ^ key) for i in range(count)])


def near(value):
    return pltpu.with_memory_space_constraint(value, pltpu.VMEM)


def far(value):
    return pltpu.with_memory_space_constraint(value, pltpu.HBM)


def window_of(width, cd_rows):
    return min(-(-(width + LANES - 1) // LANES) * LANES, cd_rows)


def window_sizes(cd_rows, width):
    most = window_of(width, cd_rows)
    return [size for size in range(256, most, 256)] + [most]


def plan(cd_ref, ab_ref, table_ref, me, cols, tile, cd_rows, width):
    sizes = window_sizes(cd_rows, width)
    tiles = cols // tile
    irreps = cd_ref.shape[0]
    fields, extras = 3 + tiles, 3 + tiles + 4 * (irreps + 1)
    starts = [(jnp.int32(0), -me * cols)]
    for g in range(irreps):
        starts.append((starts[g][0] + cd_ref[g], starts[g][1] + ab_ref[g]))
    here = [(starts[g + 1][1] > 0) & (starts[g][1] < cols) for g in range(irreps)]
    most = jnp.int32(0)
    for g in range(irreps):
        need = lax.rem(starts[g][0], LANES) + cd_ref[g]
        most = jnp.maximum(most, jnp.where(here[g], need, 0))
    size = jnp.int32(sizes[-1])
    for choice in reversed(sizes):
        size = jnp.where(most <= choice, choice, size)
    present, extra = jnp.int32(0), jnp.int32(0)
    for g in range(irreps):
        cd_start, ab_start = starts[g]
        at = jnp.minimum(cd_start - lax.rem(cd_start, LANES), cd_rows - size)
        for j, value in enumerate((jnp.int32(g), at, cd_start - at, cd_ref[g])):
            table_ref[fields + 4 * present + j] = value
        inner = jnp.maximum(ab_start, 0)
        table_ref[extras + 2 * extra] = lax.div(inner, tile)
        table_ref[extras + 2 * extra + 1] = present
        extra = extra + jnp.where(here[g] & (lax.rem(inner, tile) > 0), 1, 0)
        present = present + jnp.where(here[g], 1, 0)
    for t in range(tiles):
        passed = jnp.int32(0)
        for g in range(irreps):
            passed = passed + jnp.where(here[g] & (starts[g + 1][1] <= t * tile), 1, 0)
        table_ref[3 + t] = passed
    table_ref[0] = size
    table_ref[1] = present
    table_ref[2] = extra


def plan_kernel(tile, cd_rows, width, cols, tau_hbm, cd_hbm, ab_hbm, own_ref, table_ref, cd_ref, ab_ref, arrived):
    copies = [
        pltpu.make_async_copy(source, target, arrived.at[i])
        for i, (source, target) in enumerate(((cd_hbm, cd_ref), (ab_hbm, ab_ref), (tau_hbm, own_ref)))
    ]
    for copy in copies:
        copy.start()
    for copy in copies:
        copy.wait()
    plan(cd_ref, ab_ref, table_ref, lax.axis_index("col"), cols, tile, cd_rows, width)


def tile_copies(tile, first, extras_at, table_ref, integrals_ref, packed_ref, extra_ref, arrived, size, act):
    fields = 3 + integrals_ref.shape[0] // tile
    count = packed_ref.shape[0] // tile

    def window(t, i):
        at = pl.multiple_of(table_ref[fields + 4 * i + 1], LANES)
        return integrals_ref.at[pl.ds(pl.multiple_of(t * tile, tile), tile), pl.ds(at, size)]

    @pl.loop(0, count)
    def _(t):
        to = packed_ref.at[pl.ds(pl.multiple_of(t * tile, tile), tile), pl.ds(0, size)]
        act(pltpu.make_async_copy(window(first + t, table_ref[3 + first + t]), to, arrived.at[t]))

    if extra_ref is not None:
        @pl.loop(0, table_ref[2])
        def _(e):
            source = window(table_ref[extras_at + 2 * e], table_ref[extras_at + 2 * e + 1])
            act(pltpu.make_async_copy(source, extra_ref.at[e, :, pl.ds(0, size)], arrived.at[count + e]))


def weight_kernel(
    tile, width, table_ref, ab_hbm, irrep_hbm, occ_hbm, virt_ref, integrals_ref,
    weight_ref, label_ref, packed_ref, ab_ref, irrep_ref, occ_ref, arrived, here,
):
    copies = [
        pltpu.make_async_copy(source, target, here.at[i])
        for i, (source, target) in enumerate(((ab_hbm, ab_ref), (irrep_hbm, irrep_ref), (occ_hbm, occ_ref)))
    ]
    for copy in copies:
        copy.start()
    cols, cd_rows = integrals_ref.shape
    pairs = weight_ref.shape[1]

    def each_copy(act):
        for size in window_sizes(cd_rows, width):
            @pl.when(table_ref[0] == size)
            def _():
                tile_copies(tile, 0, 0, table_ref, integrals_ref, packed_ref, None, arrived, size, act)

    each_copy(lambda copy: copy.start())
    for copy in copies:
        copy.wait()
    label = irrep_ref[...]
    low = jnp.zeros((1, pairs), I32)
    high = jnp.zeros((1, pairs), I32)
    start = -lax.axis_index("col") * cols
    for g in range(ab_ref.shape[0]):
        end = start + ab_ref[g]
        low = jnp.where(label == g, start, low)
        high = jnp.where(label == g, end, high)
        start = end
    occ = occ_ref[...]
    for c in range(0, cols, LANES):
        span = min(LANES, cols - c)
        virt = jnp.transpose(jnp.broadcast_to(virt_ref[:, c:c + span], (LANES, span)))
        at = c + lax.broadcasted_iota(I32, (span, LANES), 0)
        for p in range(0, pairs, LANES):
            lanes = slice(p, p + LANES)
            keep = (at >= low[:, lanes]) & (at < high[:, lanes])
            weight_ref[c:c + span, lanes] = jnp.where(keep, 1.0 / (virt - occ[:, lanes]), 0.0)
    for p in range(0, pairs, LANES):
        label_ref[p:p + LANES, :] = jnp.transpose(jnp.broadcast_to(label[:, p:p + LANES].astype(F32), (LANES, LANES)))
    each_copy(lambda copy: copy.wait())


def fetch_kernel(tile, width, table_ref, after_ref, integrals_ref, packed_ref, extra_ref, mark_ref, arrived):
    del after_ref
    cols, cd_rows = integrals_ref.shape
    first = (cols - packed_ref.shape[0]) // tile
    extras_at = 3 + cols // tile + 4 * extra_ref.shape[0]
    for size in window_sizes(cd_rows, width):
        @pl.when(table_ref[0] == size)
        def _():
            args = (tile, first, extras_at, table_ref, integrals_ref, packed_ref, extra_ref, arrived, size)
            tile_copies(*args, lambda copy: copy.start())
            tile_copies(*args, lambda copy: copy.wait())
    mark_ref[...] = jnp.zeros(mark_ref.shape, F32)


def place(count, rows, first, fields, table_ref, source_ref, label_ref, tau_ref, placed_ref):
    me = lax.axis_index("col")
    half, width = source_ref.shape
    window = tau_ref.shape[1]
    keys = generators(count)
    tau_ref[:, :width] = source_ref[...].astype(F32)
    lane = lax.broadcasted_iota(I32, (1, window), 1)
    owners = []
    for block in range(half // rows):
        mask = 0 if first else keys[-1]
        for step, key in enumerate(keys[:-1]):
            mask ^= key if (block >> step) & 1 else 0
        owners.append(me ^ mask)
    labels = jnp.concatenate(
        [label_ref[pl.ds(pl.multiple_of(owner * rows, rows), rows), :] for owner in owners], axis=0
    )[:, :1]

    def moved(i):
        place_at, size = table_ref[fields + 4 * i + 2], table_ref[fields + 4 * i + 3]
        return jnp.where((lane >= place_at) & (lane < place_at + size), pltpu.roll(tau_ref[...], place_at, 1), 0.0)

    def store(values):
        for block, owner in enumerate(owners):
            to = pl.ds(pl.multiple_of(lax.div(owner, 2) * rows, rows), rows)
            placed_ref[to, :] = values[block * rows:(block + 1) * rows]

    store(moved(0))

    @pl.loop(1, table_ref[1])
    def _(i):
        old = jnp.concatenate(
            [placed_ref[pl.ds(pl.multiple_of(lax.div(owner, 2) * rows, rows), rows), :] for owner in owners], axis=0
        )
        store(jnp.where(labels == table_ref[fields + 4 * i].astype(F32), moved(i), old))


def first_kernel(count, rows, fields, table_ref, source_ref, label_ref, after_ref, placed_ref, tau_ref):
    del after_ref
    place(count, rows, True, fields, table_ref, source_ref, label_ref, tau_ref, placed_ref)


def ladder_kernel(
    count, rows, total, tile, width, cd_rows, table_ref, second_ref, label_ref, first_ref, early_ref, packed_ref, extra_ref, weight_ref,
    update_ref, energy_ref, tau_ref, other_ref, dense_ref, parts_ref,
):
    cols, pairs = weight_ref.shape
    half, window = tau_ref.shape
    tiles = cols // tile
    fields, extras = 3 + tiles, 3 + tiles + 4 * extra_ref.shape[0]
    place(count, rows, False, fields, table_ref, second_ref, label_ref, tau_ref, other_ref)
    me = lax.axis_index("col")

    def in_order(chip):
        flips = lax.shift_right_logical(me, 1) ^ chip
        odd = me & 1
        for step in range(len(generators(count)) - 1):
            odd = odd ^ (lax.shift_right_logical(flips, step) & 1)
        here = slice(chip * rows, (chip + 1) * rows)
        own, other = first_ref[here], other_ref[here]
        return [jnp.where(odd == 1, other, own), jnp.where(odd == 1, own, other)]

    @pl.loop(0, table_ref[1])
    def _(i):
        both = jnp.concatenate([part for chip in range(half // rows) for part in in_order(chip)], axis=0)
        mine = label_ref[:, :1] == table_ref[fields + 4 * i].astype(F32)
        dense_ref[i] = jnp.where(mine, both, 0.0).astype(dense_ref.dtype)

    def integrals_of(t, size):
        early = early_ref.shape[0] // tile
        source, t = (early_ref, t) if t < early else (packed_ref, t - early)
        return source[t * tile:(t + 1) * tile, :size]

    def ladder_tile(integrals, i, here, size):
        ladder = lax.dot_general(
            integrals, dense_ref[i, :, :size], (((1,), (1,)), ((), ())), preferred_element_type=F32
        )
        update = ladder * weight_ref[here, :]
        return update, jnp.sum((ladder * update).reshape(tile // 8, 8, pairs), axis=0)

    for size in window_sizes(cd_rows, width):
        @pl.when(table_ref[0] == size)
        def _():
            for t in range(tiles):
                here = pl.ds(t * tile, tile)
                update_ref[here, :], parts_ref[t] = ladder_tile(integrals_of(t, size), table_ref[3 + t], here, size)

            @pl.loop(0, table_ref[2])
            def _(e):
                t, i = table_ref[extras + 2 * e], table_ref[extras + 2 * e + 1]
                here = pl.ds(pl.multiple_of(t * tile, tile), tile)
                update, part = ladder_tile(extra_ref[e, :, :size], i, here, size)
                update_ref[here, :] += update
                parts_ref[t] += part

    energy_ref[...] = jnp.sum(jnp.sum(parts_ref[...], axis=0), axis=0, keepdims=True) / total


def shards(tau_packed, pair_irrep, cd_sizes, ab_sizes, integrals, occ_energy, virt_energy):
    cd_rows, cols = integrals.shape
    rows, width = tau_packed.shape
    pairs = pair_irrep.shape[0]
    irreps = cd_sizes.shape[0]
    count = lax.axis_size("col")
    keys = generators(count)
    tile = 160 if cols % 160 == 0 else cols
    tiles = cols // tile
    fields = 3 + tiles
    window = window_of(width, cd_rows)
    entries = fields + 4 * (irreps + 1) + 2 * (irreps + 1)

    early = (tiles * 6 // 10) * tile
    virt_row = virt_energy.reshape(1, cols)
    turned = far(integrals.T)
    held, table = pl.pallas_call(
        functools.partial(plan_kernel, tile, cd_rows, width, cols),
        out_shape=(pltpu.VMEM(tau_packed.shape, tau_packed.dtype), pltpu.SMEM((entries,), I32)),
        in_specs=[ANY] * 3,
        out_specs=(VMEM, SMEM),
        scratch_shapes=[
            pltpu.SMEM(cd_sizes.shape, I32), pltpu.SMEM(ab_sizes.shape, I32), pltpu.SemaphoreType.DMA((3,)),
        ],
        compiler_params=pltpu.CompilerParams(vmem_limit_bytes=1 << 20),
        cost_estimate=pl.CostEstimate(flops=0, bytes_accessed=1 << 20, transcendentals=0),
    )(far(tau_packed), far(cd_sizes), far(ab_sizes))
    table = pltpu.with_memory_space_constraint(table, pltpu.SMEM)
    sent = tau_packed
    for step, key in enumerate(keys[:-1]):
        held = jnp.concatenate([held, swap(sent, key, count)], axis=0)
        if step == 0:
            held, virt_row, occ_energy = lax.optimization_barrier((held, virt_row, occ_energy))
            weight, label, packed_early = pl.pallas_call(
                functools.partial(weight_kernel, tile, width),
                out_shape=(
                    pltpu.VMEM((cols, pairs), F32),
                    pltpu.VMEM((pairs, LANES), F32),
                    pltpu.VMEM((early, window), integrals.dtype),
                ),
                in_specs=[SMEM] + [ANY] * 3 + [VMEM, ANY],
                out_specs=(VMEM, VMEM, VMEM),
                scratch_shapes=[
                    pltpu.SMEM(ab_sizes.shape, I32),
                    pltpu.VMEM((1, pairs), I32),
                    pltpu.VMEM((1, pairs), F32),
                    pltpu.SemaphoreType.DMA((tiles,)),
                    pltpu.SemaphoreType.DMA((3,)),
                ],
                compiler_params=pltpu.CompilerParams(vmem_limit_bytes=2 << 20),
                cost_estimate=pl.CostEstimate(flops=10 * cols * pairs, bytes_accessed=4 * cols * pairs, transcendentals=0),
            )(
                table, far(ab_sizes), far(pair_irrep.reshape(1, pairs)), far(occ_energy.reshape(1, pairs)),
                near(virt_row), turned,
            )
        elif step == 1:
            held, label = lax.optimization_barrier((held, label))
            packed, extra, mark = pl.pallas_call(
                functools.partial(fetch_kernel, tile, width),
                out_shape=(
                    pltpu.VMEM((cols - early, window), integrals.dtype),
                    pltpu.VMEM((irreps + 1, tile, window), integrals.dtype),
                    pltpu.VMEM((8, LANES), F32),
                ),
                in_specs=[SMEM, ANY, ANY],
                out_specs=(VMEM, VMEM, VMEM),
                scratch_shapes=[pltpu.SemaphoreType.DMA((tiles + irreps + 1,))],
                compiler_params=pltpu.CompilerParams(vmem_limit_bytes=1 << 20),
                cost_estimate=pl.CostEstimate(flops=0, bytes_accessed=2 * cols * width, transcendentals=0),
            )(table, near(label), turned)
        elif step == 2:
            held, mark = lax.optimization_barrier((held, mark))
        else:
            held = lax.optimization_barrier(held)
        sent = held
    second = swap(held, keys[-1], count)
    first = pl.pallas_call(
        functools.partial(first_kernel, count, rows, fields),
        out_shape=pltpu.VMEM((pairs // 2, window), F32),
        in_specs=[SMEM, VMEM, VMEM, ANY],
        out_specs=VMEM,
        scratch_shapes=[pltpu.VMEM((pairs // 2, window), F32)],
        compiler_params=pltpu.CompilerParams(vmem_limit_bytes=(1 << 20) + 16 * pairs * window),
        cost_estimate=pl.CostEstimate(flops=10 * pairs * window, bytes_accessed=4 * pairs * window, transcendentals=0),
    )(table, near(held), near(label), near(mark))
    update, energy = pl.pallas_call(
        functools.partial(ladder_kernel, count, rows, cols * count, tile, width, cd_rows),
        out_shape=(pltpu.VMEM((cols, pairs), F32), pltpu.VMEM((1, pairs), F32)),
        in_specs=[SMEM] + [VMEM] * 7,
        out_specs=(VMEM, VMEM),
        scratch_shapes=[
            pltpu.VMEM((pairs // 2, window), F32),
            pltpu.VMEM((pairs // 2, window), F32),
            pltpu.VMEM((irreps, pairs, window), jnp.bfloat16),
            pltpu.VMEM((tiles, 8, pairs), F32),
        ],
        compiler_params=pltpu.CompilerParams(vmem_limit_bytes=(4 << 20) + 32 * pairs * window),
        cost_estimate=pl.CostEstimate(
            flops=2 * cols * width * pairs, bytes_accessed=2 * cols * width + 4 * cols * pairs, transcendentals=0
        ),
    )(table, near(second), near(label), near(first), near(packed_early), near(packed), near(extra), near(weight))
    for key in keys:
        energy = energy + swap(energy, key, count)
    return update.T, energy.reshape(pairs)


def solution(mesh):
    placed = (
        P(("job", "col"), None),
        P("job"),
        P("job"),
        P("job"),
        P("job", "col"),
        P("job"),
        P(("job", "col")),
    )
    return jax.shard_map(
        shards, mesh=mesh, in_specs=placed, out_specs=(P("job", "col"), P("job")), check_vma=False
    )
```

time: 92 us -> 30 us (0.33)
  blocking collectives: 55.9 us -> 0 us
  starting transfers between devices: 0 us -> 15.3 us
  other arithmetic: 14.7 us -> 0.56 us
  between operations: 10.8 us -> 0.68 us
  matrix products: 7.76 us -> 0 us
  waiting for transfers between devices: 0 us -> 6.4 us
  Pallas kernels: 0 us -> 5.01 us
    psum x1 -> x0, blocking collectives: 30.3 us -> none  [shards(): pair_energy = lax.psum(partial_energy, 'col')]
    all_gather x1 -> x0, blocking collectives: 25.6 us -> none  [shards(): lax.all_gather(spread, 'col', axis=0, tiled=True)]
    ppermute x0 -> x8, starting transfers between devices: none -> 15.3 us  [swap(): return lax.ppermute(value, 'col', [(i, i ^ key) for i in range(count)])]
    and x4 -> x0, other arithmetic: 10.1 us -> none  [expand(): valid = (offset >= 0) & (offset < cd_sizes[label])]
    dot_general x1 -> x0, matrix products: 7.76 us -> none  [shards(): jnp.dot(lax.all_gather(spread, 'col', axis=0, tiled=True), integrals, pre...]
    ppermute x0 -> x8, waiting for transfers between devices: none -> 6.4 us  [swap(): return lax.ppermute(value, 'col', [(i, i ^ key) for i in range(count)])]
    pallas_call x0 -> x5, Pallas kernels: none -> 5.01 us  [the longest x1 1.43 us: shards(): pl.pallas_call(functools.partial(weight_kernel, tile, width), out_shape=(...]
    slice x2 -> x0, local copies, waits for them, and re-layouts: 2.32 us -> none  [the longest x1 1.64 us: expand(): valid = (offset >= 0) & (offset < cd_sizes[label])]
  transfers between devices with their start and end apart: 0 -> 8, of which waited for: 0 -> 7; matrix products, arithmetic and copies ran while one was open for 0% -> 5% of each run, Pallas kernels for 0% -> 13%
where the time goes in v3:
time: 30 us; the launch traced here: 29.6 us
  starting transfers between devices  15.3 us (51%)
  waiting for transfers between devices  6.4 us (21%)
  Pallas kernels  5.01 us (17%)
  local copies, waits for them, and re-layouts  1.59 us (5%)
  between operations  0.68 us (2%)
  other arithmetic  0.56 us (2%)
    ppermute x8, starting transfers between devices, swap(): return lax.ppermute(value, 'col', [(i, i ^ key) for i in range(count)])  15.3 us
    ppermute x8, waiting for transfers between devices, swap(): return lax.ppermute(value, 'col', [(i, i ^ key) for i in range(count)])  6.4 us
    pallas_call x1, Pallas kernels, shards(): pl.pallas_call(functools.partial(weight_kernel, tile, width), out_shape=(...  1.43 us
    pallas_call x1, Pallas kernels, shards(): pl.pallas_call(functools.partial(fetch_kernel, tile, width), out_shape=(p...  1.32 us
    pallas_call x1, Pallas kernels, shards(): pl.pallas_call(functools.partial(ladder_kernel, count, rows, cols * count...  1.05 us
    pallas_call x1, Pallas kernels, shards(): pl.pallas_call(functools.partial(plan_kernel, tile, cd_rows, width, cols)...  0.96 us
    unnamed x1, local copies, waits for them, and re-layouts  0.89 us
    reshape x1, local copies, waits for them, and re-layouts, shards(): virt_row = virt_energy.reshape(1, cols)  0.7 us
  transfers between devices with their start and end apart: 8, of which 7 were waited for; matrix products, arithmetic and copies ran while one was open for 5% of the time, Pallas kernels for 13%

profile of v3, /device:TPU:0, one launch (start us, length us, event | category | flops | bytes accessed | tf_op | source)
XLA Modules:
  0.0 29.6 jit_solution(459543934901079619)
XLA Ops:
  0.6 3.5 %collective-permute-start = (bf16[8,1200]{1,0:T(8,128)(2,1)}, bf16[8,1200]{1,0:T(8,128)(2,1)S(1)}, u32[]{:S(2)}, u32[]{:S(2)}) collective-permute-start(bf16[8,1200]{1,0:T(8,128)(2,1)} %tau_hbm.1), channel_id=1, source_target_pairs={{0,9},{1,8},{2,11},{3,10},{4,13},{5,12},{6,15},{7,14},{8,1},{9,0},... | collective-permute-start | bytes 57608 | tf_op jit(solution)/shard_map/ppermute | solution.py:23
  4.2 0.7 %reshape.16.virt_ref = f32[1,1600]{1,0:T(1,128)S(1)} reshape(f32[1600]{0:T(1024)} %param.13) | data formatting | bytes 12800 | tf_op jit(solution)/shard_map/reshape | solution.py:282
  4.9 1.0 %shard_map.86 = (bf16[8,1200]{1,0:T(8,128)(2,1)S(1)}, s32[67]{0:T(128)S(4)}) custom-call(bf16[8,1200]{1,0:T(8,128)(2,1)} %tau_hbm.1, s32[8]{0:T(128)} %cd_hbm.1, s32[8]{0:T(128)} %ab_hbm.3), custom_call_target="tpu_custom_call" | custom-call | bytes 1048576 | tf_op jit(solution)/shard_map/pallas_call | solution.py:284
  5.8 0.1 collective-permute-done
  5.9 1.9 %collective-permute-start.1 = (bf16[16,1200]{1,0:T(8,128)(2,1)S(1)}, bf16[16,1200]{1,0:T(8,128)(2,1)S(1)}, u32[]{:S(2)}, u32[]{:S(2)}) collective-permute-start(bf16[16,1200]{1,0:T(8,128)(2,1)S(1)} %pad_maximum_fusion.2), channel_id=1, source_target_pairs={{0,5},{1,4},{2,7},{3,6},{4,1},{5,0},{6,3},{7,2},{8,13},{9,12},{10,... | collective-permute-start | bytes 115208 | tf_op jit(solution)/shard_map/ppermute | solution.py:23
  7.8 1.4 %shard_map.87 = (f32[1600,128]{1,0:T(8,128)S(1)}, f32[128,128]{1,0:T(8,128)S(1)}, bf16[960,1408]{1,0:T(8,128)(2,1)S(1)}) custom-call(s32[67]{0:T(128)S(4)} %get-tuple-element.19.table_ref, s32[8]{0:T(128)} %ab_hbm.3, s32[1,128]{1,0:T(1,128)} %bitcast.9, f32[1,128]{1,0:T(1,128)} %bitcast.10, f32[1,1600]{1,0:T(1,128)S(1)} %reshape.16.virt_ref, ...), custom_call_target="tpu_custom_call" | custom-call | flops 2048000 | bytes 819200 | tf_op jit(solution)/shard_map/pallas_call | solution.py:301
  9.3 0.2 collective-permute-done.1
  9.5 1.9 %collective-permute-start.2 = (bf16[32,1200]{1,0:T(8,128)(2,1)S(1)}, bf16[32,1200]{1,0:T(8,128)(2,1)S(1)}, u32[]{:S(2)}, u32[]{:S(2)}) collective-permute-start(bf16[32,1200]{1,0:T(8,128)(2,1)S(1)} %pad_maximum_fusion.1), channel_id=1, source_target_pairs={{0,3},{1,2},{2,1},{3,0},{4,7},{5,6},{6,5},{7,4},{8,11},{9,10},{10,... | collective-permute-start | bytes 230408 | tf_op jit(solution)/shard_map/ppermute | solution.py:23
  11.4 1.3 %shard_map.88 = (bf16[640,1408]{1,0:T(8,128)(2,1)S(1)}, bf16[9,160,1408]{2,1,0:T(8,128)(2,1)S(1)}, f32[8,128]{1,0:T(8,128)S(1)}) custom-call(s32[67]{0:T(128)S(4)} %get-tuple-element.19.table_ref, f32[128,128]{1,0:T(8,128)S(1)} %get-tuple-element.26.after_ref.label_ref, bf16[1600,3200]{1,0:T(8,128)(2,1)} %bitcast.8), custom_call_target="tpu_custom_call" | custom-call | bytes 3840000 | tf_op jit(solution)/shard_map/pallas_call | solution.py:325
  12.7 1.2 %collective-permute-done.2 = bf16[32,1200]{1,0:T(8,128)(2,1)S(1)} collective-permute-done((bf16[32,1200]{1,0:T(8,128)(2,1)S(1)}, bf16[32,1200]{1,0:T(8,128)(2,1)S(1)}, u32[]{:S(2)}, u32[]{:S(2)}) %collective-permute-start.2) | collective-permute-done | bytes 76832 | tf_op jit(solution)/shard_map/ppermute | solution.py:23
  14.0 0.3 %collective-permute-start.3 = (bf16[64,1200]{1,0:T(8,128)(2,1)S(1)}, bf16[64,1200]{1,0:T(8,128)(2,1)S(1)}, u32[]{:S(2)}, u32[]{:S(2)}) collective-permute-start(bf16[64,1200]{1,0:T(8,128)(2,1)S(1)} %pad_maximum_fusion.source_ref), channel_id=1, source_target_pairs={{0,1},{1,0},{2,3},{3,2},{4,5},{5,4},{6,7},{7,6},{8,9},{9,8},{10,11... | collective-permute-start | bytes 460808 | tf_op jit(solution)/shard_map/ppermute | solution.py:23
  14.3 0.2 shard_map.89.first_ref
  14.6 0.9 %collective-permute-done.3.second_ref = bf16[64,1200]{1,0:T(8,128)(2,1)S(1)} collective-permute-done((bf16[64,1200]{1,0:T(8,128)(2,1)S(1)}, bf16[64,1200]{1,0:T(8,128)(2,1)S(1)}, u32[]{:S(2)}, u32[]{:S(2)}) %collective-permute-start.3) | collective-permute-done | bytes 153632 | tf_op jit(solution)/shard_map/ppermute | solution.py:23
  15.4 1.1 %shard_map.90 = (f32[1600,128]{1,0:T(8,128)S(1)}, f32[1,128]{1,0:T(1,128)S(1)}) custom-call(s32[67]{0:T(128)S(4)} %get-tuple-element.19.table_ref, bf16[64,1200]{1,0:T(8,128)(2,1)S(1)} %collective-permute-done.3.second_ref, f32[128,128]{1,0:T(8,128)S(1)} %get-tuple-element.26.after_ref.label_ref, f32[64,1408]{1,0:T(8,128)S(1)} %shard_map.89.first_ref, ...), custom_call_target="tpu_custom_call" | custom-call | flops 491520000 | bytes 4659200 | tf_op jit(solution)/shard_map/pallas_call | solution.py:353
  16.5 3.6 %collective-permute-start.4 = (f32[1,128]{1,0:T(1,128)S(1)}, f32[1,128]{1,0:T(1,128)S(1)}, u32[]{:S(2)}, u32[]{:S(2)}) collective-permute-start(f32[1,128]{1,0:T(1,128)S(1)} %get-tuple-element.35), channel_id=1, source_target_pairs={{0,9},{1,8},{2,11},{3,10},{4,13},{5,12},{6,15},{7,14},{8,1},{9,0},... | collective-permute-start | bytes 1544 | tf_op jit(solution)/shard_map/ppermute | solution.py:23
  20.1 1.3 %collective-permute-done.4 = f32[1,128]{1,0:T(1,128)S(1)} collective-permute-done((f32[1,128]{1,0:T(1,128)S(1)}, f32[1,128]{1,0:T(1,128)S(1)}, u32[]{:S(2)}, u32[]{:S(2)}) %collective-permute-start.4) | collective-permute-done | bytes 544 | tf_op jit(solution)/shard_map/ppermute | solution.py:23
  21.4 1.5 %collective-permute-start.5 = (f32[1,128]{1,0:T(1,128)S(1)}, f32[1,128]{1,0:T(1,128)S(1)}, u32[]{:S(2)}, u32[]{:S(2)}) collective-permute-start(f32[1,128]{1,0:T(1,128)S(1)} %add.12), channel_id=1, source_target_pairs={{0,5},{1,4},{2,7},{3,6},{4,1},{5,0},{6,3},{7,2},{8,13},{9,12},{10,... | collective-permute-start | bytes 1544 | tf_op jit(solution)/shard_map/ppermute | solution.py:23
  22.9 1.4 %collective-permute-done.5 = f32[1,128]{1,0:T(1,128)S(1)} collective-permute-done((f32[1,128]{1,0:T(1,128)S(1)}, f32[1,128]{1,0:T(1,128)S(1)}, u32[]{:S(2)}, u32[]{:S(2)}) %collective-permute-start.5) | collective-permute-done | bytes 544 | tf_op jit(solution)/shard_map/ppermute | solution.py:23
  24.3 2.2 %collective-permute-start.6 = (f32[1,128]{1,0:T(1,128)S(1)}, f32[1,128]{1,0:T(1,128)S(1)}, u32[]{:S(2)}, u32[]{:S(2)}) collective-permute-start(f32[1,128]{1,0:T(1,128)S(1)} %add.13), channel_id=1, source_target_pairs={{0,3},{1,2},{2,1},{3,0},{4,7},{5,6},{6,5},{7,4},{8,11},{9,10},{10,... | collective-permute-start | bytes 1544 | tf_op jit(solution)/shard_map/ppermute | solution.py:23
  26.5 1.3 %collective-permute-done.6 = f32[1,128]{1,0:T(1,128)S(1)} collective-permute-done((f32[1,128]{1,0:T(1,128)S(1)}, f32[1,128]{1,0:T(1,128)S(1)}, u32[]{:S(2)}, u32[]{:S(2)}) %collective-permute-start.6) | collective-permute-done | bytes 544 | tf_op jit(solution)/shard_map/ppermute | solution.py:23
  27.8 0.3 %collective-permute-start.7 = (f32[1,128]{1,0:T(1,128)S(1)}, f32[1,128]{1,0:T(1,128)S(1)}, u32[]{:S(2)}, u32[]{:S(2)}) collective-permute-start(f32[1,128]{1,0:T(1,128)S(1)} %add.14), channel_id=1, source_target_pairs={{0,1},{1,0},{2,3},{3,2},{4,5},{5,4},{6,7},{7,6},{8,9},{9,8},{10,11... | collective-permute-start | bytes 1544 | tf_op jit(solution)/shard_map/ppermute | solution.py:23
  28.2 0.9 %copy.9 = f32[128,1600]{0,1:T(8,128)} copy(f32[128,1600]{0,1:T(8,128)S(1)} %bitcast.6) | data formatting | bytes 1638400
  29.1 0.0 collective-permute-done.7
  29.1 0.5 %add_bitcast_fusion = f32[128]{0:T(128)} fusion(f32[1,128]{1,0:T(1,128)S(1)} %add.14, f32[1,128]{1,0:T(1,128)S(1)} %collective-permute-done.7), kind=kLoop, calls=%fused_computation.3 | loop fusion | flops 128 | bytes 1536 | tf_op jit(solution)/shard_map/reshape | solution.py:371
  (6 shorter events, 0.0 us)
Async XLA Ops:
  0.6 5.3 %collective-permute-start = (bf16[8,1200]{1,0:T(8,128)(2,1)}, bf16[8,1200]{1,0:T(8,128)(2,1)S(1)}, u32[]{:S(2)}, u32[]{:S(2)}) collective-permute-start(bf16[8,1200]{1,0:T(8,128)(2,1)} %tau_hbm.1), channel_id=1, source_target_pairs={{0,9},{1,8},{2,11},{3,10},{4,13},{5,12},{6,15},{7,14},{8,1},{9,0},... | collective-permute-start | bytes 57608 | tf_op jit(solution)/shard_map/ppermute | solution.py:23
  5.9 3.6 %collective-permute-start.1 = (bf16[16,1200]{1,0:T(8,128)(2,1)S(1)}, bf16[16,1200]{1,0:T(8,128)(2,1)S(1)}, u32[]{:S(2)}, u32[]{:S(2)}) collective-permute-start(bf16[16,1200]{1,0:T(8,128)(2,1)S(1)} %pad_maximum_fusion.2), channel_id=1, source_target_pairs={{0,5},{1,4},{2,7},{3,6},{4,1},{5,0},{6,3},{7,2},{8,13},{9,12},{10,... | collective-permute-start | bytes 115208 | tf_op jit(solution)/shard_map/ppermute | solution.py:23
  9.5 4.4 %collective-permute-start.2 = (bf16[32,1200]{1,0:T(8,128)(2,1)S(1)}, bf16[32,1200]{1,0:T(8,128)(2,1)S(1)}, u32[]{:S(2)}, u32[]{:S(2)}) collective-permute-start(bf16[32,1200]{1,0:T(8,128)(2,1)S(1)} %pad_maximum_fusion.1), channel_id=1, source_target_pairs={{0,3},{1,2},{2,1},{3,0},{4,7},{5,6},{6,5},{7,4},{8,11},{9,10},{10,... | collective-permute-start | bytes 230408 | tf_op jit(solution)/shard_map/ppermute | solution.py:23
  14.0 1.5 %collective-permute-start.3 = (bf16[64,1200]{1,0:T(8,128)(2,1)S(1)}, bf16[64,1200]{1,0:T(8,128)(2,1)S(1)}, u32[]{:S(2)}, u32[]{:S(2)}) collective-permute-start(bf16[64,1200]{1,0:T(8,128)(2,1)S(1)} %pad_maximum_fusion.source_ref), channel_id=1, source_target_pairs={{0,1},{1,0},{2,3},{3,2},{4,5},{5,4},{6,7},{7,6},{8,9},{9,8},{10,11... | collective-permute-start | bytes 460808 | tf_op jit(solution)/shard_map/ppermute | solution.py:23
  16.5 4.9 %collective-permute-start.4 = (f32[1,128]{1,0:T(1,128)S(1)}, f32[1,128]{1,0:T(1,128)S(1)}, u32[]{:S(2)}, u32[]{:S(2)}) collective-permute-start(f32[1,128]{1,0:T(1,128)S(1)} %get-tuple-element.35), channel_id=1, source_target_pairs={{0,9},{1,8},{2,11},{3,10},{4,13},{5,12},{6,15},{7,14},{8,1},{9,0},... | collective-permute-start | bytes 1544 | tf_op jit(solution)/shard_map/ppermute | solution.py:23
  21.4 3.0 %collective-permute-start.5 = (f32[1,128]{1,0:T(1,128)S(1)}, f32[1,128]{1,0:T(1,128)S(1)}, u32[]{:S(2)}, u32[]{:S(2)}) collective-permute-start(f32[1,128]{1,0:T(1,128)S(1)} %add.12), channel_id=1, source_target_pairs={{0,5},{1,4},{2,7},{3,6},{4,1},{5,0},{6,3},{7,2},{8,13},{9,12},{10,... | collective-permute-start | bytes 1544 | tf_op jit(solution)/shard_map/ppermute | solution.py:23
  24.3 3.5 %collective-permute-start.6 = (f32[1,128]{1,0:T(1,128)S(1)}, f32[1,128]{1,0:T(1,128)S(1)}, u32[]{:S(2)}, u32[]{:S(2)}) collective-permute-start(f32[1,128]{1,0:T(1,128)S(1)} %add.13), channel_id=1, source_target_pairs={{0,3},{1,2},{2,1},{3,0},{4,7},{5,6},{6,5},{7,4},{8,11},{9,10},{10,... | collective-permute-start | bytes 1544 | tf_op jit(solution)/shard_map/ppermute | solution.py:23
  27.8 1.2 %collective-permute-start.7 = (f32[1,128]{1,0:T(1,128)S(1)}, f32[1,128]{1,0:T(1,128)S(1)}, u32[]{:S(2)}, u32[]{:S(2)}) collective-permute-start(f32[1,128]{1,0:T(1,128)S(1)} %add.14), channel_id=1, source_target_pairs={{0,1},{1,0},{2,3},{3,2},{4,5},{5,4},{6,7},{7,6},{8,9},{9,8},{10,11... | collective-permute-start | bytes 1544 | tf_op jit(solution)/shard_map/ppermute | solution.py:23

commit v4 on v3

--- a/solution.py
+++ b/solution.py
@@ -40,11 +40,15 @@
     return [size for size in range(256, most, 256)] + [most]
 
 
+def fields_of(tiles, irreps):
+    return 3 + 2 * tiles, 3 + 2 * tiles + 4 * (irreps + 1)
+
+
 def plan(cd_ref, ab_ref, table_ref, me, cols, tile, cd_rows, width):
     sizes = window_sizes(cd_rows, width)
     tiles = cols // tile
     irreps = cd_ref.shape[0]
-    fields, extras = 3 + tiles, 3 + tiles + 4 * (irreps + 1)
+    fields, extras = fields_of(tiles, irreps)
     starts = [(jnp.int32(0), -me * cols)]
     for g in range(irreps):
         starts.append((starts[g][0] + cd_ref[g], starts[g][1] + ab_ref[g]))
@@ -63,15 +67,22 @@
         for j, value in enumerate((jnp.int32(g), at, cd_start - at, cd_ref[g])):
             table_ref[fields + 4 * present + j] = value
         inner = jnp.maximum(ab_start, 0)
-        table_ref[extras + 2 * extra] = lax.div(inner, tile)
-        table_ref[extras + 2 * extra + 1] = present
+        t = lax.div(inner, tile)
+        for j, value in enumerate((t, present, inner - t * tile, starts[g + 1][1] - t * tile)):
+            table_ref[extras + 4 * extra + j] = value
         extra = extra + jnp.where(here[g] & (lax.rem(inner, tile) > 0), 1, 0)
         present = present + jnp.where(here[g], 1, 0)
     for t in range(tiles):
         passed = jnp.int32(0)
         for g in range(irreps):
             passed = passed + jnp.where(here[g] & (starts[g + 1][1] <= t * tile), 1, 0)
-        table_ref[3 + t] = passed
+        end = jnp.int32(tile)
+        for g in reversed(range(irreps)):
+            end = jnp.where(starts[g + 1][1] > t * tile, starts[g + 1][1] - t * tile, end)
+        table_ref[3 + 2 * t] = passed
+        table_ref[4 + 2 * t] = end
+    for j in range(4):
+        table_ref[extras + 4 * extra + j] = jnp.int32(0)
     table_ref[0] = size
     table_ref[1] = present
     table_ref[2] = extra
@@ -90,7 +101,7 @@
 
 
 def tile_copies(tile, first, extras_at, table_ref, integrals_ref, packed_ref, extra_ref, arrived, size, act):
-    fields = 3 + integrals_ref.shape[0] // tile
+    fields, _ = fields_of(integrals_ref.shape[0] // tile, 0)
     count = packed_ref.shape[0] // tile
 
     def window(t, i):
@@ -100,12 +111,12 @@
     @pl.loop(0, count)
     def _(t):
         to = packed_ref.at[pl.ds(pl.multiple_of(t * tile, tile), tile), pl.ds(0, size)]
-        act(pltpu.make_async_copy(window(first + t, table_ref[3 + first + t]), to, arrived.at[t]))
+        act(pltpu.make_async_copy(window(first + t, table_ref[3 + 2 * (first + t)]), to, arrived.at[t]))
 
     if extra_ref is not None:
         @pl.loop(0, table_ref[2])
         def _(e):
-            source = window(table_ref[extras_at + 2 * e], table_ref[extras_at + 2 * e + 1])
+            source = window(table_ref[extras_at + 4 * e], table_ref[extras_at + 4 * e + 1])
             act(pltpu.make_async_copy(source, extra_ref.at[e, :, pl.ds(0, size)], arrived.at[count + e]))
 
 
@@ -158,7 +169,7 @@
     del after_ref
     cols, cd_rows = integrals_ref.shape
     first = (cols - packed_ref.shape[0]) // tile
-    extras_at = 3 + cols // tile + 4 * extra_ref.shape[0]
+    _, extras_at = fields_of(cols // tile, extra_ref.shape[0] - 1)
     for size in window_sizes(cd_rows, width):
         @pl.when(table_ref[0] == size)
         def _():
@@ -216,7 +227,7 @@
     cols, pairs = weight_ref.shape
     half, window = tau_ref.shape
     tiles = cols // tile
-    fields, extras = 3 + tiles, 3 + tiles + 4 * extra_ref.shape[0]
+    fields, extras = fields_of(tiles, extra_ref.shape[0] - 1)
     place(count, rows, False, fields, table_ref, second_ref, label_ref, tau_ref, other_ref)
     me = lax.axis_index("col")
 
@@ -229,38 +240,46 @@
         own, other = first_ref[here], other_ref[here]
         return [jnp.where(odd == 1, other, own), jnp.where(odd == 1, own, other)]
 
-    @pl.loop(0, table_ref[1])
-    def _(i):
-        both = jnp.concatenate([part for chip in range(half // rows) for part in in_order(chip)], axis=0)
-        mine = label_ref[:, :1] == table_ref[fields + 4 * i].astype(F32)
-        dense_ref[i] = jnp.where(mine, both, 0.0).astype(dense_ref.dtype)
+    both = jnp.concatenate([part for chip in range(half // rows) for part in in_order(chip)], axis=0)
+    dense_ref[...] = both.astype(dense_ref.dtype)
 
     def integrals_of(t, size):
         early = early_ref.shape[0] // tile
         source, t = (early_ref, t) if t < early else (packed_ref, t - early)
         return source[t * tile:(t + 1) * tile, :size]
 
-    def ladder_tile(integrals, i, here, size):
+    row = lax.broadcasted_iota(I32, (tile, LANES), 0)
+    row = jnp.concatenate([row] * (pairs // LANES), axis=1)
+
+    def ladder_tile(integrals, begin, end, here, size):
         ladder = lax.dot_general(
-            integrals, dense_ref[i, :, :size], (((1,), (1,)), ((), ())), preferred_element_type=F32
+            integrals, dense_ref[:, :size], (((1,), (1,)), ((), ())), preferred_element_type=F32
         )
+        ladder = jnp.where((row >= begin) & (row < end) if begin is not None else row < end, ladder, 0.0)
         update = ladder * weight_ref[here, :]
         return update, jnp.sum((ladder * update).reshape(tile // 8, 8, pairs), axis=0)
 
+    def extra_job(e, size):
+        t, begin, end = (table_ref[extras + 4 * e + j] for j in (0, 2, 3))
+        here = pl.ds(pl.multiple_of(t * tile, tile), tile)
+        update, part = ladder_tile(extra_ref[e, :, :size], begin, end, here, size)
+        update_ref[here, :] += update
+        parts_ref[tiles + e] = part
+
+    parts_ref[tiles + 1:] = jnp.zeros((parts_ref.shape[0] - tiles - 1,) + parts_ref.shape[1:], F32)
     for size in window_sizes(cd_rows, width):
         @pl.when(table_ref[0] == size)
         def _():
             for t in range(tiles):
                 here = pl.ds(t * tile, tile)
-                update_ref[here, :], parts_ref[t] = ladder_tile(integrals_of(t, size), table_ref[3 + t], here, size)
-
-            @pl.loop(0, table_ref[2])
+                update_ref[here, :], parts_ref[t] = ladder_tile(
+                    integrals_of(t, size), None, table_ref[4 + 2 * t], here, size
+                )
+            extra_job(0, size)
+
+            @pl.loop(1, table_ref[2])
             def _(e):
-                t, i = table_ref[extras + 2 * e], table_ref[extras + 2 * e + 1]
-                here = pl.ds(pl.multiple_of(t * tile, tile), tile)
-                update, part = ladder_tile(extra_ref[e, :, :size], i, here, size)
-                update_ref[here, :] += update
-                parts_ref[t] += part
+                extra_job(e, size)
 
     energy_ref[...] = jnp.sum(jnp.sum(parts_ref[...], axis=0), axis=0, keepdims=True) / total
 
@@ -274,9 +293,9 @@
     keys = generators(count)
     tile = 160 if cols % 160 == 0 else cols
     tiles = cols // tile
-    fields = 3 + tiles
+    fields, extras = fields_of(tiles, irreps)
     window = window_of(width, cd_rows)
-    entries = fields + 4 * (irreps + 1) + 2 * (irreps + 1)
+    entries = extras + 4 * (irreps + 1)
 
     early = (tiles * 6 // 10) * tile
     virt_row = virt_energy.reshape(1, cols)
@@ -358,8 +377,8 @@
         scratch_shapes=[
             pltpu.VMEM((pairs // 2, window), F32),
             pltpu.VMEM((pairs // 2, window), F32),
-            pltpu.VMEM((irreps, pairs, window), jnp.bfloat16),
-            pltpu.VMEM((tiles, 8, pairs), F32),
+            pltpu.VMEM((pairs, window), jnp.bfloat16),
+            pltpu.VMEM((tiles + irreps + 1, 8, pairs), F32),
         ],
         compiler_params=pltpu.CompilerParams(vmem_limit_bytes=(4 << 20) + 32 * pairs * window),
         cost_estimate=pl.CostEstimate(

time: 30 us -> 30.1 us (level)
  waiting for transfers between devices: 6.4 us -> 7.31 us
  starting transfers between devices: 15.3 us -> 14.5 us
    ppermute x8, waiting for transfers between devices: 6.4 us -> 7.31 us  [swap(): return lax.ppermute(value, 'col', [(i, i ^ key) for i in range(count)])]
    ppermute x8, starting transfers between devices: 15.3 us -> 14.5 us  [swap(): return lax.ppermute(value, 'col', [(i, i ^ key) for i in range(count)])]
  transfers between devices with their start and end apart: 8 -> 8, of which waited for: 7 -> 7; matrix products, arithmetic and copies ran while one was open for 5% -> 5% of each run, Pallas kernels for 13% -> 14%
where the time goes in v4:
time: 30.1 us; the launch traced here: 29.8 us
  starting transfers between devices  14.5 us (48%)
  waiting for transfers between devices  7.31 us (24%)
  Pallas kernels  5.09 us (17%)
  local copies, waits for them, and re-layouts  1.59 us (5%)
  between operations  0.69 us (2%)
  other arithmetic  0.56 us (2%)
    ppermute x8, starting transfers between devices, swap(): return lax.ppermute(value, 'col', [(i, i ^ key) for i in range(count)])  14.5 us
    ppermute x8, waiting for transfers between devices, swap(): return lax.ppermute(value, 'col', [(i, i ^ key) for i in range(count)])  7.31 us
    pallas_call x1, Pallas kernels, shards(): pl.pallas_call(functools.partial(weight_kernel, tile, width), out_shape=(...  1.43 us
    pallas_call x1, Pallas kernels, shards(): pl.pallas_call(functools.partial(fetch_kernel, tile, width), out_shape=(p...  1.32 us
    pallas_call x1, Pallas kernels, shards(): pl.pallas_call(functools.partial(plan_kernel, tile, cd_rows, width, cols)...  1.05 us
    pallas_call x1, Pallas kernels, shards(): pl.pallas_call(functools.partial(ladder_kernel, count, rows, cols * count...  1.04 us
    unnamed x1, local copies, waits for them, and re-layouts  0.89 us
    reshape x1, local copies, waits for them, and re-layouts, shards(): virt_row = virt_energy.reshape(1, cols)  0.7 us
  transfers between devices with their start and end apart: 8, of which 7 were waited for; matrix products, arithmetic and copies ran while one was open for 5% of the time, Pallas kernels for 14%

profile of v4, /device:TPU:0, one launch (start us, length us, event | category | flops | bytes accessed | tf_op | source)
XLA Modules:
  0.0 29.8 jit_solution(1738739908287140305)
XLA Ops:
  0.6 3.5 %collective-permute-start = (bf16[8,1200]{1,0:T(8,128)(2,1)}, bf16[8,1200]{1,0:T(8,128)(2,1)S(1)}, u32[]{:S(2)}, u32[]{:S(2)}) collective-permute-start(bf16[8,1200]{1,0:T(8,128)(2,1)} %tau_hbm.1), channel_id=1, source_target_pairs={{0,9},{1,8},{2,11},{3,10},{4,13},{5,12},{6,15},{7,14},{8,1},{9,0},... | collective-permute-start | bytes 57608 | tf_op jit(solution)/shard_map/ppermute | solution.py:23
  4.2 0.7 %reshape.16.virt_ref = f32[1,1600]{1,0:T(1,128)S(1)} reshape(f32[1600]{0:T(1024)} %param.13) | data formatting | bytes 12800 | tf_op jit(solution)/shard_map/reshape | solution.py:301
  4.9 1.1 %shard_map.86 = (bf16[8,1200]{1,0:T(8,128)(2,1)S(1)}, s32[95]{0:T(128)S(4)}) custom-call(bf16[8,1200]{1,0:T(8,128)(2,1)} %tau_hbm.1, s32[8]{0:T(128)} %cd_hbm.1, s32[8]{0:T(128)} %ab_hbm.3), custom_call_target="tpu_custom_call" | custom-call | bytes 1048576 | tf_op jit(solution)/shard_map/pallas_call | solution.py:303
  5.9 0.0 collective-permute-done
  6.0 1.9 %collective-permute-start.1 = (bf16[16,1200]{1,0:T(8,128)(2,1)S(1)}, bf16[16,1200]{1,0:T(8,128)(2,1)S(1)}, u32[]{:S(2)}, u32[]{:S(2)}) collective-permute-start(bf16[16,1200]{1,0:T(8,128)(2,1)S(1)} %pad_maximum_fusion.2), channel_id=1, source_target_pairs={{0,5},{1,4},{2,7},{3,6},{4,1},{5,0},{6,3},{7,2},{8,13},{9,12},{10,... | collective-permute-start | bytes 115208 | tf_op jit(solution)/shard_map/ppermute | solution.py:23
  7.9 1.4 %shard_map.87 = (f32[1600,128]{1,0:T(8,128)S(1)}, f32[128,128]{1,0:T(8,128)S(1)}, bf16[960,1408]{1,0:T(8,128)(2,1)S(1)}) custom-call(s32[95]{0:T(128)S(4)} %get-tuple-element.19.table_ref, s32[8]{0:T(128)} %ab_hbm.3, s32[1,128]{1,0:T(1,128)} %bitcast.9, f32[1,128]{1,0:T(1,128)} %bitcast.10, f32[1,1600]{1,0:T(1,128)S(1)} %reshape.16.virt_ref, ...), custom_call_target="tpu_custom_call" | custom-call | flops 2048000 | bytes 819200 | tf_op jit(solution)/shard_map/pallas_call | solution.py:320
  9.3 0.2 collective-permute-done.1
  9.6 1.9 %collective-permute-start.2 = (bf16[32,1200]{1,0:T(8,128)(2,1)S(1)}, bf16[32,1200]{1,0:T(8,128)(2,1)S(1)}, u32[]{:S(2)}, u32[]{:S(2)}) collective-permute-start(bf16[32,1200]{1,0:T(8,128)(2,1)S(1)} %pad_maximum_fusion.1), channel_id=1, source_target_pairs={{0,3},{1,2},{2,1},{3,0},{4,7},{5,6},{6,5},{7,4},{8,11},{9,10},{10,... | collective-permute-start | bytes 230408 | tf_op jit(solution)/shard_map/ppermute | solution.py:23
  11.5 1.3 %shard_map.88 = (bf16[640,1408]{1,0:T(8,128)(2,1)S(1)}, bf16[9,160,1408]{2,1,0:T(8,128)(2,1)S(1)}, f32[8,128]{1,0:T(8,128)S(1)}) custom-call(s32[95]{0:T(128)S(4)} %get-tuple-element.19.table_ref, f32[128,128]{1,0:T(8,128)S(1)} %get-tuple-element.26.after_ref.label_ref, bf16[1600,3200]{1,0:T(8,128)(2,1)} %bitcast.8), custom_call_target="tpu_custom_call" | custom-call | bytes 3840000 | tf_op jit(solution)/shard_map/pallas_call | solution.py:344
  12.8 1.2 %collective-permute-done.2 = bf16[32,1200]{1,0:T(8,128)(2,1)S(1)} collective-permute-done((bf16[32,1200]{1,0:T(8,128)(2,1)S(1)}, bf16[32,1200]{1,0:T(8,128)(2,1)S(1)}, u32[]{:S(2)}, u32[]{:S(2)}) %collective-permute-start.2) | collective-permute-done | bytes 76832 | tf_op jit(solution)/shard_map/ppermute | solution.py:23
  14.0 0.3 %collective-permute-start.3 = (bf16[64,1200]{1,0:T(8,128)(2,1)S(1)}, bf16[64,1200]{1,0:T(8,128)(2,1)S(1)}, u32[]{:S(2)}, u32[]{:S(2)}) collective-permute-start(bf16[64,1200]{1,0:T(8,128)(2,1)S(1)} %pad_maximum_fusion.source_ref), channel_id=1, source_target_pairs={{0,1},{1,0},{2,3},{3,2},{4,5},{5,4},{6,7},{7,6},{8,9},{9,8},{10,11... | collective-permute-start | bytes 460808 | tf_op jit(solution)/shard_map/ppermute | solution.py:23
  14.4 0.2 shard_map.89.first_ref
  14.6 0.9 %collective-permute-done.3.second_ref = bf16[64,1200]{1,0:T(8,128)(2,1)S(1)} collective-permute-done((bf16[64,1200]{1,0:T(8,128)(2,1)S(1)}, bf16[64,1200]{1,0:T(8,128)(2,1)S(1)}, u32[]{:S(2)}, u32[]{:S(2)}) %collective-permute-start.3) | collective-permute-done | bytes 153632 | tf_op jit(solution)/shard_map/ppermute | solution.py:23
  15.5 1.0 %shard_map.90 = (f32[1600,128]{1,0:T(8,128)S(1)}, f32[1,128]{1,0:T(1,128)S(1)}) custom-call(s32[95]{0:T(128)S(4)} %get-tuple-element.19.table_ref, bf16[64,1200]{1,0:T(8,128)(2,1)S(1)} %collective-permute-done.3.second_ref, f32[128,128]{1,0:T(8,128)S(1)} %get-tuple-element.26.after_ref.label_ref, f32[64,1408]{1,0:T(8,128)S(1)} %shard_map.89.first_ref, ...), custom_call_target="tpu_custom_call" | custom-call | flops 491520000 | bytes 4659200 | tf_op jit(solution)/shard_map/pallas_call | solution.py:372
  16.5 3.1 %collective-permute-start.4 = (f32[1,128]{1,0:T(1,128)S(1)}, f32[1,128]{1,0:T(1,128)S(1)}, u32[]{:S(2)}, u32[]{:S(2)}) collective-permute-start(f32[1,128]{1,0:T(1,128)S(1)} %get-tuple-element.35), channel_id=1, source_target_pairs={{0,9},{1,8},{2,11},{3,10},{4,13},{5,12},{6,15},{7,14},{8,1},{9,0},... | collective-permute-start | bytes 1544 | tf_op jit(solution)/shard_map/ppermute | solution.py:23
  19.6 1.3 %collective-permute-done.4 = f32[1,128]{1,0:T(1,128)S(1)} collective-permute-done((f32[1,128]{1,0:T(1,128)S(1)}, f32[1,128]{1,0:T(1,128)S(1)}, u32[]{:S(2)}, u32[]{:S(2)}) %collective-permute-start.4) | collective-permute-done | bytes 544 | tf_op jit(solution)/shard_map/ppermute | solution.py:23
  20.9 3.0 %collective-permute-start.5 = (f32[1,128]{1,0:T(1,128)S(1)}, f32[1,128]{1,0:T(1,128)S(1)}, u32[]{:S(2)}, u32[]{:S(2)}) collective-permute-start(f32[1,128]{1,0:T(1,128)S(1)} %add.12), channel_id=1, source_target_pairs={{0,5},{1,4},{2,7},{3,6},{4,1},{5,0},{6,3},{7,2},{8,13},{9,12},{10,... | collective-permute-start | bytes 1544 | tf_op jit(solution)/shard_map/ppermute | solution.py:23
  23.9 1.3 %collective-permute-done.5 = f32[1,128]{1,0:T(1,128)S(1)} collective-permute-done((f32[1,128]{1,0:T(1,128)S(1)}, f32[1,128]{1,0:T(1,128)S(1)}, u32[]{:S(2)}, u32[]{:S(2)}) %collective-permute-start.5) | collective-permute-done | bytes 544 | tf_op jit(solution)/shard_map/ppermute | solution.py:23
  25.2 0.8 %collective-permute-start.6 = (f32[1,128]{1,0:T(1,128)S(1)}, f32[1,128]{1,0:T(1,128)S(1)}, u32[]{:S(2)}, u32[]{:S(2)}) collective-permute-start(f32[1,128]{1,0:T(1,128)S(1)} %add.13), channel_id=1, source_target_pairs={{0,3},{1,2},{2,1},{3,0},{4,7},{5,6},{6,5},{7,4},{8,11},{9,10},{10,... | collective-permute-start | bytes 1544 | tf_op jit(solution)/shard_map/ppermute | solution.py:23
  26.0 2.2 %collective-permute-done.6 = f32[1,128]{1,0:T(1,128)S(1)} collective-permute-done((f32[1,128]{1,0:T(1,128)S(1)}, f32[1,128]{1,0:T(1,128)S(1)}, u32[]{:S(2)}, u32[]{:S(2)}) %collective-permute-start.6) | collective-permute-done | bytes 544 | tf_op jit(solution)/shard_map/ppermute | solution.py:23
  28.1 0.0 collective-permute-start.7
  28.1 0.9 %copy.9 = f32[128,1600]{0,1:T(8,128)} copy(f32[128,1600]{0,1:T(8,128)S(1)} %bitcast.6) | data formatting | bytes 1638400
  29.0 0.2 collective-permute-done.7
  29.3 0.5 %add_bitcast_fusion = f32[128]{0:T(128)} fusion(f32[1,128]{1,0:T(1,128)S(1)} %add.14, f32[1,128]{1,0:T(1,128)S(1)} %collective-permute-done.7), kind=kLoop, calls=%fused_computation.3 | loop fusion | flops 128 | bytes 1536 | tf_op jit(solution)/shard_map/reshape | solution.py:390
  (6 shorter events, 0.0 us)
Async XLA Ops:
  0.6 5.3 %collective-permute-start = (bf16[8,1200]{1,0:T(8,128)(2,1)}, bf16[8,1200]{1,0:T(8,128)(2,1)S(1)}, u32[]{:S(2)}, u32[]{:S(2)}) collective-permute-start(bf16[8,1200]{1,0:T(8,128)(2,1)} %tau_hbm.1), channel_id=1, source_target_pairs={{0,9},{1,8},{2,11},{3,10},{4,13},{5,12},{6,15},{7,14},{8,1},{9,0},... | collective-permute-start | bytes 57608 | tf_op jit(solution)/shard_map/ppermute | solution.py:23
  6.0 3.6 %collective-permute-start.1 = (bf16[16,1200]{1,0:T(8,128)(2,1)S(1)}, bf16[16,1200]{1,0:T(8,128)(2,1)S(1)}, u32[]{:S(2)}, u32[]{:S(2)}) collective-permute-start(bf16[16,1200]{1,0:T(8,128)(2,1)S(1)} %pad_maximum_fusion.2), channel_id=1, source_target_pairs={{0,5},{1,4},{2,7},{3,6},{4,1},{5,0},{6,3},{7,2},{8,13},{9,12},{10,... | collective-permute-start | bytes 115208 | tf_op jit(solution)/shard_map/ppermute | solution.py:23
  9.6 4.4 %collective-permute-start.2 = (bf16[32,1200]{1,0:T(8,128)(2,1)S(1)}, bf16[32,1200]{1,0:T(8,128)(2,1)S(1)}, u32[]{:S(2)}, u32[]{:S(2)}) collective-permute-start(bf16[32,1200]{1,0:T(8,128)(2,1)S(1)} %pad_maximum_fusion.1), channel_id=1, source_target_pairs={{0,3},{1,2},{2,1},{3,0},{4,7},{5,6},{6,5},{7,4},{8,11},{9,10},{10,... | collective-permute-start | bytes 230408 | tf_op jit(solution)/shard_map/ppermute | solution.py:23
  14.0 1.5 %collective-permute-start.3 = (bf16[64,1200]{1,0:T(8,128)(2,1)S(1)}, bf16[64,1200]{1,0:T(8,128)(2,1)S(1)}, u32[]{:S(2)}, u32[]{:S(2)}) collective-permute-start(bf16[64,1200]{1,0:T(8,128)(2,1)S(1)} %pad_maximum_fusion.source_ref), channel_id=1, source_target_pairs={{0,1},{1,0},{2,3},{3,2},{4,5},{5,4},{6,7},{7,6},{8,9},{9,8},{10,11... | collective-permute-start | bytes 460808 | tf_op jit(solution)/shard_map/ppermute | solution.py:23
  16.5 4.4 %collective-permute-start.4 = (f32[1,128]{1,0:T(1,128)S(1)}, f32[1,128]{1,0:T(1,128)S(1)}, u32[]{:S(2)}, u32[]{:S(2)}) collective-permute-start(f32[1,128]{1,0:T(1,128)S(1)} %get-tuple-element.35), channel_id=1, source_target_pairs={{0,9},{1,8},{2,11},{3,10},{4,13},{5,12},{6,15},{7,14},{8,1},{9,0},... | collective-permute-start | bytes 1544 | tf_op jit(solution)/shard_map/ppermute | solution.py:23
  20.9 4.3 %collective-permute-start.5 = (f32[1,128]{1,0:T(1,128)S(1)}, f32[1,128]{1,0:T(1,128)S(1)}, u32[]{:S(2)}, u32[]{:S(2)}) collective-permute-start(f32[1,128]{1,0:T(1,128)S(1)} %add.12), channel_id=1, source_target_pairs={{0,5},{1,4},{2,7},{3,6},{4,1},{5,0},{6,3},{7,2},{8,13},{9,12},{10,... | collective-permute-start | bytes 1544 | tf_op jit(solution)/shard_map/ppermute | solution.py:23
  25.2 3.0 %collective-permute-start.6 = (f32[1,128]{1,0:T(1,128)S(1)}, f32[1,128]{1,0:T(1,128)S(1)}, u32[]{:S(2)}, u32[]{:S(2)}) collective-permute-start(f32[1,128]{1,0:T(1,128)S(1)} %add.13), channel_id=1, source_target_pairs={{0,3},{1,2},{2,1},{3,0},{4,7},{5,6},{6,5},{7,4},{8,11},{9,10},{10,... | collective-permute-start | bytes 1544 | tf_op jit(solution)/shard_map/ppermute | solution.py:23
  28.1 1.1 %collective-permute-start.7 = (f32[1,128]{1,0:T(1,128)S(1)}, f32[1,128]{1,0:T(1,128)S(1)}, u32[]{:S(2)}, u32[]{:S(2)}) collective-permute-start(f32[1,128]{1,0:T(1,128)S(1)} %add.14), channel_id=1, source_target_pairs={{0,1},{1,0},{2,3},{3,2},{4,5},{5,4},{6,7},{7,6},{8,9},{9,8},{10,11... | collective-permute-start | bytes 1544 | tf_op jit(solution)/shard_map/ppermute | solution.py:23

commit v5 on v4

--- a/solution.py
+++ b/solution.py
@@ -179,68 +179,72 @@
     mark_ref[...] = jnp.zeros(mark_ref.shape, F32)
 
 
-def place(count, rows, first, fields, table_ref, source_ref, label_ref, tau_ref, placed_ref):
+def place(count, rows, mask, fields, table_ref, source, label_ref, tau_ref, placed_ref):
     me = lax.axis_index("col")
-    half, width = source_ref.shape
+    half, width = source.shape
     window = tau_ref.shape[1]
     keys = generators(count)
-    tau_ref[:, :width] = source_ref[...].astype(F32)
+    tau_ref[:, :width] = source[...].astype(F32)
     lane = lax.broadcasted_iota(I32, (1, window), 1)
     owners = []
     for block in range(half // rows):
-        mask = 0 if first else keys[-1]
-        for step, key in enumerate(keys[:-1]):
-            mask ^= key if (block >> step) & 1 else 0
-        owners.append(me ^ mask)
+        flips = mask
+        for step, key in enumerate(keys[:-2]):
+            flips ^= key if (block >> step) & 1 else 0
+        owners.append(me ^ flips)
     labels = jnp.concatenate(
         [label_ref[pl.ds(pl.multiple_of(owner * rows, rows), rows), :] for owner in owners], axis=0
     )[:, :1]
+    places = [pl.ds(pl.multiple_of(lax.shift_right_logical(owner, 2) * rows, rows), rows) for owner in owners]
 
     def moved(i):
         place_at, size = table_ref[fields + 4 * i + 2], table_ref[fields + 4 * i + 3]
         return jnp.where((lane >= place_at) & (lane < place_at + size), pltpu.roll(tau_ref[...], place_at, 1), 0.0)
 
     def store(values):
-        for block, owner in enumerate(owners):
-            to = pl.ds(pl.multiple_of(lax.div(owner, 2) * rows, rows), rows)
+        for block, to in enumerate(places):
             placed_ref[to, :] = values[block * rows:(block + 1) * rows]
 
     store(moved(0))
 
     @pl.loop(1, table_ref[1])
     def _(i):
-        old = jnp.concatenate(
-            [placed_ref[pl.ds(pl.multiple_of(lax.div(owner, 2) * rows, rows), rows), :] for owner in owners], axis=0
-        )
+        old = jnp.concatenate([placed_ref[to, :] for to in places], axis=0)
         store(jnp.where(labels == table_ref[fields + 4 * i].astype(F32), moved(i), old))
 
 
-def first_kernel(count, rows, fields, table_ref, source_ref, label_ref, after_ref, placed_ref, tau_ref):
+def near_kernel(count, rows, fields, table_ref, own_ref, other_ref, label_ref, after_ref, placed_ref, tau_ref):
     del after_ref
-    place(count, rows, True, fields, table_ref, source_ref, label_ref, tau_ref, placed_ref)
+    for i, (mask, source) in enumerate(((0, own_ref), (generators(count)[-1], other_ref))):
+        place(count, rows, mask, fields, table_ref, source, label_ref, tau_ref, placed_ref.at[i])
+
+
+def far_kernel(count, rows, fields, table_ref, source_ref, label_ref, placed_ref, tau_ref):
+    place(count, rows, generators(count)[-2], fields, table_ref, source_ref, label_ref, tau_ref, placed_ref)
 
 
 def ladder_kernel(
-    count, rows, total, tile, width, cd_rows, table_ref, second_ref, label_ref, first_ref, early_ref, packed_ref, extra_ref, weight_ref,
+    count, rows, total, tile, width, cd_rows, table_ref, last_ref, label_ref, near_ref, far_ref, early_ref, packed_ref, extra_ref, weight_ref,
     update_ref, energy_ref, tau_ref, other_ref, dense_ref, parts_ref,
 ):
     cols, pairs = weight_ref.shape
-    half, window = tau_ref.shape
+    window = tau_ref.shape[1]
     tiles = cols // tile
     fields, extras = fields_of(tiles, extra_ref.shape[0] - 1)
-    place(count, rows, False, fields, table_ref, second_ref, label_ref, tau_ref, other_ref)
+    keys = generators(count)
+    place(count, rows, keys[-1] ^ keys[-2], fields, table_ref, last_ref, label_ref, tau_ref, other_ref)
     me = lax.axis_index("col")
 
-    def in_order(chip):
-        flips = lax.shift_right_logical(me, 1) ^ chip
-        odd = me & 1
-        for step in range(len(generators(count)) - 1):
-            odd = odd ^ (lax.shift_right_logical(flips, step) & 1)
-        here = slice(chip * rows, (chip + 1) * rows)
-        own, other = first_ref[here], other_ref[here]
-        return [jnp.where(odd == 1, other, own), jnp.where(odd == 1, own, other)]
-
-    both = jnp.concatenate([part for chip in range(half // rows) for part in in_order(chip)], axis=0)
+    def block_of(owner):
+        flips = me ^ owner
+        other = flips & 1
+        for bit in range(1, len(keys)):
+            other = other ^ (lax.shift_right_logical(flips, bit) & 1)
+        here = pl.ds(owner // 4 * rows, rows)
+        away = jnp.where(other == 1, other_ref[here, :], far_ref[here, :])
+        return jnp.where(flips & 2 == 2, away, near_ref[other, here, :])
+
+    both = jnp.concatenate([block_of(owner) for owner in range(count)], axis=0)
     dense_ref[...] = both.astype(dense_ref.dtype)
 
     def integrals_of(t, size):
@@ -313,7 +317,7 @@
     )(far(tau_packed), far(cd_sizes), far(ab_sizes))
     table = pltpu.with_memory_space_constraint(table, pltpu.SMEM)
     sent = tau_packed
-    for step, key in enumerate(keys[:-1]):
+    for step, key in enumerate(keys[:-2]):
         held = jnp.concatenate([held, swap(sent, key, count)], axis=0)
         if step == 0:
             held, virt_row, occ_energy = lax.optimization_barrier((held, virt_row, occ_energy))
@@ -339,44 +343,56 @@
                 table, far(ab_sizes), far(pair_irrep.reshape(1, pairs)), far(occ_energy.reshape(1, pairs)),
                 near(virt_row), turned,
             )
-        elif step == 1:
-            held, label = lax.optimization_barrier((held, label))
-            packed, extra, mark = pl.pallas_call(
-                functools.partial(fetch_kernel, tile, width),
-                out_shape=(
-                    pltpu.VMEM((cols - early, window), integrals.dtype),
-                    pltpu.VMEM((irreps + 1, tile, window), integrals.dtype),
-                    pltpu.VMEM((8, LANES), F32),
-                ),
-                in_specs=[SMEM, ANY, ANY],
-                out_specs=(VMEM, VMEM, VMEM),
-                scratch_shapes=[pltpu.SemaphoreType.DMA((tiles + irreps + 1,))],
-                compiler_params=pltpu.CompilerParams(vmem_limit_bytes=1 << 20),
-                cost_estimate=pl.CostEstimate(flops=0, bytes_accessed=2 * cols * width, transcendentals=0),
-            )(table, near(label), turned)
-        elif step == 2:
-            held, mark = lax.optimization_barrier((held, mark))
         else:
             held = lax.optimization_barrier(held)
         sent = held
-    second = swap(held, keys[-1], count)
-    first = pl.pallas_call(
-        functools.partial(first_kernel, count, rows, fields),
-        out_shape=pltpu.VMEM((pairs // 2, window), F32),
-        in_specs=[SMEM, VMEM, VMEM, ANY],
+    held, label = lax.optimization_barrier((held, label))
+    away = swap(held, keys[-2], count)
+    other = swap(held, keys[-1], count)
+    packed, extra, mark = pl.pallas_call(
+        functools.partial(fetch_kernel, tile, width),
+        out_shape=(
+            pltpu.VMEM((cols - early, window), integrals.dtype),
+            pltpu.VMEM((irreps + 1, tile, window), integrals.dtype),
+            pltpu.VMEM((8, LANES), F32),
+        ),
+        in_specs=[SMEM, ANY, ANY],
+        out_specs=(VMEM, VMEM, VMEM),
+        scratch_shapes=[pltpu.SemaphoreType.DMA((tiles + irreps + 1,))],
+        compiler_params=pltpu.CompilerParams(vmem_limit_bytes=1 << 20),
+        cost_estimate=pl.CostEstimate(flops=0, bytes_accessed=2 * cols * width, transcendentals=0),
+    )(table, near(label), turned)
+    place_params = pltpu.CompilerParams(vmem_limit_bytes=(1 << 20) + 16 * pairs * window)
+    place_cost = pl.CostEstimate(flops=10 * pairs * window, bytes_accessed=4 * pairs * window, transcendentals=0)
+    quarter = pairs // 4
+    placed_near = pl.pallas_call(
+        functools.partial(near_kernel, count, rows, fields),
+        out_shape=pltpu.VMEM((2, quarter, window), F32),
+        in_specs=[SMEM, VMEM, VMEM, VMEM, ANY],
         out_specs=VMEM,
-        scratch_shapes=[pltpu.VMEM((pairs // 2, window), F32)],
-        compiler_params=pltpu.CompilerParams(vmem_limit_bytes=(1 << 20) + 16 * pairs * window),
-        cost_estimate=pl.CostEstimate(flops=10 * pairs * window, bytes_accessed=4 * pairs * window, transcendentals=0),
-    )(table, near(held), near(label), near(mark))
+        scratch_shapes=[pltpu.VMEM((quarter, window), F32)],
+        compiler_params=place_params,
+        cost_estimate=place_cost,
+    )(table, near(held), near(other), near(label), near(mark))
+    away, placed_near = lax.optimization_barrier((away, placed_near))
+    last = swap(away, keys[-1], count)
+    placed_far = pl.pallas_call(
+        functools.partial(far_kernel, count, rows, fields),
+        out_shape=pltpu.VMEM((quarter, window), F32),
+        in_specs=[SMEM, VMEM, VMEM],
+        out_specs=VMEM,
+        scratch_shapes=[pltpu.VMEM((quarter, window), F32)],
+        compiler_params=place_params,
+        cost_estimate=place_cost,
+    )(table, near(away), near(label))
     update, energy = pl.pallas_call(
         functools.partial(ladder_kernel, count, rows, cols * count, tile, width, cd_rows),
         out_shape=(pltpu.VMEM((cols, pairs), F32), pltpu.VMEM((1, pairs), F32)),
-        in_specs=[SMEM] + [VMEM] * 7,
+        in_specs=[SMEM] + [VMEM] * 8,
         out_specs=(VMEM, VMEM),
         scratch_shapes=[
-            pltpu.VMEM((pairs // 2, window), F32),
-            pltpu.VMEM((pairs // 2, window), F32),
+            pltpu.VMEM((quarter, window), F32),
+            pltpu.VMEM((quarter, window), F32),
             pltpu.VMEM((pairs, window), jnp.bfloat16),
             pltpu.VMEM((tiles + irreps + 1, 8, pairs), F32),
         ],
@@ -384,7 +400,7 @@
         cost_estimate=pl.CostEstimate(
             flops=2 * cols * width * pairs, bytes_accessed=2 * cols * width + 4 * cols * pairs, transcendentals=0
         ),
-    )(table, near(second), near(label), near(first), near(packed_early), near(packed), near(extra), near(weight))
+    )(table, near(last), near(label), near(placed_near), near(placed_far), near(packed_early), near(packed), near(extra), near(weight))
     for key in keys:
         energy = energy + swap(energy, key, count)
     return update.T, energy.reshape(pairs)

time: 30.1 us -> 30 us (level)
  Pallas kernels: 5.09 us -> 7.38 us
  waiting for transfers between devices: 7.31 us -> 6.03 us
  starting transfers between devices: 14.5 us -> 13.4 us
    ppermute x8 -> x9, waiting for transfers between devices: 7.31 us -> 6.03 us  [swap(): return lax.ppermute(value, 'col', [(i, i ^ key) for i in range(count)])]
    ppermute x8 -> x9, starting transfers between devices: 14.5 us -> 13.4 us  [swap(): return lax.ppermute(value, 'col', [(i, i ^ key) for i in range(count)])]
    pallas_call x1, Pallas kernels: 1.04 us -> 1.86 us  [shards(): pl.pallas_call(functools.partial(ladder_kernel, count, rows, cols * count...]
    pallas_call x1 -> x2, Pallas kernels: 0.24 us -> 1.03 us  [the longest x1 0.69 us: shards(): pl.pallas_call(functools.partial(near_kernel, count, rows, fields), out_s...]
    pallas_call x1, Pallas kernels: 1.32 us -> 1.67 us  [shards(): pl.pallas_call(functools.partial(fetch_kernel, tile, width), out_shape=(p...]
    pallas_call x1, Pallas kernels: 1.43 us -> 1.77 us  [shards(): pl.pallas_call(functools.partial(weight_kernel, tile, width), out_shape=(...]
  transfers between devices with their start and end apart: 8 -> 9, of which waited for: 7 -> 5; matrix products, arithmetic and copies ran while one was open for 5% -> 5% of each run, Pallas kernels for 14% -> 19%
where the time goes in v5:
time: 30 us; the launch traced here: 29.6 us
  starting transfers between devices  13.4 us (45%)
  Pallas kernels  7.38 us (25%)
  waiting for transfers between devices  6.03 us (20%)
  local copies, waits for them, and re-layouts  1.59 us (5%)
  between operations  0.72 us (2%)
  other arithmetic  0.54 us (2%)
    ppermute x9, starting transfers between devices, swap(): return lax.ppermute(value, 'col', [(i, i ^ key) for i in range(count)])  13.4 us
    ppermute x9, waiting for transfers between devices, swap(): return lax.ppermute(value, 'col', [(i, i ^ key) for i in range(count)])  6.03 us
    pallas_call x1, Pallas kernels, shards(): pl.pallas_call(functools.partial(ladder_kernel, count, rows, cols * count...  1.86 us
    pallas_call x1, Pallas kernels, shards(): pl.pallas_call(functools.partial(weight_kernel, tile, width), out_shape=(...  1.77 us
    pallas_call x1, Pallas kernels, shards(): pl.pallas_call(functools.partial(fetch_kernel, tile, width), out_shape=(p...  1.67 us
    pallas_call x1, Pallas kernels, shards(): pl.pallas_call(functools.partial(plan_kernel, tile, cd_rows, width, cols)...  1.05 us
    unnamed x1, local copies, waits for them, and re-layouts  0.89 us
    reshape x1, local copies, waits for them, and re-layouts, shards(): virt_row = virt_energy.reshape(1, cols)  0.7 us
  transfers between devices with their start and end apart: 9, of which 5 were waited for; matrix products, arithmetic and copies ran while one was open for 5% of the time, Pallas kernels for 19%

profile of v5, /device:TPU:0, one launch (start us, length us, event | category | flops | bytes accessed | tf_op | source)
XLA Modules:
  0.0 29.6 jit_solution(12137325266040560332)
XLA Ops:
  0.6 3.5 %collective-permute-start = (bf16[8,1200]{1,0:T(8,128)(2,1)}, bf16[8,1200]{1,0:T(8,128)(2,1)S(1)}, u32[]{:S(2)}, u32[]{:S(2)}) collective-permute-start(bf16[8,1200]{1,0:T(8,128)(2,1)} %tau_hbm.1), channel_id=1, source_target_pairs={{0,9},{1,8},{2,11},{3,10},{4,13},{5,12},{6,15},{7,14},{8,1},{9,0},... | collective-permute-start | bytes 57608 | tf_op jit(solution)/shard_map/ppermute | solution.py:23
  4.2 0.7 %reshape.16.virt_ref = f32[1,1600]{1,0:T(1,128)S(1)} reshape(f32[1600]{0:T(1024)} %param.13) | data formatting | bytes 12800 | tf_op jit(solution)/shard_map/reshape | solution.py:305
  4.9 1.1 %shard_map.86 = (bf16[8,1200]{1,0:T(8,128)(2,1)S(1)}, s32[95]{0:T(128)S(4)}) custom-call(bf16[8,1200]{1,0:T(8,128)(2,1)} %tau_hbm.1, s32[8]{0:T(128)} %cd_hbm.1, s32[8]{0:T(128)} %ab_hbm.3), custom_call_target="tpu_custom_call" | custom-call | bytes 1048576 | tf_op jit(solution)/shard_map/pallas_call | solution.py:307
  5.9 0.0 collective-permute-done
  6.0 1.9 %collective-permute-start.1 = (bf16[16,1200]{1,0:T(8,128)(2,1)S(1)}, bf16[16,1200]{1,0:T(8,128)(2,1)S(1)}, u32[]{:S(2)}, u32[]{:S(2)}) collective-permute-start(bf16[16,1200]{1,0:T(8,128)(2,1)S(1)} %pad_maximum_fusion.1), channel_id=1, source_target_pairs={{0,5},{1,4},{2,7},{3,6},{4,1},{5,0},{6,3},{7,2},{8,13},{9,12},{10,... | collective-permute-start | bytes 115208 | tf_op jit(solution)/shard_map/ppermute | solution.py:23
  7.9 1.8 %shard_map.87 = (f32[1600,128]{1,0:T(8,128)S(1)}, f32[128,128]{1,0:T(8,128)S(1)}, bf16[960,1408]{1,0:T(8,128)(2,1)S(1)}) custom-call(s32[95]{0:T(128)S(4)} %get-tuple-element.19.table_ref, s32[8]{0:T(128)} %ab_hbm.3, s32[1,128]{1,0:T(1,128)} %bitcast.9, f32[1,128]{1,0:T(1,128)} %bitcast.10, f32[1,1600]{1,0:T(1,128)S(1)} %reshape.16.virt_ref, ...), custom_call_target="tpu_custom_call" | custom-call | flops 2048000 | bytes 819200 | tf_op jit(solution)/shard_map/pallas_call | solution.py:324
  9.7 0.0 collective-permute-done.1
  9.7 0.5 %collective-permute-start.3 = (bf16[32,1200]{1,0:T(8,128)(2,1)S(1)}, bf16[32,1200]{1,0:T(8,128)(2,1)S(1)}, u32[]{:S(2)}, u32[]{:S(2)}) collective-permute-start(bf16[32,1200]{1,0:T(8,128)(2,1)S(1)} %pad_maximum_fusion.own_ref), channel_id=1, source_target_pairs={{0,1},{1,0},{2,3},{3,2},{4,5},{5,4},{6,7},{7,6},{8,9},{9,8},{10,11... | collective-permute-start | bytes 230408 | tf_op jit(solution)/shard_map/ppermute | solution.py:23
  10.2 1.6 %collective-permute-start.2 = (bf16[32,1200]{1,0:T(8,128)(2,1)S(1)}, bf16[32,1200]{1,0:T(8,128)(2,1)S(1)}, u32[]{:S(2)}, u32[]{:S(2)}) collective-permute-start(bf16[32,1200]{1,0:T(8,128)(2,1)S(1)} %pad_maximum_fusion.own_ref), channel_id=1, source_target_pairs={{0,3},{1,2},{2,1},{3,0},{4,7},{5,6},{6,5},{7,4},{8,11},{9,10},{10,... | collective-permute-start | bytes 230408 | tf_op jit(solution)/shard_map/ppermute | solution.py:23
  11.8 1.7 %shard_map.88 = (bf16[640,1408]{1,0:T(8,128)(2,1)S(1)}, bf16[9,160,1408]{2,1,0:T(8,128)(2,1)S(1)}, f32[8,128]{1,0:T(8,128)S(1)}) custom-call(s32[95]{0:T(128)S(4)} %get-tuple-element.19.table_ref, f32[128,128]{1,0:T(8,128)S(1)} %get-tuple-element.26.after_ref.label_ref, bf16[1600,3200]{1,0:T(8,128)(2,1)} %bitcast.8), custom_call_target="tpu_custom_call" | custom-call | bytes 3840000 | tf_op jit(solution)/shard_map/pallas_call | solution.py:352
  13.5 0.0 collective-permute-done.3.other_ref
  13.5 0.7 %shard_map.89.near_ref = f32[2,32,1408]{2,1,0:T(8,128)S(1)} custom-call(s32[95]{0:T(128)S(4)} %get-tuple-element.19.table_ref, bf16[32,1200]{1,0:T(8,128)(2,1)S(1)} %pad_maximum_fusion.own_ref, bf16[32,1200]{1,0:T(8,128)(2,1)S(1)} %collective-permute-done.3.other_ref, f32[128,128]{1,0:T(8,128)S(1)} %get-tuple-element.26.after_ref.label_ref, ...), custom_call_target="tpu_custom_call" | custom-call | flops 1802240 | bytes 720896 | tf_op jit(solution)/shard_map/pallas_call | solution.py:368
  14.2 0.5 %collective-permute-done.2.source_ref = bf16[32,1200]{1,0:T(8,128)(2,1)S(1)} collective-permute-done((bf16[32,1200]{1,0:T(8,128)(2,1)S(1)}, bf16[32,1200]{1,0:T(8,128)(2,1)S(1)}, u32[]{:S(2)}, u32[]{:S(2)}) %collective-permute-start.2) | collective-permute-done | bytes 76832 | tf_op jit(solution)/shard_map/ppermute | solution.py:23
  14.7 0.1 collective-permute-start.4
  14.8 0.3 %shard_map.90.far_ref = f32[32,1408]{1,0:T(8,128)S(1)} custom-call(s32[95]{0:T(128)S(4)} %get-tuple-element.19.table_ref, bf16[32,1200]{1,0:T(8,128)(2,1)S(1)} %collective-permute-done.2.source_ref, f32[128,128]{1,0:T(8,128)S(1)} %get-tuple-element.26.after_ref.label_ref), custom_call_target="tpu_custom_call" | custom-call | flops 1802240 | bytes 720896 | tf_op jit(solution)/shard_map/pallas_call | solution.py:379
  15.2 0.8 %collective-permute-done.4.last_ref = bf16[32,1200]{1,0:T(8,128)(2,1)S(1)} collective-permute-done((bf16[32,1200]{1,0:T(8,128)(2,1)S(1)}, bf16[32,1200]{1,0:T(8,128)(2,1)S(1)}, u32[]{:S(2)}, u32[]{:S(2)}) %collective-permute-start.4) | collective-permute-done | bytes 76832 | tf_op jit(solution)/shard_map/ppermute | solution.py:23
  16.0 1.9 %shard_map.91 = (f32[1600,128]{1,0:T(8,128)S(1)}, f32[1,128]{1,0:T(1,128)S(1)}) custom-call(s32[95]{0:T(128)S(4)} %get-tuple-element.19.table_ref, bf16[32,1200]{1,0:T(8,128)(2,1)S(1)} %collective-permute-done.4.last_ref, f32[128,128]{1,0:T(8,128)S(1)} %get-tuple-element.26.after_ref.label_ref, f32[2,32,1408]{2,1,0:T(8,128)S(1)} %shard_map.89.near_ref, ...), custom_call_target="tpu_custom_call" | custom-call | flops 491520000 | bytes 4659200 | tf_op jit(solution)/shard_map/pallas_call | solution.py:388
  17.8 2.2 %collective-permute-start.5 = (f32[1,128]{1,0:T(1,128)S(1)}, f32[1,128]{1,0:T(1,128)S(1)}, u32[]{:S(2)}, u32[]{:S(2)}) collective-permute-start(f32[1,128]{1,0:T(1,128)S(1)} %get-tuple-element.35), channel_id=1, source_target_pairs={{0,9},{1,8},{2,11},{3,10},{4,13},{5,12},{6,15},{7,14},{8,1},{9,0},... | collective-permute-start | bytes 1544 | tf_op jit(solution)/shard_map/ppermute | solution.py:23
  20.1 1.7 %collective-permute-done.5 = f32[1,128]{1,0:T(1,128)S(1)} collective-permute-done((f32[1,128]{1,0:T(1,128)S(1)}, f32[1,128]{1,0:T(1,128)S(1)}, u32[]{:S(2)}, u32[]{:S(2)}) %collective-permute-start.5) | collective-permute-done | bytes 544 | tf_op jit(solution)/shard_map/ppermute | solution.py:23
  21.8 1.5 %collective-permute-start.6 = (f32[1,128]{1,0:T(1,128)S(1)}, f32[1,128]{1,0:T(1,128)S(1)}, u32[]{:S(2)}, u32[]{:S(2)}) collective-permute-start(f32[1,128]{1,0:T(1,128)S(1)} %add.12), channel_id=1, source_target_pairs={{0,5},{1,4},{2,7},{3,6},{4,1},{5,0},{6,3},{7,2},{8,13},{9,12},{10,... | collective-permute-start | bytes 1544 | tf_op jit(solution)/shard_map/ppermute | solution.py:23
  23.2 1.5 %collective-permute-done.6 = f32[1,128]{1,0:T(1,128)S(1)} collective-permute-done((f32[1,128]{1,0:T(1,128)S(1)}, f32[1,128]{1,0:T(1,128)S(1)}, u32[]{:S(2)}, u32[]{:S(2)}) %collective-permute-start.6) | collective-permute-done | bytes 544 | tf_op jit(solution)/shard_map/ppermute | solution.py:23
  24.7 1.4 %collective-permute-start.7 = (f32[1,128]{1,0:T(1,128)S(1)}, f32[1,128]{1,0:T(1,128)S(1)}, u32[]{:S(2)}, u32[]{:S(2)}) collective-permute-start(f32[1,128]{1,0:T(1,128)S(1)} %add.13), channel_id=1, source_target_pairs={{0,3},{1,2},{2,1},{3,0},{4,7},{5,6},{6,5},{7,4},{8,11},{9,10},{10,... | collective-permute-start | bytes 1544 | tf_op jit(solution)/shard_map/ppermute | solution.py:23
  26.1 1.6 %collective-permute-done.7 = f32[1,128]{1,0:T(1,128)S(1)} collective-permute-done((f32[1,128]{1,0:T(1,128)S(1)}, f32[1,128]{1,0:T(1,128)S(1)}, u32[]{:S(2)}, u32[]{:S(2)}) %collective-permute-start.7) | collective-permute-done | bytes 544 | tf_op jit(solution)/shard_map/ppermute | solution.py:23
  27.7 0.5 %collective-permute-start.8 = (f32[1,128]{1,0:T(1,128)S(1)}, f32[1,128]{1,0:T(1,128)S(1)}, u32[]{:S(2)}, u32[]{:S(2)}) collective-permute-start(f32[1,128]{1,0:T(1,128)S(1)} %add.14), channel_id=1, source_target_pairs={{0,1},{1,0},{2,3},{3,2},{4,5},{5,4},{6,7},{7,6},{8,9},{9,8},{10,11... | collective-permute-start | bytes 1544 | tf_op jit(solution)/shard_map/ppermute | solution.py:23
  28.2 0.9 %copy.9 = f32[128,1600]{0,1:T(8,128)} copy(f32[128,1600]{0,1:T(8,128)S(1)} %bitcast.6) | data formatting | bytes 1638400
  29.1 0.0 collective-permute-done.8
  29.1 0.5 %add_bitcast_fusion = f32[128]{0:T(128)} fusion(f32[1,128]{1,0:T(1,128)S(1)} %add.14, f32[1,128]{1,0:T(1,128)S(1)} %collective-permute-done.8), kind=kLoop, calls=%fused_computation.2 | loop fusion | flops 128 | bytes 1536 | tf_op jit(solution)/shard_map/reshape | solution.py:406
  (5 shorter events, 0.0 us)
Async XLA Ops:
  0.6 5.3 %collective-permute-start = (bf16[8,1200]{1,0:T(8,128)(2,1)}, bf16[8,1200]{1,0:T(8,128)(2,1)S(1)}, u32[]{:S(2)}, u32[]{:S(2)}) collective-permute-start(bf16[8,1200]{1,0:T(8,128)(2,1)} %tau_hbm.1), channel_id=1, source_target_pairs={{0,9},{1,8},{2,11},{3,10},{4,13},{5,12},{6,15},{7,14},{8,1},{9,0},... | collective-permute-start | bytes 57608 | tf_op jit(solution)/shard_map/ppermute | solution.py:23
  6.0 3.7 %collective-permute-start.1 = (bf16[16,1200]{1,0:T(8,128)(2,1)S(1)}, bf16[16,1200]{1,0:T(8,128)(2,1)S(1)}, u32[]{:S(2)}, u32[]{:S(2)}) collective-permute-start(bf16[16,1200]{1,0:T(8,128)(2,1)S(1)} %pad_maximum_fusion.1), channel_id=1, source_target_pairs={{0,5},{1,4},{2,7},{3,6},{4,1},{5,0},{6,3},{7,2},{8,13},{9,12},{10,... | collective-permute-start | bytes 115208 | tf_op jit(solution)/shard_map/ppermute | solution.py:23
  9.7 3.8 %collective-permute-start.3 = (bf16[32,1200]{1,0:T(8,128)(2,1)S(1)}, bf16[32,1200]{1,0:T(8,128)(2,1)S(1)}, u32[]{:S(2)}, u32[]{:S(2)}) collective-permute-start(bf16[32,1200]{1,0:T(8,128)(2,1)S(1)} %pad_maximum_fusion.own_ref), channel_id=1, source_target_pairs={{0,1},{1,0},{2,3},{3,2},{4,5},{5,4},{6,7},{7,6},{8,9},{9,8},{10,11... | collective-permute-start | bytes 230408 | tf_op jit(solution)/shard_map/ppermute | solution.py:23
  10.2 4.5 %collective-permute-start.2 = (bf16[32,1200]{1,0:T(8,128)(2,1)S(1)}, bf16[32,1200]{1,0:T(8,128)(2,1)S(1)}, u32[]{:S(2)}, u32[]{:S(2)}) collective-permute-start(bf16[32,1200]{1,0:T(8,128)(2,1)S(1)} %pad_maximum_fusion.own_ref), channel_id=1, source_target_pairs={{0,3},{1,2},{2,1},{3,0},{4,7},{5,6},{6,5},{7,4},{8,11},{9,10},{10,... | collective-permute-start | bytes 230408 | tf_op jit(solution)/shard_map/ppermute | solution.py:23
  14.7 1.3 %collective-permute-start.4 = (bf16[32,1200]{1,0:T(8,128)(2,1)S(1)}, bf16[32,1200]{1,0:T(8,128)(2,1)S(1)}, u32[]{:S(2)}, u32[]{:S(2)}) collective-permute-start(bf16[32,1200]{1,0:T(8,128)(2,1)S(1)} %collective-permute-done.2.source_ref), channel_id=1, source_target_pairs={{0,1},{1,0},{2,3},{3,2},{4,5},{5,4},{6,7},{7,6},{8,9},{9,8},{10,11... | collective-permute-start | bytes 230408 | tf_op jit(solution)/shard_map/ppermute | solution.py:23
  17.8 3.9 %collective-permute-start.5 = (f32[1,128]{1,0:T(1,128)S(1)}, f32[1,128]{1,0:T(1,128)S(1)}, u32[]{:S(2)}, u32[]{:S(2)}) collective-permute-start(f32[1,128]{1,0:T(1,128)S(1)} %get-tuple-element.35), channel_id=1, source_target_pairs={{0,9},{1,8},{2,11},{3,10},{4,13},{5,12},{6,15},{7,14},{8,1},{9,0},... | collective-permute-start | bytes 1544 | tf_op jit(solution)/shard_map/ppermute | solution.py:23
  21.8 3.0 %collective-permute-start.6 = (f32[1,128]{1,0:T(1,128)S(1)}, f32[1,128]{1,0:T(1,128)S(1)}, u32[]{:S(2)}, u32[]{:S(2)}) collective-permute-start(f32[1,128]{1,0:T(1,128)S(1)} %add.12), channel_id=1, source_target_pairs={{0,5},{1,4},{2,7},{3,6},{4,1},{5,0},{6,3},{7,2},{8,13},{9,12},{10,... | collective-permute-start | bytes 1544 | tf_op jit(solution)/shard_map/ppermute | solution.py:23
  24.7 3.0 %collective-permute-start.7 = (f32[1,128]{1,0:T(1,128)S(1)}, f32[1,128]{1,0:T(1,128)S(1)}, u32[]{:S(2)}, u32[]{:S(2)}) collective-permute-start(f32[1,128]{1,0:T(1,128)S(1)} %add.13), channel_id=1, source_target_pairs={{0,3},{1,2},{2,1},{3,0},{4,7},{5,6},{6,5},{7,4},{8,11},{9,10},{10,... | collective-permute-start | bytes 1544 | tf_op jit(solution)/shard_map/ppermute | solution.py:23
  27.7 1.4 %collective-permute-start.8 = (f32[1,128]{1,0:T(1,128)S(1)}, f32[1,128]{1,0:T(1,128)S(1)}, u32[]{:S(2)}, u32[]{:S(2)}) collective-permute-start(f32[1,128]{1,0:T(1,128)S(1)} %add.14), channel_id=1, source_target_pairs={{0,1},{1,0},{2,3},{3,2},{4,5},{5,4},{6,7},{7,6},{8,9},{9,8},{10,11... | collective-permute-start | bytes 1544 | tf_op jit(solution)/shard_map/ppermute | solution.py:23

commit v6 on v5

--- a/solution.py
+++ b/solution.py
@@ -88,13 +88,14 @@
     table_ref[2] = extra
 
 
-def plan_kernel(tile, cd_rows, width, cols, tau_hbm, cd_hbm, ab_hbm, own_ref, table_ref, cd_ref, ab_ref, arrived):
+def plan_kernel(tile, cd_rows, width, cols, tau_ref, cd_hbm, ab_hbm, own_ref, table_ref, cd_ref, ab_ref, arrived):
     copies = [
         pltpu.make_async_copy(source, target, arrived.at[i])
-        for i, (source, target) in enumerate(((cd_hbm, cd_ref), (ab_hbm, ab_ref), (tau_hbm, own_ref)))
+        for i, (source, target) in enumerate(((cd_hbm, cd_ref), (ab_hbm, ab_ref)))
     ]
     for copy in copies:
         copy.start()
+    own_ref[...] = tau_ref[...]
     for copy in copies:
         copy.wait()
     plan(cd_ref, ab_ref, table_ref, lax.axis_index("col"), cols, tile, cd_rows, width)
@@ -121,12 +122,14 @@
 
 
 def weight_kernel(
-    tile, width, table_ref, ab_hbm, irrep_hbm, occ_hbm, virt_ref, integrals_ref,
-    weight_ref, label_ref, packed_ref, ab_ref, irrep_ref, occ_ref, arrived, here,
+    tile, width, table_ref, ab_hbm, irrep_hbm, occ_hbm, virt_hbm, integrals_ref,
+    weight_ref, label_ref, packed_ref, ab_ref, irrep_ref, occ_ref, virt_ref, arrived, here,
 ):
     copies = [
         pltpu.make_async_copy(source, target, here.at[i])
-        for i, (source, target) in enumerate(((ab_hbm, ab_ref), (irrep_hbm, irrep_ref), (occ_hbm, occ_ref)))
+        for i, (source, target) in enumerate(
+            ((ab_hbm, ab_ref), (irrep_hbm, irrep_ref), (occ_hbm, occ_ref), (virt_hbm, virt_ref))
+        )
     ]
     for copy in copies:
         copy.start()
@@ -154,7 +157,7 @@
     occ = occ_ref[...]
     for c in range(0, cols, LANES):
         span = min(LANES, cols - c)
-        virt = jnp.transpose(jnp.broadcast_to(virt_ref[:, c:c + span], (LANES, span)))
+        virt = jnp.transpose(jnp.broadcast_to(virt_ref[c:c + span].reshape(1, span), (LANES, span)))
         at = c + lax.broadcasted_iota(I32, (span, LANES), 0)
         for p in range(0, pairs, LANES):
             lanes = slice(p, p + LANES)
@@ -301,26 +304,25 @@
     window = window_of(width, cd_rows)
     entries = extras + 4 * (irreps + 1)
 
-    early = (tiles * 6 // 10) * tile
-    virt_row = virt_energy.reshape(1, cols)
+    early = (tiles // 2) * tile
     turned = far(integrals.T)
     held, table = pl.pallas_call(
         functools.partial(plan_kernel, tile, cd_rows, width, cols),
         out_shape=(pltpu.VMEM(tau_packed.shape, tau_packed.dtype), pltpu.SMEM((entries,), I32)),
-        in_specs=[ANY] * 3,
+        in_specs=[VMEM, ANY, ANY],
         out_specs=(VMEM, SMEM),
         scratch_shapes=[
-            pltpu.SMEM(cd_sizes.shape, I32), pltpu.SMEM(ab_sizes.shape, I32), pltpu.SemaphoreType.DMA((3,)),
+            pltpu.SMEM(cd_sizes.shape, I32), pltpu.SMEM(ab_sizes.shape, I32), pltpu.SemaphoreType.DMA((2,)),
         ],
         compiler_params=pltpu.CompilerParams(vmem_limit_bytes=1 << 20),
         cost_estimate=pl.CostEstimate(flops=0, bytes_accessed=1 << 20, transcendentals=0),
-    )(far(tau_packed), far(cd_sizes), far(ab_sizes))
+    )(tau_packed, far(cd_sizes), far(ab_sizes))
     table = pltpu.with_memory_space_constraint(table, pltpu.SMEM)
     sent = tau_packed
     for step, key in enumerate(keys[:-2]):
         held = jnp.concatenate([held, swap(sent, key, count)], axis=0)
         if step == 0:
-            held, virt_row, occ_energy = lax.optimization_barrier((held, virt_row, occ_energy))
+            held, occ_energy = lax.optimization_barrier((held, occ_energy))
             weight, label, packed_early = pl.pallas_call(
                 functools.partial(weight_kernel, tile, width),
                 out_shape=(
@@ -328,20 +330,21 @@
                     pltpu.VMEM((pairs, LANES), F32),
                     pltpu.VMEM((early, window), integrals.dtype),
                 ),
-                in_specs=[SMEM] + [ANY] * 3 + [VMEM, ANY],
+                in_specs=[SMEM] + [ANY] * 5,
                 out_specs=(VMEM, VMEM, VMEM),
                 scratch_shapes=[
                     pltpu.SMEM(ab_sizes.shape, I32),
                     pltpu.VMEM((1, pairs), I32),
                     pltpu.VMEM((1, pairs), F32),
+                    pltpu.VMEM((cols,), F32),
                     pltpu.SemaphoreType.DMA((tiles,)),
-                    pltpu.SemaphoreType.DMA((3,)),
+                    pltpu.SemaphoreType.DMA((4,)),
                 ],
                 compiler_params=pltpu.CompilerParams(vmem_limit_bytes=2 << 20),
                 cost_estimate=pl.CostEstimate(flops=10 * cols * pairs, bytes_accessed=4 * cols * pairs, transcendentals=0),
             )(
                 table, far(ab_sizes), far(pair_irrep.reshape(1, pairs)), far(occ_energy.reshape(1, pairs)),
-                near(virt_row), turned,
+                far(virt_energy), turned,
             )
         else:
             held = lax.optimization_barrier(held)

time: 30 us -> 29.7 us (0.990)
  Pallas kernels: 7.38 us -> 5.84 us
  waiting for transfers between devices: 6.03 us -> 6.65 us
  starting transfers between devices: 13.4 us -> 14 us
    unnamed x1 -> x3, local copies, waits for them, and re-layouts: 0.89 us -> 1.65 us
    reshape x1 -> x0, local copies, waits for them, and re-layouts: 0.7 us -> none  [shards(): virt_row = virt_energy.reshape(1, cols)]
    pallas_call x1, Pallas kernels: 1.86 us -> 1.21 us  [shards(): pl.pallas_call(functools.partial(ladder_kernel, count, rows, cols * count...]
    ppermute x9, starting transfers between devices: 13.4 us -> 14 us  [swap(): return lax.ppermute(value, 'col', [(i, i ^ key) for i in range(count)])]
    ppermute x9, waiting for transfers between devices: 6.03 us -> 6.65 us  [swap(): return lax.ppermute(value, 'col', [(i, i ^ key) for i in range(count)])]
    pallas_call x1, Pallas kernels: 0.69 us -> 0.32 us  [shards(): pl.pallas_call(functools.partial(near_kernel, count, rows, fields), out_s...]
  transfers between devices with their start and end apart: 9 -> 9, of which waited for: 5 -> 7; matrix products, arithmetic and copies ran while one was open for 5% -> 3% of each run, Pallas kernels for 19% -> 16%
where the time goes in v6:
time: 29.7 us; the launch traced here: 29.4 us
  starting transfers between devices  14 us (47%)
  waiting for transfers between devices  6.65 us (22%)
  Pallas kernels  5.84 us (20%)
  local copies, waits for them, and re-layouts  1.65 us (6%)
  between operations  0.71 us (2%)
  other arithmetic  0.54 us (2%)
    ppermute x9, starting transfers between devices, swap(): return lax.ppermute(value, 'col', [(i, i ^ key) for i in range(count)])  14 us
    ppermute x9, waiting for transfers between devices, swap(): return lax.ppermute(value, 'col', [(i, i ^ key) for i in range(count)])  6.65 us
    unnamed x3, local copies, waits for them, and re-layouts  1.65 us
    pallas_call x1, Pallas kernels, shards(): pl.pallas_call(functools.partial(fetch_kernel, tile, width), out_shape=(p...  1.56 us
    pallas_call x1, Pallas kernels, shards(): pl.pallas_call(functools.partial(weight_kernel, tile, width), out_shape=(...  1.55 us
    pallas_call x1, Pallas kernels, shards(): pl.pallas_call(functools.partial(ladder_kernel, count, rows, cols * count...  1.21 us
    pallas_call x1, Pallas kernels, shards(): pl.pallas_call(functools.partial(plan_kernel, tile, cd_rows, width, cols)...  1.05 us
  transfers between devices with their start and end apart: 9, of which 7 were waited for; matrix products, arithmetic and copies ran while one was open for 3% of the time, Pallas kernels for 16%

profile of v6, /device:TPU:0, one launch (start us, length us, event | category | flops | bytes accessed | tf_op | source)
XLA Modules:
  0.0 29.4 jit_solution(6128440481358718636)
XLA Ops:
  0.6 3.5 %collective-permute-start = (bf16[8,1200]{1,0:T(8,128)(2,1)}, bf16[8,1200]{1,0:T(8,128)(2,1)S(1)}, u32[]{:S(2)}, u32[]{:S(2)}) collective-permute-start(bf16[8,1200]{1,0:T(8,128)(2,1)} %tau_ref.1), channel_id=1, source_target_pairs={{0,9},{1,8},{2,11},{3,10},{4,13},{5,12},{6,15},{7,14},{8,1},{9,0},... | collective-permute-start | bytes 57608 | tf_op jit(solution)/shard_map/ppermute | solution.py:23
  4.2 0.0 copy-start
  4.2 0.8 %copy-done = bf16[8,1200]{1,0:T(8,128)(2,1)S(1)} copy-done((bf16[8,1200]{1,0:T(8,128)(2,1)S(1)}, bf16[8,1200]{1,0:T(8,128)(2,1)}, u32[]{:S(2)}) %copy-start) | copy-done | bytes 19224
  4.9 1.0 %shard_map.86 = (bf16[8,1200]{1,0:T(8,128)(2,1)S(1)}, s32[95]{0:T(128)S(4)}) custom-call(bf16[8,1200]{1,0:T(8,128)(2,1)S(1)} %copy-done, s32[8]{0:T(128)} %cd_hbm.1, s32[8]{0:T(128)} %ab_hbm.3), custom_call_target="tpu_custom_call" | custom-call | bytes 1048576 | tf_op jit(solution)/shard_map/pallas_call | solution.py:309
  6.0 0.0 collective-permute-done
  6.0 1.9 %collective-permute-start.1 = (bf16[16,1200]{1,0:T(8,128)(2,1)S(1)}, bf16[16,1200]{1,0:T(8,128)(2,1)S(1)}, u32[]{:S(2)}, u32[]{:S(2)}) collective-permute-start(bf16[16,1200]{1,0:T(8,128)(2,1)S(1)} %pad_maximum_fusion.1), channel_id=1, source_target_pairs={{0,5},{1,4},{2,7},{3,6},{4,1},{5,0},{6,3},{7,2},{8,13},{9,12},{10,... | collective-permute-start | bytes 115208 | tf_op jit(solution)/shard_map/ppermute | solution.py:23
  7.9 1.5 %shard_map.87 = (f32[1600,128]{1,0:T(8,128)S(1)}, f32[128,128]{1,0:T(8,128)S(1)}, bf16[800,1408]{1,0:T(8,128)(2,1)S(1)}) custom-call(s32[95]{0:T(128)S(4)} %get-tuple-element.18.table_ref, s32[8]{0:T(128)} %ab_hbm.3, s32[1,128]{1,0:T(1,128)} %bitcast.9, f32[1,128]{1,0:T(1,128)} %bitcast.10, f32[1600]{0:T(1024)} %virt_hbm.1, bf16[1600,3200]{1,0:T(8,128)(2,1)} %bitcast.7), custom_call_target="tpu_custom_call" | custom-call | flops 2048000 | bytes 819200 | tf_op jit(solution)/shard_map/pallas_call | solution.py:326
  9.5 0.1 collective-permute-done.1
  9.6 0.6 %collective-permute-start.3 = (bf16[32,1200]{1,0:T(8,128)(2,1)S(1)}, bf16[32,1200]{1,0:T(8,128)(2,1)S(1)}, u32[]{:S(2)}, u32[]{:S(2)}) collective-permute-start(bf16[32,1200]{1,0:T(8,128)(2,1)S(1)} %pad_maximum_fusion.own_ref), channel_id=1, source_target_pairs={{0,1},{1,0},{2,3},{3,2},{4,5},{5,4},{6,7},{7,6},{8,9},{9,8},{10,11... | collective-permute-start | bytes 230408 | tf_op jit(solution)/shard_map/ppermute | solution.py:23
  10.3 1.5 %collective-permute-start.2 = (bf16[32,1200]{1,0:T(8,128)(2,1)S(1)}, bf16[32,1200]{1,0:T(8,128)(2,1)S(1)}, u32[]{:S(2)}, u32[]{:S(2)}) collective-permute-start(bf16[32,1200]{1,0:T(8,128)(2,1)S(1)} %pad_maximum_fusion.own_ref), channel_id=1, source_target_pairs={{0,3},{1,2},{2,1},{3,0},{4,7},{5,6},{6,5},{7,4},{8,11},{9,10},{10,... | collective-permute-start | bytes 230408 | tf_op jit(solution)/shard_map/ppermute | solution.py:23
  11.8 1.6 %shard_map.88 = (bf16[800,1408]{1,0:T(8,128)(2,1)S(1)}, bf16[9,160,1408]{2,1,0:T(8,128)(2,1)S(1)}, f32[8,128]{1,0:T(8,128)S(1)}) custom-call(s32[95]{0:T(128)S(4)} %get-tuple-element.18.table_ref, f32[128,128]{1,0:T(8,128)S(1)} %get-tuple-element.24.after_ref.label_ref, bf16[1600,3200]{1,0:T(8,128)(2,1)} %bitcast.8), custom_call_target="tpu_custom_call" | custom-call | bytes 3840000 | tf_op jit(solution)/shard_map/pallas_call | solution.py:355
  13.3 0.0 collective-permute-done.3.other_ref
  13.4 0.3 %shard_map.89.near_ref = f32[2,32,1408]{2,1,0:T(8,128)S(1)} custom-call(s32[95]{0:T(128)S(4)} %get-tuple-element.18.table_ref, bf16[32,1200]{1,0:T(8,128)(2,1)S(1)} %pad_maximum_fusion.own_ref, bf16[32,1200]{1,0:T(8,128)(2,1)S(1)} %collective-permute-done.3.other_ref, f32[128,128]{1,0:T(8,128)S(1)} %get-tuple-element.24.after_ref.label_ref, ...), custom_call_target="tpu_custom_call" | custom-call | flops 1802240 | bytes 720896 | tf_op jit(solution)/shard_map/pallas_call | solution.py:371
  13.7 1.1 %collective-permute-done.2.source_ref = bf16[32,1200]{1,0:T(8,128)(2,1)S(1)} collective-permute-done((bf16[32,1200]{1,0:T(8,128)(2,1)S(1)}, bf16[32,1200]{1,0:T(8,128)(2,1)S(1)}, u32[]{:S(2)}, u32[]{:S(2)}) %collective-permute-start.2) | collective-permute-done | bytes 76832 | tf_op jit(solution)/shard_map/ppermute | solution.py:23
  14.7 0.1 collective-permute-start.4
  14.9 0.2 shard_map.90.far_ref
  15.0 1.0 %collective-permute-done.4.last_ref = bf16[32,1200]{1,0:T(8,128)(2,1)S(1)} collective-permute-done((bf16[32,1200]{1,0:T(8,128)(2,1)S(1)}, bf16[32,1200]{1,0:T(8,128)(2,1)S(1)}, u32[]{:S(2)}, u32[]{:S(2)}) %collective-permute-start.4) | collective-permute-done | bytes 76832 | tf_op jit(solution)/shard_map/ppermute | solution.py:23
  16.0 1.2 %shard_map.91 = (f32[1600,128]{1,0:T(8,128)S(1)}, f32[1,128]{1,0:T(1,128)S(1)}) custom-call(s32[95]{0:T(128)S(4)} %get-tuple-element.18.table_ref, bf16[32,1200]{1,0:T(8,128)(2,1)S(1)} %collective-permute-done.4.last_ref, f32[128,128]{1,0:T(8,128)S(1)} %get-tuple-element.24.after_ref.label_ref, f32[2,32,1408]{2,1,0:T(8,128)S(1)} %shard_map.89.near_ref, ...), custom_call_target="tpu_custom_call" | custom-call | flops 491520000 | bytes 4659200 | tf_op jit(solution)/shard_map/pallas_call | solution.py:391
  17.2 2.5 %collective-permute-start.5 = (f32[1,128]{1,0:T(1,128)S(1)}, f32[1,128]{1,0:T(1,128)S(1)}, u32[]{:S(2)}, u32[]{:S(2)}) collective-permute-start(f32[1,128]{1,0:T(1,128)S(1)} %get-tuple-element.33), channel_id=1, source_target_pairs={{0,9},{1,8},{2,11},{3,10},{4,13},{5,12},{6,15},{7,14},{8,1},{9,0},... | collective-permute-start | bytes 1544 | tf_op jit(solution)/shard_map/ppermute | solution.py:23
  19.8 1.4 %collective-permute-done.5 = f32[1,128]{1,0:T(1,128)S(1)} collective-permute-done((f32[1,128]{1,0:T(1,128)S(1)}, f32[1,128]{1,0:T(1,128)S(1)}, u32[]{:S(2)}, u32[]{:S(2)}) %collective-permute-start.5) | collective-permute-done | bytes 544 | tf_op jit(solution)/shard_map/ppermute | solution.py:23
  21.2 2.3 %collective-permute-start.6 = (f32[1,128]{1,0:T(1,128)S(1)}, f32[1,128]{1,0:T(1,128)S(1)}, u32[]{:S(2)}, u32[]{:S(2)}) collective-permute-start(f32[1,128]{1,0:T(1,128)S(1)} %add.12), channel_id=1, source_target_pairs={{0,5},{1,4},{2,7},{3,6},{4,1},{5,0},{6,3},{7,2},{8,13},{9,12},{10,... | collective-permute-start | bytes 1544 | tf_op jit(solution)/shard_map/ppermute | solution.py:23
  23.5 1.3 %collective-permute-done.6 = f32[1,128]{1,0:T(1,128)S(1)} collective-permute-done((f32[1,128]{1,0:T(1,128)S(1)}, f32[1,128]{1,0:T(1,128)S(1)}, u32[]{:S(2)}, u32[]{:S(2)}) %collective-permute-start.6) | collective-permute-done | bytes 544 | tf_op jit(solution)/shard_map/ppermute | solution.py:23
  24.8 1.4 %collective-permute-start.7 = (f32[1,128]{1,0:T(1,128)S(1)}, f32[1,128]{1,0:T(1,128)S(1)}, u32[]{:S(2)}, u32[]{:S(2)}) collective-permute-start(f32[1,128]{1,0:T(1,128)S(1)} %add.13), channel_id=1, source_target_pairs={{0,3},{1,2},{2,1},{3,0},{4,7},{5,6},{6,5},{7,4},{8,11},{9,10},{10,... | collective-permute-start | bytes 1544 | tf_op jit(solution)/shard_map/ppermute | solution.py:23
  26.2 1.6 %collective-permute-done.7 = f32[1,128]{1,0:T(1,128)S(1)} collective-permute-done((f32[1,128]{1,0:T(1,128)S(1)}, f32[1,128]{1,0:T(1,128)S(1)}, u32[]{:S(2)}, u32[]{:S(2)}) %collective-permute-start.7) | collective-permute-done | bytes 544 | tf_op jit(solution)/shard_map/ppermute | solution.py:23
  27.7 0.0 collective-permute-start.8
  27.7 0.9 %copy.9 = f32[128,1600]{0,1:T(8,128)} copy(f32[128,1600]{0,1:T(8,128)S(1)} %bitcast.6) | data formatting | bytes 1638400
  28.6 0.2 collective-permute-done.8
  28.9 0.5 %add_bitcast_fusion = f32[128]{0:T(128)} fusion(f32[1,128]{1,0:T(1,128)S(1)} %add.14, f32[1,128]{1,0:T(1,128)S(1)} %collective-permute-done.8), kind=kLoop, calls=%fused_computation.2 | loop fusion | flops 128 | bytes 1536 | tf_op jit(solution)/shard_map/reshape | solution.py:409
  (5 shorter events, 0.0 us)
Async XLA Ops:
  0.6 5.4 %collective-permute-start = (bf16[8,1200]{1,0:T(8,128)(2,1)}, bf16[8,1200]{1,0:T(8,128)(2,1)S(1)}, u32[]{:S(2)}, u32[]{:S(2)}) collective-permute-start(bf16[8,1200]{1,0:T(8,128)(2,1)} %tau_ref.1), channel_id=1, source_target_pairs={{0,9},{1,8},{2,11},{3,10},{4,13},{5,12},{6,15},{7,14},{8,1},{9,0},... | collective-permute-start | bytes 57608 | tf_op jit(solution)/shard_map/ppermute | solution.py:23
  4.2 0.8 %copy-start = (bf16[8,1200]{1,0:T(8,128)(2,1)S(1)}, bf16[8,1200]{1,0:T(8,128)(2,1)}, u32[]{:S(2)}) copy-start(bf16[8,1200]{1,0:T(8,128)(2,1)} %tau_ref.1) | copy-start | bytes 57604
  6.0 3.6 %collective-permute-start.1 = (bf16[16,1200]{1,0:T(8,128)(2,1)S(1)}, bf16[16,1200]{1,0:T(8,128)(2,1)S(1)}, u32[]{:S(2)}, u32[]{:S(2)}) collective-permute-start(bf16[16,1200]{1,0:T(8,128)(2,1)S(1)} %pad_maximum_fusion.1), channel_id=1, source_target_pairs={{0,5},{1,4},{2,7},{3,6},{4,1},{5,0},{6,3},{7,2},{8,13},{9,12},{10,... | collective-permute-start | bytes 115208 | tf_op jit(solution)/shard_map/ppermute | solution.py:23
  9.6 3.7 %collective-permute-start.3 = (bf16[32,1200]{1,0:T(8,128)(2,1)S(1)}, bf16[32,1200]{1,0:T(8,128)(2,1)S(1)}, u32[]{:S(2)}, u32[]{:S(2)}) collective-permute-start(bf16[32,1200]{1,0:T(8,128)(2,1)S(1)} %pad_maximum_fusion.own_ref), channel_id=1, source_target_pairs={{0,1},{1,0},{2,3},{3,2},{4,5},{5,4},{6,7},{7,6},{8,9},{9,8},{10,11... | collective-permute-start | bytes 230408 | tf_op jit(solution)/shard_map/ppermute | solution.py:23
  10.3 4.5 %collective-permute-start.2 = (bf16[32,1200]{1,0:T(8,128)(2,1)S(1)}, bf16[32,1200]{1,0:T(8,128)(2,1)S(1)}, u32[]{:S(2)}, u32[]{:S(2)}) collective-permute-start(bf16[32,1200]{1,0:T(8,128)(2,1)S(1)} %pad_maximum_fusion.own_ref), channel_id=1, source_target_pairs={{0,3},{1,2},{2,1},{3,0},{4,7},{5,6},{6,5},{7,4},{8,11},{9,10},{10,... | collective-permute-start | bytes 230408 | tf_op jit(solution)/shard_map/ppermute | solution.py:23
  14.7 1.3 %collective-permute-start.4 = (bf16[32,1200]{1,0:T(8,128)(2,1)S(1)}, bf16[32,1200]{1,0:T(8,128)(2,1)S(1)}, u32[]{:S(2)}, u32[]{:S(2)}) collective-permute-start(bf16[32,1200]{1,0:T(8,128)(2,1)S(1)} %collective-permute-done.2.source_ref), channel_id=1, source_target_pairs={{0,1},{1,0},{2,3},{3,2},{4,5},{5,4},{6,7},{7,6},{8,9},{9,8},{10,11... | collective-permute-start | bytes 230408 | tf_op jit(solution)/shard_map/ppermute | solution.py:23
  17.2 3.9 %collective-permute-start.5 = (f32[1,128]{1,0:T(1,128)S(1)}, f32[1,128]{1,0:T(1,128)S(1)}, u32[]{:S(2)}, u32[]{:S(2)}) collective-permute-start(f32[1,128]{1,0:T(1,128)S(1)} %get-tuple-element.33), channel_id=1, source_target_pairs={{0,9},{1,8},{2,11},{3,10},{4,13},{5,12},{6,15},{7,14},{8,1},{9,0},... | collective-permute-start | bytes 1544 | tf_op jit(solution)/shard_map/ppermute | solution.py:23
  21.2 3.6 %collective-permute-start.6 = (f32[1,128]{1,0:T(1,128)S(1)}, f32[1,128]{1,0:T(1,128)S(1)}, u32[]{:S(2)}, u32[]{:S(2)}) collective-permute-start(f32[1,128]{1,0:T(1,128)S(1)} %add.12), channel_id=1, source_target_pairs={{0,5},{1,4},{2,7},{3,6},{4,1},{5,0},{6,3},{7,2},{8,13},{9,12},{10,... | collective-permute-start | bytes 1544 | tf_op jit(solution)/shard_map/ppermute | solution.py:23
  24.8 3.0 %collective-permute-start.7 = (f32[1,128]{1,0:T(1,128)S(1)}, f32[1,128]{1,0:T(1,128)S(1)}, u32[]{:S(2)}, u32[]{:S(2)}) collective-permute-start(f32[1,128]{1,0:T(1,128)S(1)} %add.13), channel_id=1, source_target_pairs={{0,3},{1,2},{2,1},{3,0},{4,7},{5,6},{6,5},{7,4},{8,11},{9,10},{10,... | collective-permute-start | bytes 1544 | tf_op jit(solution)/shard_map/ppermute | solution.py:23
  27.7 1.1 %collective-permute-start.8 = (f32[1,128]{1,0:T(1,128)S(1)}, f32[1,128]{1,0:T(1,128)S(1)}, u32[]{:S(2)}, u32[]{:S(2)}) collective-permute-start(f32[1,128]{1,0:T(1,128)S(1)} %add.14), channel_id=1, source_target_pairs={{0,1},{1,0},{2,3},{3,2},{4,5},{5,4},{6,7},{7,6},{8,9},{9,8},{10,11... | collective-permute-start | bytes 1544 | tf_op jit(solution)/shard_map/ppermute | solution.py:23

commit v7 on v6

--- a/solution.py
+++ b/solution.py
@@ -185,9 +185,9 @@
 def place(count, rows, mask, fields, table_ref, source, label_ref, tau_ref, placed_ref):
     me = lax.axis_index("col")
     half, width = source.shape
-    window = tau_ref.shape[1]
+    window = tau_ref.shape[1] // 2
     keys = generators(count)
-    tau_ref[:, :width] = source[...].astype(F32)
+    tau_ref[:, window:window + width] = source[...].astype(F32)
     lane = lax.broadcasted_iota(I32, (1, window), 1)
     owners = []
     for block in range(half // rows):
@@ -202,7 +202,12 @@
 
     def moved(i):
         place_at, size = table_ref[fields + 4 * i + 2], table_ref[fields + 4 * i + 3]
-        return jnp.where((lane >= place_at) & (lane < place_at + size), pltpu.roll(tau_ref[...], place_at, 1), 0.0)
+        turn = lax.rem(place_at, LANES)
+        values = tau_ref[:, pl.ds(pl.multiple_of(window + turn - place_at, LANES), window)]
+        pieces = [pltpu.roll(values[:, c:c + LANES], turn, 1) for c in range(0, window, LANES)]
+        wrapped = lane[:, :LANES] < turn
+        shifted = [jnp.where(wrapped, before, piece) for before, piece in zip(pieces[-1:] + pieces[:-1], pieces)]
+        return jnp.where((lane >= place_at) & (lane < place_at + size), jnp.concatenate(shifted, axis=1), 0.0)
 
     def store(values):
         for block, to in enumerate(places):
@@ -231,7 +236,6 @@
     update_ref, energy_ref, tau_ref, other_ref, dense_ref, parts_ref,
 ):
     cols, pairs = weight_ref.shape
-    window = tau_ref.shape[1]
     tiles = cols // tile
     fields, extras = fields_of(tiles, extra_ref.shape[0] - 1)
     keys = generators(count)
@@ -373,7 +377,7 @@
         out_shape=pltpu.VMEM((2, quarter, window), F32),
         in_specs=[SMEM, VMEM, VMEM, VMEM, ANY],
         out_specs=VMEM,
-        scratch_shapes=[pltpu.VMEM((quarter, window), F32)],
+        scratch_shapes=[pltpu.VMEM((quarter, 2 * window), F32)],
         compiler_params=place_params,
         cost_estimate=place_cost,
     )(table, near(held), near(other), near(label), near(mark))
@@ -384,7 +388,7 @@
         out_shape=pltpu.VMEM((quarter, window), F32),
         in_specs=[SMEM, VMEM, VMEM],
         out_specs=VMEM,
-        scratch_shapes=[pltpu.VMEM((quarter, window), F32)],
+        scratch_shapes=[pltpu.VMEM((quarter, 2 * window), F32)],
         compiler_params=place_params,
         cost_estimate=place_cost,
     )(table, near(away), near(label))
@@ -394,7 +398,7 @@
         in_specs=[SMEM] + [VMEM] * 8,
         out_specs=(VMEM, VMEM),
         scratch_shapes=[
-            pltpu.VMEM((quarter, window), F32),
+            pltpu.VMEM((quarter, 2 * window), F32),
             pltpu.VMEM((quarter, window), F32),
             pltpu.VMEM((pairs, window), jnp.bfloat16),
             pltpu.VMEM((tiles + irreps + 1, 8, pairs), F32),

time: 29.7 us -> 29.5 us (level)
  Pallas kernels: 5.84 us -> 4.58 us
  starting transfers between devices: 14 us -> 14.7 us
    ppermute x9, starting transfers between devices: 14 us -> 14.7 us  [swap(): return lax.ppermute(value, 'col', [(i, i ^ key) for i in range(count)])]
    pallas_call x1, Pallas kernels: 1.21 us -> 0.71 us  [shards(): pl.pallas_call(functools.partial(ladder_kernel, count, rows, cols * count...]
    pallas_call x1, Pallas kernels: 1.56 us -> 1.22 us  [shards(): pl.pallas_call(functools.partial(fetch_kernel, tile, width), out_shape=(p...]
    pallas_call x1, Pallas kernels: 1.55 us -> 1.22 us  [shards(): pl.pallas_call(functools.partial(weight_kernel, tile, width), out_shape=(...]
  transfers between devices with their start and end apart: 9 -> 9, of which waited for: 7 -> 6; matrix products, arithmetic and copies ran while one was open for 3% -> 3% of each run, Pallas kernels for 16% -> 13%
where the time goes in v7:
time: 29.5 us; the launch traced here: 29 us
  starting transfers between devices  14.7 us (50%)
  waiting for transfers between devices  6.87 us (23%)
  Pallas kernels  4.58 us (16%)
  local copies, waits for them, and re-layouts  1.65 us (6%)
  between operations  0.71 us (2%)
  other arithmetic  0.54 us (2%)
    ppermute x9, starting transfers between devices, swap(): return lax.ppermute(value, 'col', [(i, i ^ key) for i in range(count)])  14.7 us
    ppermute x9, waiting for transfers between devices, swap(): return lax.ppermute(value, 'col', [(i, i ^ key) for i in range(count)])  6.87 us
    unnamed x3, local copies, waits for them, and re-layouts  1.65 us
    pallas_call x1, Pallas kernels, shards(): pl.pallas_call(functools.partial(weight_kernel, tile, width), out_shape=(...  1.22 us
    pallas_call x1, Pallas kernels, shards(): pl.pallas_call(functools.partial(fetch_kernel, tile, width), out_shape=(p...  1.22 us
    pallas_call x1, Pallas kernels, shards(): pl.pallas_call(functools.partial(plan_kernel, tile, cd_rows, width, cols)...  1.05 us
    pallas_call x1, Pallas kernels, shards(): pl.pallas_call(functools.partial(ladder_kernel, count, rows, cols * count...  0.71 us
  transfers between devices with their start and end apart: 9, of which 6 were waited for; matrix products, arithmetic and copies ran while one was open for 3% of the time, Pallas kernels for 13%

profile of v7, /device:TPU:0, one launch (start us, length us, event | category | flops | bytes accessed | tf_op | source)
XLA Modules:
  0.0 29.0 jit_solution(6616089121289467330)
XLA Ops:
  0.6 3.5 %collective-permute-start = (bf16[8,1200]{1,0:T(8,128)(2,1)}, bf16[8,1200]{1,0:T(8,128)(2,1)S(1)}, u32[]{:S(2)}, u32[]{:S(2)}) collective-permute-start(bf16[8,1200]{1,0:T(8,128)(2,1)} %tau_ref.1), channel_id=1, source_target_pairs={{0,9},{1,8},{2,11},{3,10},{4,13},{5,12},{6,15},{7,14},{8,1},{9,0},... | collective-permute-start | bytes 57608 | tf_op jit(solution)/shard_map/ppermute | solution.py:23
  4.2 0.0 copy-start
  4.2 0.8 %copy-done = bf16[8,1200]{1,0:T(8,128)(2,1)S(1)} copy-done((bf16[8,1200]{1,0:T(8,128)(2,1)S(1)}, bf16[8,1200]{1,0:T(8,128)(2,1)}, u32[]{:S(2)}) %copy-start) | copy-done | bytes 19224
  4.9 1.0 %shard_map.86 = (bf16[8,1200]{1,0:T(8,128)(2,1)S(1)}, s32[95]{0:T(128)S(4)}) custom-call(bf16[8,1200]{1,0:T(8,128)(2,1)S(1)} %copy-done, s32[8]{0:T(128)} %cd_hbm.1, s32[8]{0:T(128)} %ab_hbm.3), custom_call_target="tpu_custom_call" | custom-call | bytes 1048576 | tf_op jit(solution)/shard_map/pallas_call | solution.py:313
  6.0 0.0 collective-permute-done
  6.0 1.9 %collective-permute-start.1 = (bf16[16,1200]{1,0:T(8,128)(2,1)S(1)}, bf16[16,1200]{1,0:T(8,128)(2,1)S(1)}, u32[]{:S(2)}, u32[]{:S(2)}) collective-permute-start(bf16[16,1200]{1,0:T(8,128)(2,1)S(1)} %pad_maximum_fusion.1), channel_id=1, source_target_pairs={{0,5},{1,4},{2,7},{3,6},{4,1},{5,0},{6,3},{7,2},{8,13},{9,12},{10,... | collective-permute-start | bytes 115208 | tf_op jit(solution)/shard_map/ppermute | solution.py:23
  7.9 1.2 %shard_map.87 = (f32[1600,128]{1,0:T(8,128)S(1)}, f32[128,128]{1,0:T(8,128)S(1)}, bf16[800,1408]{1,0:T(8,128)(2,1)S(1)}) custom-call(s32[95]{0:T(128)S(4)} %get-tuple-element.18.table_ref, s32[8]{0:T(128)} %ab_hbm.3, s32[1,128]{1,0:T(1,128)} %bitcast.9, f32[1,128]{1,0:T(1,128)} %bitcast.10, f32[1600]{0:T(1024)} %virt_hbm.1, bf16[1600,3200]{1,0:T(8,128)(2,1)} %bitcast.7), custom_call_target="tpu_custom_call" | custom-call | flops 2048000 | bytes 819200 | tf_op jit(solution)/shard_map/pallas_call | solution.py:330
  9.2 0.5 %collective-permute-done.1 = bf16[16,1200]{1,0:T(8,128)(2,1)S(1)} collective-permute-done((bf16[16,1200]{1,0:T(8,128)(2,1)S(1)}, bf16[16,1200]{1,0:T(8,128)(2,1)S(1)}, u32[]{:S(2)}, u32[]{:S(2)}) %collective-permute-start.1) | collective-permute-done | bytes 38432 | tf_op jit(solution)/shard_map/ppermute | solution.py:23
  9.6 0.6 %collective-permute-start.3 = (bf16[32,1200]{1,0:T(8,128)(2,1)S(1)}, bf16[32,1200]{1,0:T(8,128)(2,1)S(1)}, u32[]{:S(2)}, u32[]{:S(2)}) collective-permute-start(bf16[32,1200]{1,0:T(8,128)(2,1)S(1)} %pad_maximum_fusion.own_ref), channel_id=1, source_target_pairs={{0,1},{1,0},{2,3},{3,2},{4,5},{5,4},{6,7},{7,6},{8,9},{9,8},{10,11... | collective-permute-start | bytes 230408 | tf_op jit(solution)/shard_map/ppermute | solution.py:23
  10.3 1.5 %collective-permute-start.2 = (bf16[32,1200]{1,0:T(8,128)(2,1)S(1)}, bf16[32,1200]{1,0:T(8,128)(2,1)S(1)}, u32[]{:S(2)}, u32[]{:S(2)}) collective-permute-start(bf16[32,1200]{1,0:T(8,128)(2,1)S(1)} %pad_maximum_fusion.own_ref), channel_id=1, source_target_pairs={{0,3},{1,2},{2,1},{3,0},{4,7},{5,6},{6,5},{7,4},{8,11},{9,10},{10,... | collective-permute-start | bytes 230408 | tf_op jit(solution)/shard_map/ppermute | solution.py:23
  11.8 1.2 %shard_map.88 = (bf16[800,1408]{1,0:T(8,128)(2,1)S(1)}, bf16[9,160,1408]{2,1,0:T(8,128)(2,1)S(1)}, f32[8,128]{1,0:T(8,128)S(1)}) custom-call(s32[95]{0:T(128)S(4)} %get-tuple-element.18.table_ref, f32[128,128]{1,0:T(8,128)S(1)} %get-tuple-element.24.after_ref.label_ref, bf16[1600,3200]{1,0:T(8,128)(2,1)} %bitcast.8), custom_call_target="tpu_custom_call" | custom-call | bytes 3840000 | tf_op jit(solution)/shard_map/pallas_call | solution.py:359
  13.0 0.0 collective-permute-done.3.other_ref
  13.0 0.3 shard_map.89.near_ref
  13.3 1.5 %collective-permute-done.2.source_ref = bf16[32,1200]{1,0:T(8,128)(2,1)S(1)} collective-permute-done((bf16[32,1200]{1,0:T(8,128)(2,1)S(1)}, bf16[32,1200]{1,0:T(8,128)(2,1)S(1)}, u32[]{:S(2)}, u32[]{:S(2)}) %collective-permute-start.2) | collective-permute-done | bytes 76832 | tf_op jit(solution)/shard_map/ppermute | solution.py:23
  14.7 0.1 collective-permute-start.4
  14.9 0.1 shard_map.90.far_ref
  15.0 1.0 %collective-permute-done.4.last_ref = bf16[32,1200]{1,0:T(8,128)(2,1)S(1)} collective-permute-done((bf16[32,1200]{1,0:T(8,128)(2,1)S(1)}, bf16[32,1200]{1,0:T(8,128)(2,1)S(1)}, u32[]{:S(2)}, u32[]{:S(2)}) %collective-permute-start.4) | collective-permute-done | bytes 76832 | tf_op jit(solution)/shard_map/ppermute | solution.py:23
  16.0 0.7 %shard_map.91 = (f32[1600,128]{1,0:T(8,128)S(1)}, f32[1,128]{1,0:T(1,128)S(1)}) custom-call(s32[95]{0:T(128)S(4)} %get-tuple-element.18.table_ref, bf16[32,1200]{1,0:T(8,128)(2,1)S(1)} %collective-permute-done.4.last_ref, f32[128,128]{1,0:T(8,128)S(1)} %get-tuple-element.24.after_ref.label_ref, f32[2,32,1408]{2,1,0:T(8,128)S(1)} %shard_map.89.near_ref, ...), custom_call_target="tpu_custom_call" | custom-call | flops 491520000 | bytes 4659200 | tf_op jit(solution)/shard_map/pallas_call | solution.py:395
  16.7 2.8 %collective-permute-start.5 = (f32[1,128]{1,0:T(1,128)S(1)}, f32[1,128]{1,0:T(1,128)S(1)}, u32[]{:S(2)}, u32[]{:S(2)}) collective-permute-start(f32[1,128]{1,0:T(1,128)S(1)} %get-tuple-element.33), channel_id=1, source_target_pairs={{0,9},{1,8},{2,11},{3,10},{4,13},{5,12},{6,15},{7,14},{8,1},{9,0},... | collective-permute-start | bytes 1544 | tf_op jit(solution)/shard_map/ppermute | solution.py:23
  19.6 1.3 %collective-permute-done.5 = f32[1,128]{1,0:T(1,128)S(1)} collective-permute-done((f32[1,128]{1,0:T(1,128)S(1)}, f32[1,128]{1,0:T(1,128)S(1)}, u32[]{:S(2)}, u32[]{:S(2)}) %collective-permute-start.5) | collective-permute-done | bytes 544 | tf_op jit(solution)/shard_map/ppermute | solution.py:23
  20.9 1.8 %collective-permute-start.6 = (f32[1,128]{1,0:T(1,128)S(1)}, f32[1,128]{1,0:T(1,128)S(1)}, u32[]{:S(2)}, u32[]{:S(2)}) collective-permute-start(f32[1,128]{1,0:T(1,128)S(1)} %add.12), channel_id=1, source_target_pairs={{0,5},{1,4},{2,7},{3,6},{4,1},{5,0},{6,3},{7,2},{8,13},{9,12},{10,... | collective-permute-start | bytes 1544 | tf_op jit(solution)/shard_map/ppermute | solution.py:23
  22.7 1.3 %collective-permute-done.6 = f32[1,128]{1,0:T(1,128)S(1)} collective-permute-done((f32[1,128]{1,0:T(1,128)S(1)}, f32[1,128]{1,0:T(1,128)S(1)}, u32[]{:S(2)}, u32[]{:S(2)}) %collective-permute-start.6) | collective-permute-done | bytes 544 | tf_op jit(solution)/shard_map/ppermute | solution.py:23
  24.0 2.1 %collective-permute-start.7 = (f32[1,128]{1,0:T(1,128)S(1)}, f32[1,128]{1,0:T(1,128)S(1)}, u32[]{:S(2)}, u32[]{:S(2)}) collective-permute-start(f32[1,128]{1,0:T(1,128)S(1)} %add.13), channel_id=1, source_target_pairs={{0,3},{1,2},{2,1},{3,0},{4,7},{5,6},{6,5},{7,4},{8,11},{9,10},{10,... | collective-permute-start | bytes 1544 | tf_op jit(solution)/shard_map/ppermute | solution.py:23
  26.1 1.3 %collective-permute-done.7 = f32[1,128]{1,0:T(1,128)S(1)} collective-permute-done((f32[1,128]{1,0:T(1,128)S(1)}, f32[1,128]{1,0:T(1,128)S(1)}, u32[]{:S(2)}, u32[]{:S(2)}) %collective-permute-start.7) | collective-permute-done | bytes 544 | tf_op jit(solution)/shard_map/ppermute | solution.py:23
  27.4 0.2 collective-permute-start.8
  27.6 0.9 %copy.9 = f32[128,1600]{0,1:T(8,128)} copy(f32[128,1600]{0,1:T(8,128)S(1)} %bitcast.6) | data formatting | bytes 1638400
  28.5 0.0 collective-permute-done.8
  28.5 0.5 %add_bitcast_fusion = f32[128]{0:T(128)} fusion(f32[1,128]{1,0:T(1,128)S(1)} %add.14, f32[1,128]{1,0:T(1,128)S(1)} %collective-permute-done.8), kind=kLoop, calls=%fused_computation.2 | loop fusion | flops 128 | bytes 1536 | tf_op jit(solution)/shard_map/reshape | solution.py:413
  (5 shorter events, 0.0 us)
Async XLA Ops:
  0.6 5.4 %collective-permute-start = (bf16[8,1200]{1,0:T(8,128)(2,1)}, bf16[8,1200]{1,0:T(8,128)(2,1)S(1)}, u32[]{:S(2)}, u32[]{:S(2)}) collective-permute-start(bf16[8,1200]{1,0:T(8,128)(2,1)} %tau_ref.1), channel_id=1, source_target_pairs={{0,9},{1,8},{2,11},{3,10},{4,13},{5,12},{6,15},{7,14},{8,1},{9,0},... | collective-permute-start | bytes 57608 | tf_op jit(solution)/shard_map/ppermute | solution.py:23
  4.2 0.8 %copy-start = (bf16[8,1200]{1,0:T(8,128)(2,1)S(1)}, bf16[8,1200]{1,0:T(8,128)(2,1)}, u32[]{:S(2)}) copy-start(bf16[8,1200]{1,0:T(8,128)(2,1)} %tau_ref.1) | copy-start | bytes 57604
  6.0 3.6 %collective-permute-start.1 = (bf16[16,1200]{1,0:T(8,128)(2,1)S(1)}, bf16[16,1200]{1,0:T(8,128)(2,1)S(1)}, u32[]{:S(2)}, u32[]{:S(2)}) collective-permute-start(bf16[16,1200]{1,0:T(8,128)(2,1)S(1)} %pad_maximum_fusion.1), channel_id=1, source_target_pairs={{0,5},{1,4},{2,7},{3,6},{4,1},{5,0},{6,3},{7,2},{8,13},{9,12},{10,... | collective-permute-start | bytes 115208 | tf_op jit(solution)/shard_map/ppermute | solution.py:23
  9.6 3.4 %collective-permute-start.3 = (bf16[32,1200]{1,0:T(8,128)(2,1)S(1)}, bf16[32,1200]{1,0:T(8,128)(2,1)S(1)}, u32[]{:S(2)}, u32[]{:S(2)}) collective-permute-start(bf16[32,1200]{1,0:T(8,128)(2,1)S(1)} %pad_maximum_fusion.own_ref), channel_id=1, source_target_pairs={{0,1},{1,0},{2,3},{3,2},{4,5},{5,4},{6,7},{7,6},{8,9},{9,8},{10,11... | collective-permute-start | bytes 230408 | tf_op jit(solution)/shard_map/ppermute | solution.py:23
  10.3 4.5 %collective-permute-start.2 = (bf16[32,1200]{1,0:T(8,128)(2,1)S(1)}, bf16[32,1200]{1,0:T(8,128)(2,1)S(1)}, u32[]{:S(2)}, u32[]{:S(2)}) collective-permute-start(bf16[32,1200]{1,0:T(8,128)(2,1)S(1)} %pad_maximum_fusion.own_ref), channel_id=1, source_target_pairs={{0,3},{1,2},{2,1},{3,0},{4,7},{5,6},{6,5},{7,4},{8,11},{9,10},{10,... | collective-permute-start | bytes 230408 | tf_op jit(solution)/shard_map/ppermute | solution.py:23
  14.7 1.3 %collective-permute-start.4 = (bf16[32,1200]{1,0:T(8,128)(2,1)S(1)}, bf16[32,1200]{1,0:T(8,128)(2,1)S(1)}, u32[]{:S(2)}, u32[]{:S(2)}) collective-permute-start(bf16[32,1200]{1,0:T(8,128)(2,1)S(1)} %collective-permute-done.2.source_ref), channel_id=1, source_target_pairs={{0,1},{1,0},{2,3},{3,2},{4,5},{5,4},{6,7},{7,6},{8,9},{9,8},{10,11... | collective-permute-start | bytes 230408 | tf_op jit(solution)/shard_map/ppermute | solution.py:23
  16.7 4.1 %collective-permute-start.5 = (f32[1,128]{1,0:T(1,128)S(1)}, f32[1,128]{1,0:T(1,128)S(1)}, u32[]{:S(2)}, u32[]{:S(2)}) collective-permute-start(f32[1,128]{1,0:T(1,128)S(1)} %get-tuple-element.33), channel_id=1, source_target_pairs={{0,9},{1,8},{2,11},{3,10},{4,13},{5,12},{6,15},{7,14},{8,1},{9,0},... | collective-permute-start | bytes 1544 | tf_op jit(solution)/shard_map/ppermute | solution.py:23
  20.9 3.1 %collective-permute-start.6 = (f32[1,128]{1,0:T(1,128)S(1)}, f32[1,128]{1,0:T(1,128)S(1)}, u32[]{:S(2)}, u32[]{:S(2)}) collective-permute-start(f32[1,128]{1,0:T(1,128)S(1)} %add.12), channel_id=1, source_target_pairs={{0,5},{1,4},{2,7},{3,6},{4,1},{5,0},{6,3},{7,2},{8,13},{9,12},{10,... | collective-permute-start | bytes 1544 | tf_op jit(solution)/shard_map/ppermute | solution.py:23
  24.0 3.4 %collective-permute-start.7 = (f32[1,128]{1,0:T(1,128)S(1)}, f32[1,128]{1,0:T(1,128)S(1)}, u32[]{:S(2)}, u32[]{:S(2)}) collective-permute-start(f32[1,128]{1,0:T(1,128)S(1)} %add.13), channel_id=1, source_target_pairs={{0,3},{1,2},{2,1},{3,0},{4,7},{5,6},{6,5},{7,4},{8,11},{9,10},{10,... | collective-permute-start | bytes 1544 | tf_op jit(solution)/shard_map/ppermute | solution.py:23
  27.4 1.1 %collective-permute-start.8 = (f32[1,128]{1,0:T(1,128)S(1)}, f32[1,128]{1,0:T(1,128)S(1)}, u32[]{:S(2)}, u32[]{:S(2)}) collective-permute-start(f32[1,128]{1,0:T(1,128)S(1)} %add.14), channel_id=1, source_target_pairs={{0,1},{1,0},{2,3},{3,2},{4,5},{5,4},{6,7},{7,6},{8,9},{9,8},{10,11... | collective-permute-start | bytes 1544 | tf_op jit(solution)/shard_map/ppermute | solution.py:23
